TPU v7x, 512 devices: a whole 4x4x16 slice. The times are simulated.
512 devices in a mesh: dp: 4 (over x_lo, core), ctx: 128 (over z, x_hi, y).
Axes of the slice: x: 4 (x_hi: 2, x_lo: 2; x = x_hi * 2 + x_lo), y: 4, z: 16, core: 2. Of those that a mesh axis runs over, the one named last changes fastest.
Arguments:
- features: bfloat16 [4, 16384, 4096], P('dp', 'ctx'), may hold values from -6 to 6
- gate_values: bfloat16 [4, 16384, 4096], P('dp', 'ctx'), may hold values from -6 to 6
- upstream: bfloat16 [4, 16384, 4096], P('dp', 'ctx'), may hold values from -6 to 6
- short_filter: float32 [7, 4096], replicated, may hold values from -2 to 2
- long_filter: bfloat16 [32, 4096], replicated, may hold values from -0.09375 to 0.09375
- loss_scale: float32 [1], replicated, may hold values from 8 to 64
Outputs:
- input_grad: bfloat16 [4, 16384, 4096], P('dp', 'ctx')
- short_grad: float32 [7, 4096], P(None, 'ctx')
- grad_norm: float32 [1], replicated
All inputs are finite; a program needn't handle non-finite values.
Results may differ from a plain program's by a relative error of at most 0.0057.
Values may be sent and summed in bfloat16 or wider, within the bound.
No kernel may reach another device: no remote copies, remote signals or barrier semaphores. Data moves between devices by JAX's collectives and lax.ppermute only.
A program may use at most 128 MiB of HBM per device.

v0:
```python
import jax
import jax.numpy as jnp
from jax import lax
from jax.sharding import PartitionSpec as P

C = 4096
BLOCK = 512


def shifted_2(block, axis, distance):
    devices = range(lax.axis_size(axis))
    route = [(i - distance, i) for i in devices if i - distance in devices]
    return lax.ppermute(block, axis, route)


def lag_tiles(taps_padded, start, width):
    window = taps_padded[:, start : start + 2 * width]
    repeat = jnp.tile(window, (1, width))[:, width : width + width * (2 * width - 1)]
    return repeat.reshape(window.shape[0], width, 2 * width - 1)[:, :, :width]


def conv_back(gated_cols, long_filter, chan_start):
    seq_rows, length, chan_count = gated_cols.shape
    groups, tap_count = long_filter.shape
    group_width = C // groups
    group_part = min(chan_count, group_width)
    local_groups = chan_count // group_part
    first_group = chan_start // group_width
    filters = lax.dynamic_slice_in_dim(long_filter, first_group, local_groups, 0)
    nblocks = length // BLOCK
    lane_span = seq_rows * group_part
    lag_count = min(tap_count // BLOCK + 1, nblocks)
    taps_padded = jnp.pad(filters, ((0, 0), (BLOCK, BLOCK)))
    arranged = gated_cols.reshape(seq_rows, nblocks, BLOCK, local_groups, group_part)
    arranged = arranged.transpose(3, 2, 1, 0, 4).reshape(local_groups, BLOCK, nblocks * lane_span)
    padded_src = jnp.pad(arranged, ((0, 0), (0, 0), (0, lag_count * lane_span)))
    toeplitz = jnp.concatenate(
        [lag_tiles(taps_padded, offset * BLOCK, BLOCK) for offset in range(lag_count)], axis=2
    )
    windows = jnp.concatenate(
        [
            padded_src[:, :, offset * lane_span : offset * lane_span + nblocks * lane_span]
            for offset in range(lag_count)
        ],
        axis=1,
    )
    running = jnp.einsum("gab,gbn->gan", toeplitz, windows, preferred_element_type=jnp.float32)
    result = running.astype(jnp.bfloat16).reshape(
        local_groups, BLOCK, nblocks, seq_rows, group_part
    )
    return result.transpose(3, 2, 1, 0, 4).reshape(seq_rows, length, chan_count)


def short_back(conv_grad, later, weights):
    length = conv_grad.shape[1]
    extended = jnp.concatenate([conv_grad, later], axis=1)
    result = jnp.zeros(conv_grad.shape, jnp.float32)
    for position in range(weights.shape[0]):
        result = result + weights[position] * extended[:, position : position + length]
    return result.astype(jnp.bfloat16)


def filter_terms(conv_grad, earlier_ext, width):
    length = conv_grad.shape[1]
    rim = width - 1
    row_terms = []
    for position in range(width):
        shifted = earlier_ext[:, rim - position : rim - position + length]
        row_terms.append(
            jnp.einsum("stc,stc->c", conv_grad, shifted, preferred_element_type=jnp.float32)
        )
    return jnp.stack(row_terms)


def per_device(features, gate_values, upstream, short_filter, long_filter, loss_scale):
    gated = (upstream.astype(jnp.float32) * gate_values.astype(jnp.float32)).astype(jnp.bfloat16)
    shards = lax.axis_size("ctx")
    chan_count = features.shape[2] // shards
    chan_start = lax.axis_index("ctx") * chan_count
    width = short_filter.shape[0]
    rim = width - 1
    gated_cols = lax.all_to_all(gated, "ctx", split_axis=2, concat_axis=1, tiled=True)
    conv_cols = conv_back(gated_cols, long_filter, chan_start)
    conv_grad = lax.all_to_all(conv_cols, "ctx", split_axis=1, concat_axis=2, tiled=True)
    later = shifted_2(conv_grad[:, :rim, :], "ctx", -1)
    earlier = shifted_2(features[:, -rim:, :], "ctx", 1)
    input_grad = short_back(conv_grad, later, short_filter)
    partial_terms = filter_terms(conv_grad, jnp.concatenate([earlier, features], axis=1), width)
    summed = lax.psum(partial_terms, ("dp", "ctx")) / loss_scale[0]
    norm_sq = jnp.sum(summed * summed)
    unscaled = lax.dynamic_slice_in_dim(summed, chan_start, chan_count, 1)
    norm_value = jnp.sqrt(norm_sq)
    short_grad = jnp.where(jnp.isfinite(norm_value), unscaled, jnp.zeros_like(unscaled))
    return (input_grad, short_grad, norm_value.reshape(1))


def solution(mesh):
    placed = (P("dp", "ctx", None), P("dp", "ctx", None), P("dp", "ctx", None), P(), P(), P())
    return jax.shard_map(
        per_device,
        mesh=mesh,
        in_specs=placed,
        out_specs=(P("dp", "ctx", None), P(None, "ctx"), P()),
        check_vma=False,
    )
```

profile of v0, /device:TPU:1, one launch (start us, length us, event | category | flops | bytes accessed | tf_op | source)
XLA Modules:
  0.0 975.0 jit_solution(17651294548892226936)
XLA Ops:
  9.0 2.8 copy.31
  12.3 22.4 %reduce.50 = bf16[4096,128]{1,0:T(8,128)(2,1)S(1)} reduce(bf16[4096,1,128]{2,1,0:T(2,128)(2,1)S(1)} %bitcast.163, bf16[]{:T(256)} %broadcast.77), dimensions={1}, to_apply=%bitcast.143.reduce_sub_computation | reduce | bytes 2097154
  35.8 23.5 %all-to-all-start = ((bf16[128,2,2048]{2,1,0:T(2,128)(2,1)}), bf16[128,2,2048]{2,1,0:T(2,128)(2,1)S(1)}, u32[]{:S(2)}, u32[]{:S(2)}) async-start(bf16[128,2,2048]{2,1,0:T(2,128)(2,1)} %reshape.273), calls=%async_computation | async-start | bytes 2097152 | tf_op jit(solution)/shard_map/all_to_all | solution.py:82
  62.1 18.5 %slice_reduce_fusion.8 = bf16[523776]{0:T(1024)(128)(2,1)} fusion(bf16[1,524288]{1,0:T(2,128)(2,1)S(1)} %bitcast.164), kind=kLoop, calls=%fused_computation.35 | loop fusion | bytes 2095104 | tf_op jit(solution)/shard_map/slice | solution.py:18
  83.3 18.7 %slice_reduce_fusion.7 = bf16[523776]{0:T(1024)(128)(2,1)} fusion(bf16[1,524288]{1,0:T(2,128)(2,1)S(1)} %bitcast.165), kind=kLoop, calls=%fused_computation.34 | loop fusion | bytes 2095104 | tf_op jit(solution)/shard_map/slice | solution.py:18
  103.8 18.7 %slice_reduce_fusion.6 = bf16[523776]{0:T(1024)(128)(2,1)} fusion(bf16[1,524288]{1,0:T(2,128)(2,1)S(1)} %bitcast.166), kind=kLoop, calls=%fused_computation.33 | loop fusion | bytes 2095104 | tf_op jit(solution)/shard_map/slice | solution.py:18
  124.1 18.5 %slice_reduce_fusion.5 = bf16[523776]{0:T(1024)(128)(2,1)} fusion(bf16[1,524288]{1,0:T(2,128)(2,1)S(1)} %bitcast.167), kind=kLoop, calls=%fused_computation.32 | loop fusion | bytes 2095104 | tf_op jit(solution)/shard_map/slice | solution.py:18
  144.4 18.9 %slice_reduce_fusion.4 = bf16[523776]{0:T(1024)(128)(2,1)} fusion(bf16[1,524288]{1,0:T(2,128)(2,1)S(1)} %bitcast.168), kind=kLoop, calls=%fused_computation.31 | loop fusion | bytes 2095104 | tf_op jit(solution)/shard_map/slice | solution.py:18
  164.9 18.7 %slice_reduce_fusion.3 = bf16[523776]{0:T(1024)(128)(2,1)} fusion(bf16[1,524288]{1,0:T(2,128)(2,1)S(1)} %bitcast.169), kind=kLoop, calls=%fused_computation.30 | loop fusion | bytes 2095104 | tf_op jit(solution)/shard_map/slice | solution.py:18
  183.6 2.6 reshape.210
  186.3 3.9 reshape.211
  190.2 2.6 reshape.212
  192.8 4.0 reshape.213
  196.8 2.6 reshape.214
  199.5 3.8 reshape.215
  205.1 18.7 %slice_reduce_fusion.2 = bf16[523776]{0:T(1024)(128)(2,1)} fusion(bf16[1,524288]{1,0:T(2,128)(2,1)S(1)} %bitcast.170), kind=kLoop, calls=%fused_computation.29 | loop fusion | bytes 2095104 | tf_op jit(solution)/shard_map/slice | solution.py:18
  223.8 4.0 reshape.216
  229.3 17.9 %slice_reduce_fusion.1 = bf16[523776]{0:T(1024)(128)(2,1)S(1)} fusion(bf16[1,524288]{1,0:T(2,128)(2,1)S(1)} %bitcast.171), kind=kLoop, calls=%fused_computation.28 | loop fusion | bytes 2095104 | tf_op jit(solution)/shard_map/slice | solution.py:18
  247.2 2.6 reshape.217
  251.5 17.7 %slice_reduce_fusion = bf16[523776]{0:T(1024)(128)(2,1)S(1)} fusion(bf16[1,524288]{1,0:T(2,128)(2,1)S(1)} %bitcast.172), kind=kLoop, calls=%fused_computation.27 | loop fusion | bytes 2095104 | tf_op jit(solution)/shard_map/slice | solution.py:18
  269.2 2.6 reshape.218
  285.6 7.0 fusion.3
  294.3 12.9 %copy.36 = bf16[1,16384,32]{2,0,1:T(2,128)(2,1)} copy(bf16[1,16384,32]{1,2,0:T(8,128)(2,1)S(1)} %reshape.224) | data formatting | bytes 2097152 | tf_op jit(solution)/shard_map/reshape | solution.py:51
  307.2 90.8 %reduce.51 = bf16[16384,32]{1,0:T(8,128)(2,1)} reduce(bf16[16384,1,32]{2,1,0:T(2,128)(2,1)} %bitcast.158, bf16[]{:T(256)} %broadcast.77), dimensions={1}, to_apply=%bitcast.145.reduce_sub_computation | reduce | bytes 2097154
  397.9 7.3 reshape.275
  405.3 18.2 %all-to-all-start.1 = ((bf16[128,2,2048]{2,1,0:T(2,128)(2,1)}), bf16[128,2,2048]{2,1,0:T(2,128)(2,1)S(1)}, u32[]{:S(2)}, u32[]{:S(2)}) async-start(bf16[128,2,2048]{2,1,0:T(2,128)(2,1)} %reshape.275), calls=%async_computation.1 | async-start | bytes 2097152 | tf_op jit(solution)/shard_map/all_to_all | solution.py:84
  427.6 47.7 %all-to-all-done.1 = bf16[128,2,2048]{2,1,0:T(2,128)(2,1)S(1)} async-done(((bf16[128,2,2048]{2,1,0:T(2,128)(2,1)}), bf16[128,2,2048]{2,1,0:T(2,128)(2,1)S(1)}, u32[]{:S(2)}, u32[]{:S(2)}) %all-to-all-start.1) | async-done | bytes 1048608 | tf_op jit(solution)/shard_map/all_to_all | solution.py:84
  475.4 14.1 %reshape.276 = bf16[16384,1,32]{2,1,0:T(2,128)(2,1)} reshape(bf16[128,2,2048]{2,1,0:T(2,128)(2,1)S(1)} %all-to-all-done.1) | data formatting | bytes 2097152
  489.4 15.1 %copy.37 = bf16[1,16384,32]{1,2,0:T(8,128)(2,1)S(1)} copy(bf16[1,16384,32]{2,0,1:T(2,128)(2,1)} %bitcast.159) | data formatting | bytes 2097152 | tf_op jit(solution)/shard_map/all_to_all | solution.py:84
  511.5 5.4 multiply_reduce_fusion
  518.4 7.7 add_convert_fusion
  527.4 436.5 %all-reduce.4.cloned.1.call-done = f32[7,4096]{1,0:T(8,128)} async-done(((f32[7,4096]{1,0:T(8,128)}), f32[7,4096]{1,0:T(8,128)}) %all-reduce.4.cloned.1.call-update) | async-done | bytes 114704 | tf_op jit(solution)/shard_map/psum | solution.py:89
  (87 shorter events, 51.3 us)
Async XLA Ops:
  35.8 246.2 %all-to-all-start = ((bf16[128,2,2048]{2,1,0:T(2,128)(2,1)}), bf16[128,2,2048]{2,1,0:T(2,128)(2,1)S(1)}, u32[]{:S(2)}, u32[]{:S(2)}) async-start(bf16[128,2,2048]{2,1,0:T(2,128)(2,1)} %reshape.273), calls=%async_computation | async-start | bytes 2097152 | tf_op jit(solution)/shard_map/all_to_all | solution.py:82
  164.9 18.7 %copy-start = (bf16[523776]{0:T(1024)(128)(2,1)S(1)}, bf16[523776]{0:T(1024)(128)(2,1)}, u32[]{:S(2)}) copy-start(bf16[523776]{0:T(1024)(128)(2,1)} %slice_reduce_fusion.8) | copy-start | bytes 3142660
  186.3 3.9 copy-start.1
  192.8 4.0 copy-start.2
  269.1 6.7 copy-start.6
  271.8 4.9 copy-start.5
  271.8 5.8 copy-start.4
  273.9 4.7 copy-start.3
  275.9 3.6 copy-start.7
  276.7 3.6 copy-start.8
  277.6 3.6 copy-start.9
  405.3 22.3 %copy-start.10 = (f32[7,4096]{1,0:T(8,128)S(1)}, f32[7,4096]{1,0:T(8,128)}, u32[]{:S(2)}) copy-start(f32[7,4096]{1,0:T(8,128)} %param.9) | copy-start | bytes 344068
  405.3 70.1 %all-to-all-start.1 = ((bf16[128,2,2048]{2,1,0:T(2,128)(2,1)}), bf16[128,2,2048]{2,1,0:T(2,128)(2,1)S(1)}, u32[]{:S(2)}, u32[]{:S(2)}) async-start(bf16[128,2,2048]{2,1,0:T(2,128)(2,1)} %reshape.275), calls=%async_computation.1 | async-start | bytes 2097152 | tf_op jit(solution)/shard_map/all_to_all | solution.py:84
  423.5 540.4 %all-reduce.4.cloned.1.call-start = ((), (), s32[]{:S(2)}) async-start(), calls=%async_computation.2 | async-start | bytes 262144 | tf_op jit(solution)/shard_map/psum | solution.py:89
  424.4 87.2 %collective-permute-start.1 = (bf16[1,6,4096]{2,1,0:T(8,128)(2,1)S(1)}, bf16[1,6,4096]{2,1,0:T(8,128)(2,1)S(1)}, u32[]{:S(2)}, u32[]{:S(2)}) collective-permute-start(bf16[1,6,4096]{2,1,0:T(8,128)(2,1)S(1)} %slice.225), channel_id=1, source_target_pairs={{0,1},{1,2},{2,3},{3,4},{4,5},{5,6},{6,7},{7,8},{8,9},{9,10},{10,1... | collective-permute-start | bytes 147464 | tf_op jit(solution)/shard_map/ppermute | solution.py:13
  508.1 9.8 %collective-permute-start = (bf16[1,6,4096]{2,1,0:T(8,128)(2,1)}, bf16[1,6,4096]{2,1,0:T(8,128)(2,1)S(1)}, u32[]{:S(2)}, u32[]{:S(2)}) collective-permute-start(bf16[1,6,4096]{2,1,0:T(8,128)(2,1)} %copy.39), channel_id=1, source_target_pairs={{1,0},{2,1},{3,2},{4,3},{5,4},{6,5},{7,6},{8,7},{9,8},{10,9},{11,1... | collective-permute-start | bytes 147464 | tf_op jit(solution)/shard_map/ppermute | solution.py:13
Sparse Core Ops, SparseCore 0:
  518.0 445.8 all-reduce.3
where the time goes:
time: 982 us; the launch traced here: 975 us
  waiting for transfers between devices  484 us (49%)
  local copies, waits for them, and re-layouts  289 us (29%)
  other arithmetic  132 us (13%)
  starting transfers between devices  45.5 us (5%)
  between operations  17.2 us (2%)
    psum x1, waiting for transfers between devices, per_device(): summed = lax.psum(partial_terms, ('dp', 'ctx')) / loss_scale[0]  437 us
    slice x9, local copies, waits for them, and re-layouts, lag_tiles(): jnp.tile(window, (1, width))[:, width:width + width * (2 * width - 1)]  166 us
    unnamed x3, other arithmetic  115 us
    unnamed x61, local copies, waits for them, and re-layouts  53.2 us
    all_to_all x1, waiting for transfers between devices, per_device(): lax.all_to_all(conv_cols, 'ctx', split_axis=1, concat_axis=2, tiled=True)  47.7 us
    reshape x9, local copies, waits for them, and re-layouts, lag_tiles(): return repeat.reshape(window.shape[0], width, 2 * width - 1)[:, :, :width]  28.9 us
    all_to_all x1, starting transfers between devices, per_device(): lax.all_to_all(gated, 'ctx', split_axis=2, concat_axis=1, tiled=True)  23.5 us
  transfers between devices with their start and end apart: 5, of which 2 were waited for; matrix products, arithmetic and copies ran while one was open for 28% of the time, Pallas kernels for 0%

commit v1 on v0

v1 whole, which is shorter than its diff:
```python
import functools

import jax
import jax.numpy as jnp
from jax import lax
from jax.experimental import pallas as pl
from jax.experimental.pallas import tpu as pltpu
from jax.sharding import PartitionSpec as P

PLANE = 8
BLK = 256
GW = 128
HEAD = 16
SHORT = 64
VMEM = 56 * 1024 * 1024
F32, BF16 = jnp.float32, jnp.bfloat16


def params(grid=True):
    kwargs = {"dimension_semantics": ("arbitrary",)} if grid else {}
    return pltpu.CompilerParams(vmem_limit_bytes=VMEM, **kwargs)


def cost(flops, nbytes):
    return pl.CostEstimate(
        flops=int(flops) // SHORT, bytes_accessed=int(nbytes) // SHORT, transcendentals=0
    )


def dot(a, b):
    return jnp.dot(a, b, preferred_element_type=F32)


def gate_kernel(up_ref, gate_ref, out_ref):
    width = out_ref.shape[2]
    for p in range(PLANE):
        cols = slice(p * width, (p + 1) * width)
        prod = up_ref[0, :, cols].astype(F32) * gate_ref[0, :, cols].astype(F32)
        out_ref[p] = prod.astype(BF16)


def gate(upstream, gates):
    _, rows, chans = upstream.shape
    return pl.pallas_call(
        gate_kernel,
        out_shape=jax.ShapeDtypeStruct((PLANE, rows, chans // PLANE), BF16),
        compiler_params=params(False),
        cost_estimate=cost(upstream.size, 6 * upstream.size),
        name="gate",
    )(upstream, gates)


def pack_kernel(src_ref, out_ref):
    width = out_ref.shape[2]
    for p in range(PLANE):
        out_ref[p] = src_ref[0, :, p * width : (p + 1) * width]


def pack(features):
    _, rows, chans = features.shape
    return pl.pallas_call(
        pack_kernel,
        out_shape=jax.ShapeDtypeStruct((PLANE, rows, chans // PLANE), BF16),
        compiler_params=params(False),
        cost_estimate=cost(0, 4 * features.size),
        name="pack",
    )(features)


def split_terms(x):
    high = x.astype(BF16)
    rest = x - high.astype(F32)
    mid = rest.astype(BF16)
    return high, mid, (rest - mid.astype(F32)).astype(BF16)


def prepare_kernel(lane, half_ref, scale_ref, copies, out_ref):
    total = copies[0]
    for n in range(1, copies.shape[0]):
        total = total + copies[n]
    unscaled = total / scale_ref[0]
    norm = jnp.sum(unscaled * unscaled, keepdims=True)
    norm = split_terms(jnp.broadcast_to(norm, (8, 8)))
    span = PLANE * lane
    mine = unscaled[:, :span]
    for n in range(1, unscaled.shape[1] // span):
        mine = jnp.where(half_ref[0] == n, unscaled[:, n * span : (n + 1) * span], mine)
    parts = split_terms(mine)
    pad = jnp.zeros((8, GW - 3 * lane - 24), BF16)
    for p in range(PLANE):
        row = [x[:, p * lane : (p + 1) * lane] for x in parts]
        tile = jnp.concatenate([*row, *norm, pad], axis=1).astype(F32)
        out_ref[p] = jnp.concatenate([tile, jnp.zeros_like(tile)], axis=0).astype(BF16)


def prepare(half, scale, copies, lane):
    return pl.pallas_call(
        functools.partial(prepare_kernel, lane),
        in_specs=[pl.BlockSpec(memory_space=pltpu.SMEM)] * 2 + [pl.BlockSpec(memory_space=pltpu.VMEM)],
        out_shape=jax.ShapeDtypeStruct((PLANE, HEAD, GW), BF16),
        compiler_params=params(False),
        cost_estimate=cost(copies.size, 4 * copies.size),
        name="prepare",
    )(half.reshape(1), scale, copies)


def unpack_kernel(lane, source_ref, got, out_ref, short_ref, norm_ref):
    width = got.shape[2]
    rows = out_ref.shape[1]
    norm = jnp.zeros((8, 1), F32)
    short = jnp.zeros((8, lane), F32)
    for p in range(PLANE):
        out_ref[0, :, p * width : (p + 1) * width] = got[p, :rows, :]
        tile = got[p, rows:, :GW].astype(F32)[:8]
        at = 3 * lane
        norm = norm + (tile[:, at : at + 1] + tile[:, at + 8 : at + 9] + tile[:, at + 16 : at + 17])
        terms = tile[:, :lane] + tile[:, lane : 2 * lane] + tile[:, 2 * lane : 3 * lane]
        short = jnp.where(source_ref[0] == p, terms, short)
    norm = jnp.sqrt(norm)
    short = jnp.where(jnp.abs(norm) < jnp.inf, short, jnp.zeros_like(short))
    short_ref[...] = short[: short_ref.shape[0], :]
    norm_ref[...] = norm[:1, :]


def unpack(source, got, rows, width, lane):
    return pl.pallas_call(
        functools.partial(unpack_kernel, lane),
        in_specs=[pl.BlockSpec(memory_space=pltpu.SMEM), pl.BlockSpec(memory_space=pltpu.VMEM)],
        out_shape=[
            jax.ShapeDtypeStruct((1, rows, PLANE * got.shape[2]), BF16),
            jax.ShapeDtypeStruct((width, lane), F32),
            jax.ShapeDtypeStruct((1, 1), F32),
        ],
        compiler_params=params(False),
        cost_estimate=cost(0, 4 * got.size),
        name="unpack",
    )(source.reshape(1), got)


def toeplitz_kernel(taps_ref, all_ref, far_ref):
    taps = taps_ref.shape[2]
    half = BLK // 2
    row = jnp.concatenate([taps_ref[0], jnp.zeros((1, BLK), F32)], axis=1)
    base = jnp.broadcast_to(row, (half, taps + BLK))
    base = pltpu.roll(base, 0, 1, stride=1, stride_axis=0).astype(BF16)
    all_ref[0, :half, :] = base
    all_ref[0, half:, :half] = jnp.zeros((half, half), BF16)
    all_ref[0, half:, half:] = base[:, : taps + BLK - half]
    far_ref[0] = all_ref[0, :, taps - 7 * BLK :]


def toeplitz(filters):
    groups, taps = filters.shape
    return pl.pallas_call(
        toeplitz_kernel,
        grid=(groups,),
        in_specs=[pl.BlockSpec((1, 1, taps), lambda g: (g, 0, 0))],
        out_specs=[
            pl.BlockSpec((1, BLK, taps + BLK), lambda g: (g, 0, 0)),
            pl.BlockSpec((1, BLK, 8 * BLK), lambda g: (g, 0, 0)),
        ],
        out_shape=[
            jax.ShapeDtypeStruct((groups, BLK, taps + BLK), BF16),
            jax.ShapeDtypeStruct((groups, BLK, 8 * BLK), BF16),
        ],
        compiler_params=params(),
        cost_estimate=cost(groups * BLK * taps * 16, 2 * groups * BLK * taps * 3),
        name="toeplitz",
    )(filters.astype(F32).reshape(groups, 1, taps))


def fill_pairs(pairs_ref, planes):
    rows = sum(x.shape[0] for x in planes)
    zero = jnp.zeros((BLK, GW), BF16)
    pairs_ref[:BLK, :GW] = zero
    at = 0
    for x in planes:
        pairs_ref[BLK + at : BLK + at + x.shape[0], :GW] = x[...]
        pairs_ref[at : at + x.shape[0], GW:] = x[...]
        at += x.shape[0]
    pairs_ref[rows : rows + BLK, GW:] = zero


def tile_products(tiles_ref, first, last, pairs_ref, distance, blocks):
    out = []
    for pair in (0, 2):
        low, high = distance - 1 - pair, distance + blocks - 1 - pair
        k0, k1 = max(low, first), min(high, last)
        tiles = tiles_ref[0, :, (k0 - first) * BLK : (k1 + 1 - first) * BLK]
        window = pairs_ref[(k0 - low) * BLK : (k1 + 1 - low) * BLK, :]
        out.append(dot(tiles, window))
    return out


def store_rows(ref, products, add=None):
    for n, prod in enumerate(products):
        for m in range(2):
            rows = slice((2 * n + m) * BLK, (2 * n + m + 1) * BLK)
            value = prod[:, m * GW : (m + 1) * GW]
            ref[rows, :] = value if add is None else add[rows, :] + value


def correlate(conv_ref, feat_ref, before, feat_wide, terms):
    rows = conv_ref.shape[0]
    feat_wide[:8, :] = before[before.shape[0] - 8 :, :].astype(F32)
    feat_wide[8:, :] = feat_ref[...].astype(F32)
    for r in range(0, rows, 128):
        conv = conv_ref[r : r + 128, :]
        for j in range(len(terms)):
            prod = conv * feat_wide[r + 8 - j : r + 136 - j, :]
            terms[j] = terms[j] + jnp.sum(prod.reshape(16, 8, GW), axis=0)
    return terms


def add_terms(raw_ref, terms, add=None):
    out = [jnp.sum(t, axis=0, keepdims=True) for t in terms]
    out.append(jnp.zeros((8 - len(terms), GW), F32))
    out = jnp.concatenate(out, axis=0)
    raw_ref[...] = out if add is None else add[...] + out


def put_terms(raw_ref, terms, add=None):
    out = [jnp.sum(t, axis=0, keepdims=True) for t in terms]
    out.append(jnp.zeros((8 - len(terms), GW), F32))
    out = jnp.concatenate(out, axis=0)
    raw_ref[...] = out if add is None else add[...] + out


def by_group(kernel, name, flops, args, outs, scratch):
    groups = outs[0].shape[1] // GW

    def spec(x):
        if len(x.shape) == 3:
            return pl.BlockSpec((1,) + x.shape[1:], lambda g: (g, 0, 0))
        return pl.BlockSpec((x.shape[0], GW), lambda g: (0, g))

    moved = sum(x.size * x.dtype.itemsize for x in (*args, *outs))
    return pl.pallas_call(
        kernel,
        grid=(groups,),
        in_specs=[spec(x) for x in args],
        out_specs=[spec(x) for x in outs],
        out_shape=outs,
        scratch_shapes=scratch,
        compiler_params=params(),
        cost_estimate=cost(flops * groups, moved),
        name=name,
    )(*args)


def pairs_of(rows):
    return pltpu.VMEM((rows + BLK, 2 * GW), BF16)


def early_kernel(x0, x1, tiles, acc_ref, mid_ref, pairs):
    last = tiles.shape[2] // BLK - 1
    fill_pairs(pairs, [x0, x1])
    store_rows(acc_ref, tile_products(tiles, 0, last, pairs, 0, 8))
    fill_pairs(pairs, [x1])
    store_rows(mid_ref, tile_products(tiles, 0, last, pairs, 8, 4))


def early(x0, x1, tiles):
    rows, own = x0.shape
    out = jax.ShapeDtypeStruct((rows, own), F32)
    return by_group(
        early_kernel, "early", 24 * rows * rows * GW, [x0, x1, tiles], [out, out], [pairs_of(2 * rows)]
    )


def own_terms_kernel(width, acc, f0, f1, raw_ref, feat_wide):
    terms = [jnp.zeros((8, GW), F32)] * width
    before = f1[f1.shape[0] - HEAD :, :]
    put_terms(raw_ref, correlate(acc, f0, before, feat_wide, terms))


def own_terms(width, acc, f0, f1):
    rows, own = acc.shape
    out = jax.ShapeDtypeStruct((8, own), F32)
    scratch = [pltpu.VMEM((rows + 8, GW), F32)]
    kernel = functools.partial(own_terms_kernel, width)
    return by_group(kernel, "own_terms", 14 * rows * GW, [acc, f0, f1], [out], scratch)[0]


def far_terms_kernel(width, mid, raw, x2, f1, f2, f3_tail, tiles, raw_ref, pairs, far, feat_wide):
    fill_pairs(pairs, [x2])
    terms = [jnp.zeros((8, GW), F32)] * width
    before = f2[f2.shape[0] - HEAD :, :]
    store_rows(far, tile_products(tiles, 9, 16, pairs, 12, 4), add=mid)
    terms = correlate(far, f1, before, feat_wide, terms)
    store_rows(far, tile_products(tiles, 9, 16, pairs, 16, 4))
    terms = correlate(far, f2, f3_tail[...], feat_wide, terms)
    put_terms(raw_ref, terms, add=raw)


def far_terms(width, mid, raw, x2, f1, f2, f3_tail, tiles):
    rows, own = mid.shape
    out = jax.ShapeDtypeStruct((8, own), F32)
    scratch = [pairs_of(rows), pltpu.VMEM((rows, GW), F32), pltpu.VMEM((rows + 8, GW), F32)]
    kernel = functools.partial(far_terms_kernel, width)
    args = [mid, raw, x2, f1, f2, f3_tail, tiles]
    return by_group(kernel, "far_terms", 16 * rows * rows * GW, args, [out], scratch)[0]


def third_kernel(acc_in, x2, x3, x4_head, tiles, acc_ref, head_ref, pairs):
    last = tiles.shape[2] // BLK - 1
    fill_pairs(pairs, [x2, x3])
    store_rows(acc_ref, tile_products(tiles, 0, last, pairs, 8, 8), add=acc_in)
    ahead = jnp.concatenate([x4_head[...], jnp.zeros((GW - HEAD, GW), BF16)], axis=0)
    corner = tiles[0, :HEAD, last * BLK : last * BLK + GW]
    head_ref[...] = (acc_ref[:HEAD, :] + dot(corner, ahead)).astype(BF16)


def third(acc, x2, x3, x4_head, tiles):
    rows, own = acc.shape
    outs = [jax.ShapeDtypeStruct((rows, own), F32), jax.ShapeDtypeStruct((HEAD, own), BF16)]
    args = [acc, x2, x3, x4_head, tiles]
    return by_group(third_kernel, "third", 18 * rows * rows * GW, args, outs, [pairs_of(2 * rows)])


def last_kernel(width, acc_in, x4, tiles, next_head, taps, extra, out_ref, pairs, wide):
    rows = x4.shape[0]
    step = rows // PLANE
    fill_pairs(pairs, [x4])
    for n, prod in enumerate(tile_products(tiles, 13, 16, pairs, 16, 4)):
        for m in range(2):
            at = slice((2 * n + m) * BLK, (2 * n + m + 1) * BLK)
            value = acc_in[at, :] + prod[:, m * GW : (m + 1) * GW]
            wide[at, :] = value.astype(BF16).astype(F32)
    wide[rows:, :] = next_head[:8, :].astype(F32)
    for r in range(PLANE):
        total = taps[0:1, :] * wide[r * step : (r + 1) * step, :]
        for j in range(1, width):
            total = total + taps[j : j + 1, :] * wide[r * step + j : (r + 1) * step + j, :]
        out_ref[r, :step, :] = total.astype(BF16)
        out_ref[r, step:, :] = extra[r]


def finish(width, acc, x4, tiles, next_head, taps, extra):
    rows, own = x4.shape
    groups = own // GW
    step = rows // PLANE + HEAD
    col = pl.BlockSpec((rows, GW), lambda g: (0, g))
    return pl.pallas_call(
        functools.partial(last_kernel, width),
        grid=(groups,),
        in_specs=[
            col,
            col,
            pl.BlockSpec((1, BLK, 4 * BLK), lambda g: (g, 0, 1)),
            pl.BlockSpec((HEAD, GW), lambda g: (0, g)),
            pl.BlockSpec((width, GW), lambda g: (0, g)),
            pl.BlockSpec((PLANE, HEAD, GW), lambda g: (0, 0, 0)),
        ],
        out_specs=pl.BlockSpec((PLANE, step, GW), lambda g: (0, 0, g)),
        out_shape=jax.ShapeDtypeStruct((PLANE, step, own), BF16),
        scratch_shapes=[
            pltpu.VMEM((rows + BLK, 2 * GW), BF16),
            pltpu.VMEM((rows + 8, GW), F32),
        ],
        compiler_params=params(),
        cost_estimate=cost(2 * 3 * rows * rows * GW * groups, 8 * rows * own),
        name="finish",
    )(acc, x4, tiles, next_head, taps, extra)


def per_device(features, gate_values, upstream, short_filter, long_filter, loss_scale):
    shards = lax.axis_size("ctx")
    planes = shards // PLANE
    index = lax.axis_index("ctx")
    z, p = index // PLANE, index % PLANE
    width, chans = short_filter.shape
    own = chans // PLANE
    groups = own // GW
    rows = PLANE * features.shape[1]
    in_plane = [[k * PLANE + i for i in range(PLANE)] for k in range(planes)]
    along_z = [[k * PLANE + i for k in range(planes)] for i in range(PLANE)]

    def swap(x):
        return lax.all_to_all(x, "ctx", 0, 0, axis_index_groups=in_plane, tiled=True)

    def hop(x, count):
        step = PLANE * count
        route = [(i, i + step) for i in range(shards) if 0 <= i + step < shards]
        return lax.ppermute(x, "ctx", route)

    def after(x, *others):
        return lax.optimization_barrier((x,) + others)[0]

    packed = gate(upstream, gate_values)
    feat1 = hop(features, 1)
    x0 = swap(packed)
    filters = lax.dynamic_slice_in_dim(after(long_filter, packed), p * groups, groups, 0)
    taps = lax.dynamic_slice_in_dim(after(short_filter, packed), p * own, own, 1)
    tiles, far_tiles = toeplitz(filters)
    x0 = x0.reshape(rows, own)
    feat1 = swap(pack(after(feat1, x0)))
    x1 = after(hop(x0, -1), feat1, tiles)
    feat0 = swap(pack(after(features, feat1)))
    feat0, feat1 = (x.reshape(rows, own) for x in (feat0, feat1))

    feat2 = hop(feat1, 1)
    feat3_tail = hop(feat1[rows - HEAD :], 2)
    x4_head = hop(x0[:HEAD], -4)

    acc, mid = early(x0, x1, tiles)
    x2 = after(hop(x1, -1), acc, feat0, feat2, x4_head)
    raw = own_terms(width, acc, feat0, feat1)
    raw = far_terms(width, mid, raw, x2, feat1, feat2, feat3_tail, far_tiles)
    raw = lax.psum(raw, "dp")
    x3 = after(hop(x2, -1), raw)
    x4 = hop(x3, -1)
    acc, head = third(acc, x2, x3, x4_head, tiles)
    next_head = hop(head, -1)

    raw = after(raw, x3, head)
    copies = jnp.broadcast_to(raw[None], (planes,) + raw.shape)
    copies = lax.all_to_all(copies, "ctx", 0, 0, axis_index_groups=along_z, tiled=True)
    lane = chans // shards
    spans = own // lane // PLANE
    extra = prepare(z % spans, loss_scale, after(copies, x4), lane)
    got = swap(finish(width, acc, x4, far_tiles, next_head, taps, extra))
    input_grad, short_grad, norm_value = unpack(z // spans, got, rows // PLANE, width, lane)
    return (input_grad, short_grad, norm_value.reshape(1))


def solution(mesh):
    placed = (P("dp", "ctx", None), P("dp", "ctx", None), P("dp", "ctx", None), P(), P(), P())
    return jax.shard_map(
        per_device,
        mesh=mesh,
        in_specs=placed,
        out_specs=(P("dp", "ctx", None), P(None, "ctx"), P()),
        check_vma=False,
    )
```

time: 982 us -> 195 us (0.20)
  the two profiles are of different devices: /device:TPU:1 before, /device:TPU:34 now
where the time goes in v1:
time: 195 us; the launch traced here: 194 us
  starting transfers between devices  52 us (27%)
  Pallas kernels  51.5 us (26%)
  waiting for transfers between devices  47.6 us (24%)
  blocking collectives  33.5 us (17%)
  local copies, waits for them, and re-layouts  6.88 us (4%)
    pallas_call x4, Pallas kernels, by_group(): pl.pallas_call(kernel, grid=(groups,), in_specs=[spec(x) for x in args],...  28.5 us
    ppermute x9, starting transfers between devices, hop(): return lax.ppermute(x, 'ctx', route)  27.6 us
    all_to_all x1, blocking collectives, swap(): lax.all_to_all(x, 'ctx', 0, 0, axis_index_groups=in_plane, tiled=True)  22.9 us
    all_to_all x1, waiting for transfers between devices, per_device(): lax.all_to_all(copies, 'ctx', 0, 0, axis_index_groups=along_z, tiled=True)  17.7 us
    ppermute x9, waiting for transfers between devices, hop(): return lax.ppermute(x, 'ctx', route)  15.3 us
    all_to_all x3, waiting for transfers between devices, swap(): lax.all_to_all(x, 'ctx', 0, 0, axis_index_groups=in_plane, tiled=True)  14.6 us
    all_to_all x1, starting transfers between devices, per_device(): lax.all_to_all(copies, 'ctx', 0, 0, axis_index_groups=along_z, tiled=True)  13.1 us
    all_to_all x3, starting transfers between devices, swap(): lax.all_to_all(x, 'ctx', 0, 0, axis_index_groups=in_plane, tiled=True)  11.3 us
  transfers between devices with their start and end apart: 13, of which 4 were waited for; matrix products, arithmetic and copies ran while one was open for 1% of the time, Pallas kernels for 22%

profile of v1, /device:TPU:34, one launch (start us, length us, event | category | flops | bytes accessed | tf_op | source)
XLA Modules:
  0.0 193.9 jit_solution(15085755778215089232)
XLA Ops:
  0.6 4.0 %collective-permute-start.1 = (bf16[1,128,4096]{2,1,0:T(8,128)(2,1)}, bf16[1,128,4096]{2,1,0:T(8,128)(2,1)S(1)}, u32[]{:S(2)}, u32[]{:S(2)}) collective-permute-start(bf16[1,128,4096]{2,1,0:T(8,128)(2,1)} %src_ref), channel_id=1, source_target_pairs={{0,8},{1,9},{2,10},{3,11},{4,12},{5,13},{6,14},{7,15},{8,16},{9,17... | collective-permute-start | bytes 3145736 | tf_op jit(solution)/shard_map/ppermute | solution.py:385
  4.6 2.8 %gate.1 = bf16[8,128,512]{2,1,0:T(8,128)(2,1)} custom-call(bf16[1,128,4096]{2,1,0:T(8,128)(2,1)} %up_ref.1, bf16[1,128,4096]{2,1,0:T(8,128)(2,1)} %gate_ref.1), custom_call_target="tpu_custom_call" | custom-call | flops 8192 | bytes 49152 | tf_op jit(solution)/shard_map/gate/pallas_call | solution.py:44
  7.4 22.9 %all_to_all.25 = bf16[8,128,512]{2,1,0:T(8,128)(2,1)S(1)} all-to-all(bf16[8,128,512]{2,1,0:T(8,128)(2,1)} %gate.1), channel_id=1, replica_groups={{0,1,2,3,4,5,6,7},{8,9,10,11,12,13,14,15},{16,17,18,19,20,21,22,23},{24..., dimensions={0} | all-to-all | bytes 2097152 | tf_op jit(solution)/shard_map/all_to_all | solution.py:380
  30.3 2.1 %collective-permute-start = (bf16[1024,512]{1,0:T(8,128)(2,1)S(1)}, bf16[1024,512]{1,0:T(8,128)(2,1)S(1)}, u32[]{:S(2)}, u32[]{:S(2)}) collective-permute-start(bf16[1024,512]{1,0:T(8,128)(2,1)S(1)} %bitcast.10), channel_id=1, source_target_pairs={{8,0},{9,1},{10,2},{11,3},{12,4},{13,5},{14,6},{15,7},{16,8},{17,9... | collective-permute-start | bytes 3145736 | tf_op jit(solution)/shard_map/ppermute | solution.py:385
  33.3 2.3 %pack.2 = bf16[8,128,512]{2,1,0:T(8,128)(2,1)} custom-call(bf16[1,128,4096]{2,1,0:T(8,128)(2,1)} %copy-done.6), custom_call_target="tpu_custom_call" | custom-call | bytes 32768 | tf_op jit(solution)/shard_map/pack/pallas_call | solution.py:61
  35.6 3.6 %all-to-all-start.1 = ((bf16[8,128,512]{2,1,0:T(8,128)(2,1)}), bf16[8,128,512]{2,1,0:T(8,128)(2,1)S(1)}, u32[]{:S(2)}, u32[]{:S(2)}) async-start(bf16[8,128,512]{2,1,0:T(8,128)(2,1)} %pack.2), calls=%async_computation.1 | async-start | bytes 2097152 | tf_op jit(solution)/shard_map/all_to_all | solution.py:380
  40.7 6.0 %toeplitz.1 = (bf16[4,256,4352]{2,1,0:T(8,128)(2,1)}, bf16[4,256,2048]{2,1,0:T(8,128)(2,1)}) custom-call(f32[4,1,4096]{2,1,0:T(1,128)} %reshape.39.taps_ref), custom_call_target="tpu_custom_call" | custom-call | flops 1048576 | bytes 393216 | tf_op jit(solution)/shard_map/toeplitz/pallas_call | solution.py:154
  46.7 8.4 %collective-permute-done.x1 = bf16[1024,512]{1,0:T(8,128)(2,1)S(1)} collective-permute-done((bf16[1024,512]{1,0:T(8,128)(2,1)S(1)}, bf16[1024,512]{1,0:T(8,128)(2,1)S(1)}, u32[]{:S(2)}, u32[]{:S(2)}) %collective-permute-start) | collective-permute-done | bytes 1048608 | tf_op jit(solution)/shard_map/ppermute | solution.py:385
  55.1 1.0 copy-done.8
  56.1 2.0 %collective-permute-start.2 = (bf16[1024,512]{1,0:T(8,128)(2,1)}, bf16[1024,512]{1,0:T(8,128)(2,1)S(1)}, u32[]{:S(2)}, u32[]{:S(2)}) collective-permute-start(bf16[1024,512]{1,0:T(8,128)(2,1)} %copy-done.8), channel_id=1, source_target_pairs={{8,0},{9,1},{10,2},{11,3},{12,4},{13,5},{14,6},{15,7},{16,8},{17,9... | collective-permute-start | bytes 3145736 | tf_op jit(solution)/shard_map/ppermute | solution.py:385
  58.1 4.9 %collective-permute-start.3 = (bf16[1024,512]{1,0:T(8,128)(2,1)S(1)}, bf16[1024,512]{1,0:T(8,128)(2,1)}, u32[]{:S(2)}, u32[]{:S(2)}) collective-permute-start(bf16[1024,512]{1,0:T(8,128)(2,1)S(1)} %bitcast.6), channel_id=1, source_target_pairs={{0,8},{1,9},{2,10},{3,11},{4,12},{5,13},{6,14},{7,15},{8,16},{9,17... | collective-permute-start | bytes 3145736 | tf_op jit(solution)/shard_map/ppermute | solution.py:385
  63.0 2.3 %pack.3 = bf16[8,128,512]{2,1,0:T(8,128)(2,1)} custom-call(bf16[1,128,4096]{2,1,0:T(8,128)(2,1)} %src_ref), custom_call_target="tpu_custom_call" | custom-call | bytes 32768 | tf_op jit(solution)/shard_map/pack/pallas_call | solution.py:61
  65.4 4.2 %all-to-all-start.2 = ((bf16[8,128,512]{2,1,0:T(8,128)(2,1)}), bf16[8,128,512]{2,1,0:T(8,128)(2,1)}, u32[]{:S(2)}, u32[]{:S(2)}) async-start(bf16[8,128,512]{2,1,0:T(8,128)(2,1)} %pack.3), calls=%async_computation.2 | async-start | bytes 2097152 | tf_op jit(solution)/shard_map/all_to_all | solution.py:380
  69.6 1.3 collective-permute-start.4
  70.9 8.5 %early.1 = (f32[1024,512]{1,0:T(8,128)}, f32[1024,512]{1,0:T(8,128)}) custom-call(bf16[1024,512]{1,0:T(8,128)(2,1)} %bitcast.12, bf16[1024,512]{1,0:T(8,128)(2,1)} %copy-done.8, bf16[4,256,4352]{2,1,0:T(8,128)(2,1)} %get-tuple-element.23.tiles), custom_call_target="tpu_custom_call" | custom-call | flops 201326592 | bytes 237568 | tf_op jit(solution)/shard_map/early/pallas_call | solution.py:238
  79.4 6.9 %collective-permute-done.4.x4_head = bf16[16,512]{1,0:T(8,128)(2,1)S(1)} collective-permute-done((bf16[16,512]{1,0:T(8,128)(2,1)S(1)}, bf16[16,512]{1,0:T(8,128)(2,1)S(1)}, u32[]{:S(2)}, u32[]{:S(2)}) %collective-permute-start.4) | collective-permute-done | bytes 16416 | tf_op jit(solution)/shard_map/ppermute | solution.py:385
  86.3 4.4 %collective-permute-start.5 = (bf16[1024,512]{1,0:T(8,128)(2,1)S(1)}, bf16[1024,512]{1,0:T(8,128)(2,1)S(1)}, u32[]{:S(2)}, u32[]{:S(2)}) collective-permute-start(bf16[1024,512]{1,0:T(8,128)(2,1)S(1)} %collective-permute-done.2.x2), channel_id=1, source_target_pairs={{8,0},{9,1},{10,2},{11,3},{12,4},{13,5},{14,6},{15,7},{16,8},{17,9... | collective-permute-start | bytes 3145736 | tf_op jit(solution)/shard_map/ppermute | solution.py:385
  90.8 5.0 %collective-permute-start.6 = (bf16[16,512]{1,0:T(8,128)(2,1)S(1)}, bf16[16,512]{1,0:T(8,128)(2,1)S(1)}, u32[]{:S(2)}, u32[]{:S(2)}) collective-permute-start(bf16[16,512]{1,0:T(8,128)(2,1)S(1)} %slice.9), channel_id=1, source_target_pairs={{0,16},{1,17},{2,18},{3,19},{4,20},{5,21},{6,22},{7,23},{8,24},{9,... | collective-permute-start | bytes 49160 | tf_op jit(solution)/shard_map/ppermute | solution.py:385
  95.8 4.2 %own_terms.1.raw = f32[8,512]{1,0:T(8,128)} custom-call(f32[1024,512]{1,0:T(8,128)} %get-tuple-element.25.acc.acc_in, bf16[1024,512]{1,0:T(8,128)(2,1)} %bitcast.2.f0, bf16[1024,512]{1,0:T(8,128)(2,1)} %bitcast.8), custom_call_target="tpu_custom_call" | custom-call | flops 114688 | bytes 65792 | tf_op jit(solution)/shard_map/own_terms/pallas_call | solution.py:238
  100.6 7.8 %far_terms.1 = f32[8,512]{1,0:T(8,128)} custom-call(f32[1024,512]{1,0:T(8,128)} %get-tuple-element.28.mid, f32[8,512]{1,0:T(8,128)} %own_terms.1.raw, bf16[1024,512]{1,0:T(8,128)(2,1)} %copy-done.4, bf16[1024,512]{1,0:T(8,128)(2,1)} %bitcast.9, bf16[1024,512]{1,0:T(8,128)(2,1)} %collective-permute-done.3.f2, bf16[16,512]{1,0:T(8,128)(2,1)} %copy-done.12, ...), custom_call_target="tpu_custom_call" | custom-call | flops 134217728 | bytes 148224 | tf_op jit(solution)/shard_map/far_terms/pallas_call | solution.py:238
  108.4 10.6 %psum.7 = f32[8,512]{1,0:T(8,128)S(1)} all-reduce(f32[8,512]{1,0:T(8,128)} %far_terms.1), channel_id=1, replica_groups=mesh['dp'=4,'ctx'=128] {'dp'}, use_global_device_ids=true, to_apply=%region_0.1 | all-reduce | flops 4096 | bytes 32768 | tf_op jit(solution)/shard_map/psum | solution.py:410
  119.0 1.9 collective-permute-start.7
  120.9 8.0 %third.1 = (f32[1024,512]{1,0:T(8,128)}, bf16[16,512]{1,0:T(8,128)(2,1)}) custom-call(f32[1024,512]{1,0:T(8,128)} %get-tuple-element.25.acc.acc_in, bf16[1024,512]{1,0:T(8,128)(2,1)} %copy-done.4, bf16[1024,512]{1,0:T(8,128)(2,1)} %copy-done.5, bf16[16,512]{1,0:T(8,128)(2,1)} %copy-done.11, bf16[4,256,4352]{2,1,0:T(8,128)(2,1)} %get-tuple-element.23.tiles), custom_call_target="tpu_custom_call" | custom-call | flops 150994944 | bytes 238080 | tf_op jit(solution)/shard_map/third/pallas_call | solution.py:238
  129.7 13.1 %all-to-all-start.3 = ((f32[16,8,512]{2,1,0:T(8,128)}), f32[16,8,512]{2,1,0:T(8,128)S(1)}, u32[]{:S(2)}, u32[]{:S(2)}) async-start(f32[16,8,512]{2,1,0:T(8,128)} %broadcast_in_dim.2), calls=%async_computation.3 | async-start | bytes 524288 | tf_op jit(solution)/shard_map/all_to_all | solution.py:418
  142.8 2.0 %collective-permute-start.8 = (bf16[16,512]{1,0:T(8,128)(2,1)}, bf16[16,512]{1,0:T(8,128)(2,1)S(1)}, u32[]{:S(2)}, u32[]{:S(2)}) collective-permute-start(bf16[16,512]{1,0:T(8,128)(2,1)} %get-tuple-element.32), channel_id=1, source_target_pairs={{8,0},{9,1},{10,2},{11,3},{12,4},{13,5},{14,6},{15,7},{16,8},{17,9... | collective-permute-start | bytes 49160 | tf_op jit(solution)/shard_map/ppermute | solution.py:385
  146.1 17.7 %all-to-all-done.3.copies = f32[16,8,512]{2,1,0:T(8,128)S(1)} async-done(((f32[16,8,512]{2,1,0:T(8,128)}), f32[16,8,512]{2,1,0:T(8,128)S(1)}, u32[]{:S(2)}, u32[]{:S(2)}) %all-to-all-start.3) | async-done | bytes 262176 | tf_op jit(solution)/shard_map/all_to_all | solution.py:418
  164.5 1.7 prepare.1.extra
  166.8 5.6 %finish.1 = bf16[8,144,512]{2,1,0:T(8,128)(2,1)} custom-call(f32[1024,512]{1,0:T(8,128)} %get-tuple-element.31.acc_in, bf16[1024,512]{1,0:T(8,128)(2,1)} %copy-done.9, bf16[4,256,2048]{2,1,0:T(8,128)(2,1)} %get-tuple-element.29.tiles, bf16[16,512]{1,0:T(8,128)(2,1)} %copy-done.10, f32[7,512]{1,0:T(8,128)} %constant_dynamic-slice_fusion.taps, ...), custom_call_target="tpu_custom_call" | custom-call | flops 50331648 | bytes 65536 | tf_op jit(solution)/shard_map/finish/pallas_call | solution.py:344
  172.4 3.6 %all-to-all-start.4 = ((bf16[8,144,512]{2,1,0:T(8,128)(2,1)}), bf16[8,144,512]{2,1,0:T(8,128)(2,1)S(1)}, u32[]{:S(2)}, u32[]{:S(2)}) async-start(bf16[8,144,512]{2,1,0:T(8,128)(2,1)} %finish.1), calls=%async_computation.4 | async-start | bytes 2359296 | tf_op jit(solution)/shard_map/all_to_all | solution.py:380
  176.0 14.6 %all-to-all-done.4.got = bf16[8,144,512]{2,1,0:T(8,128)(2,1)S(1)} async-done(((bf16[8,144,512]{2,1,0:T(8,128)(2,1)}), bf16[8,144,512]{2,1,0:T(8,128)(2,1)S(1)}, u32[]{:S(2)}, u32[]{:S(2)}) %all-to-all-start.4) | async-done | bytes 1179680 | tf_op jit(solution)/shard_map/all_to_all | solution.py:380
  190.5 1.0 copy-done.2
  191.6 2.4 %unpack.1 = (bf16[1,128,4096]{2,1,0:T(8,128)(2,1)}, f32[7,32]{1,0:T(8,128)}, f32[1,1]{1,0:T(1,128)}) custom-call(s32[1]{0:T(128)} %bitcast.source_ref, bf16[8,144,512]{2,1,0:T(8,128)(2,1)} %copy-done.2), custom_call_target="tpu_custom_call" | custom-call | bytes 36864 | tf_op jit(solution)/shard_map/unpack/pallas_call | solution.py:126
  (39 shorter events, 5.8 us)
Async XLA Ops:
  0.6 144.2 %copy-start = (f32[7,4096]{1,0:T(8,128)S(1)}, f32[7,4096]{1,0:T(8,128)}, u32[]{:S(2)}) copy-start(f32[7,4096]{1,0:T(8,128)} %param.9) | copy-start | bytes 344068
  0.6 31.7 %collective-permute-start.1 = (bf16[1,128,4096]{2,1,0:T(8,128)(2,1)}, bf16[1,128,4096]{2,1,0:T(8,128)(2,1)S(1)}, u32[]{:S(2)}, u32[]{:S(2)}) collective-permute-start(bf16[1,128,4096]{2,1,0:T(8,128)(2,1)} %src_ref), channel_id=1, source_target_pairs={{0,8},{1,9},{2,10},{3,11},{4,12},{5,13},{6,14},{7,15},{8,16},{9,17... | collective-permute-start | bytes 3145736 | tf_op jit(solution)/shard_map/ppermute | solution.py:385
  30.3 39.3 %copy-start.3 = (bf16[8,128,512]{2,1,0:T(8,128)(2,1)}, bf16[8,128,512]{2,1,0:T(8,128)(2,1)S(1)}, u32[]{:S(2)}) copy-start(bf16[8,128,512]{2,1,0:T(8,128)(2,1)S(1)} %all_to_all.25) | copy-start | bytes 3145732
  30.3 24.8 %collective-permute-start = (bf16[1024,512]{1,0:T(8,128)(2,1)S(1)}, bf16[1024,512]{1,0:T(8,128)(2,1)S(1)}, u32[]{:S(2)}, u32[]{:S(2)}) collective-permute-start(bf16[1024,512]{1,0:T(8,128)(2,1)S(1)} %bitcast.10), channel_id=1, source_target_pairs={{8,0},{9,1},{10,2},{11,3},{12,4},{13,5},{14,6},{15,7},{16,8},{17,9... | collective-permute-start | bytes 3145736 | tf_op jit(solution)/shard_map/ppermute | solution.py:385
  32.3 1.0 copy-start.6
  35.6 19.5 %all-to-all-start.1 = ((bf16[8,128,512]{2,1,0:T(8,128)(2,1)}), bf16[8,128,512]{2,1,0:T(8,128)(2,1)S(1)}, u32[]{:S(2)}, u32[]{:S(2)}) async-start(bf16[8,128,512]{2,1,0:T(8,128)(2,1)} %pack.2), calls=%async_computation.1 | async-start | bytes 2097152 | tf_op jit(solution)/shard_map/all_to_all | solution.py:380
  55.1 1.0 copy-start.8
  56.1 34.7 %copy-start.1 = (bf16[8,128,512]{2,1,0:T(8,128)(2,1)}, bf16[8,128,512]{2,1,0:T(8,128)(2,1)S(1)}, u32[]{:S(2)}) copy-start(bf16[8,128,512]{2,1,0:T(8,128)(2,1)S(1)} %all-to-all-done.1) | copy-start | bytes 3145732
  56.1 30.2 %collective-permute-start.2 = (bf16[1024,512]{1,0:T(8,128)(2,1)}, bf16[1024,512]{1,0:T(8,128)(2,1)S(1)}, u32[]{:S(2)}, u32[]{:S(2)}) collective-permute-start(bf16[1024,512]{1,0:T(8,128)(2,1)} %copy-done.8), channel_id=1, source_target_pairs={{8,0},{9,1},{10,2},{11,3},{12,4},{13,5},{14,6},{15,7},{16,8},{17,9... | collective-permute-start | bytes 3145736 | tf_op jit(solution)/shard_map/ppermute | solution.py:385
  58.1 28.2 %collective-permute-start.3 = (bf16[1024,512]{1,0:T(8,128)(2,1)S(1)}, bf16[1024,512]{1,0:T(8,128)(2,1)}, u32[]{:S(2)}, u32[]{:S(2)}) collective-permute-start(bf16[1024,512]{1,0:T(8,128)(2,1)S(1)} %bitcast.6), channel_id=1, source_target_pairs={{0,8},{1,9},{2,10},{3,11},{4,12},{5,13},{6,14},{7,15},{8,16},{9,17... | collective-permute-start | bytes 3145736 | tf_op jit(solution)/shard_map/ppermute | solution.py:385
  65.4 20.9 %all-to-all-start.2 = ((bf16[8,128,512]{2,1,0:T(8,128)(2,1)}), bf16[8,128,512]{2,1,0:T(8,128)(2,1)}, u32[]{:S(2)}, u32[]{:S(2)}) async-start(bf16[8,128,512]{2,1,0:T(8,128)(2,1)} %pack.3), calls=%async_computation.2 | async-start | bytes 2097152 | tf_op jit(solution)/shard_map/all_to_all | solution.py:380
  69.6 16.7 %collective-permute-start.4 = (bf16[16,512]{1,0:T(8,128)(2,1)S(1)}, bf16[16,512]{1,0:T(8,128)(2,1)S(1)}, u32[]{:S(2)}, u32[]{:S(2)}) collective-permute-start(bf16[16,512]{1,0:T(8,128)(2,1)S(1)} %slice.8), channel_id=1, source_target_pairs={{32,0},{33,1},{34,2},{35,3},{36,4},{37,5},{38,6},{39,7},{40,8},{41... | collective-permute-start | bytes 49160 | tf_op jit(solution)/shard_map/ppermute | solution.py:385
  86.3 13.7 %copy-start.11 = (bf16[16,512]{1,0:T(8,128)(2,1)}, bf16[16,512]{1,0:T(8,128)(2,1)S(1)}, u32[]{:S(2)}) copy-start(bf16[16,512]{1,0:T(8,128)(2,1)S(1)} %collective-permute-done.4.x4_head) | copy-start | bytes 49156
  86.3 13.7 %copy-start.4 = (bf16[1024,512]{1,0:T(8,128)(2,1)}, bf16[1024,512]{1,0:T(8,128)(2,1)S(1)}, u32[]{:S(2)}) copy-start(bf16[1024,512]{1,0:T(8,128)(2,1)S(1)} %collective-permute-done.2.x2) | copy-start | bytes 3145732
  86.3 32.7 %collective-permute-start.5 = (bf16[1024,512]{1,0:T(8,128)(2,1)S(1)}, bf16[1024,512]{1,0:T(8,128)(2,1)S(1)}, u32[]{:S(2)}, u32[]{:S(2)}) collective-permute-start(bf16[1024,512]{1,0:T(8,128)(2,1)S(1)} %collective-permute-done.2.x2), channel_id=1, source_target_pairs={{8,0},{9,1},{10,2},{11,3},{12,4},{13,5},{14,6},{15,7},{16,8},{17,9... | collective-permute-start | bytes 3145736 | tf_op jit(solution)/shard_map/ppermute | solution.py:385
  90.8 9.2 %collective-permute-start.6 = (bf16[16,512]{1,0:T(8,128)(2,1)S(1)}, bf16[16,512]{1,0:T(8,128)(2,1)S(1)}, u32[]{:S(2)}, u32[]{:S(2)}) collective-permute-start(bf16[16,512]{1,0:T(8,128)(2,1)S(1)} %slice.9), channel_id=1, source_target_pairs={{0,16},{1,17},{2,18},{3,19},{4,20},{5,21},{6,22},{7,23},{8,24},{9,... | collective-permute-start | bytes 49160 | tf_op jit(solution)/shard_map/ppermute | solution.py:385
  100.0 0.6 copy-start.12
  119.0 1.9 copy-start.5
  119.0 44.8 %collective-permute-start.7 = (bf16[1024,512]{1,0:T(8,128)(2,1)S(1)}, bf16[1024,512]{1,0:T(8,128)(2,1)S(1)}, u32[]{:S(2)}, u32[]{:S(2)}) collective-permute-start(bf16[1024,512]{1,0:T(8,128)(2,1)S(1)} %collective-permute-done.5.x3), channel_id=1, source_target_pairs={{8,0},{9,1},{10,2},{11,3},{12,4},{13,5},{14,6},{15,7},{16,8},{17,9... | collective-permute-start | bytes 3145736 | tf_op jit(solution)/shard_map/ppermute | solution.py:385
  129.7 34.1 %all-to-all-start.3 = ((f32[16,8,512]{2,1,0:T(8,128)}), f32[16,8,512]{2,1,0:T(8,128)S(1)}, u32[]{:S(2)}, u32[]{:S(2)}) async-start(f32[16,8,512]{2,1,0:T(8,128)} %broadcast_in_dim.2), calls=%async_computation.3 | async-start | bytes 524288 | tf_op jit(solution)/shard_map/all_to_all | solution.py:418
  142.8 23.3 %collective-permute-start.8 = (bf16[16,512]{1,0:T(8,128)(2,1)}, bf16[16,512]{1,0:T(8,128)(2,1)S(1)}, u32[]{:S(2)}, u32[]{:S(2)}) collective-permute-start(bf16[16,512]{1,0:T(8,128)(2,1)} %get-tuple-element.32), channel_id=1, source_target_pairs={{8,0},{9,1},{10,2},{11,3},{12,4},{13,5},{14,6},{15,7},{16,8},{17,9... | collective-permute-start | bytes 49160 | tf_op jit(solution)/shard_map/ppermute | solution.py:385
  163.8 0.7 copy-start.7
  163.8 2.4 %copy-start.9 = (bf16[1024,512]{1,0:T(8,128)(2,1)}, bf16[1024,512]{1,0:T(8,128)(2,1)S(1)}, u32[]{:S(2)}) copy-start(bf16[1024,512]{1,0:T(8,128)(2,1)S(1)} %collective-permute-done.7.x4) | copy-start | bytes 3145732
  166.2 0.6 copy-start.10
  172.4 18.2 %all-to-all-start.4 = ((bf16[8,144,512]{2,1,0:T(8,128)(2,1)}), bf16[8,144,512]{2,1,0:T(8,128)(2,1)S(1)}, u32[]{:S(2)}, u32[]{:S(2)}) async-start(bf16[8,144,512]{2,1,0:T(8,128)(2,1)} %finish.1), calls=%async_computation.4 | async-start | bytes 2359296 | tf_op jit(solution)/shard_map/all_to_all | solution.py:380
  190.5 1.0 copy-start.2

commit v2 on v1

--- a/solution.py
+++ b/solution.py
@@ -74,11 +74,8 @@
     return high, mid, (rest - mid.astype(F32)).astype(BF16)
 
 
-def prepare_kernel(lane, half_ref, scale_ref, copies, out_ref):
-    total = copies[0]
-    for n in range(1, copies.shape[0]):
-        total = total + copies[n]
-    unscaled = total / scale_ref[0]
+def prepare_kernel(lane, half_ref, scale_ref, raw, out_ref):
+    unscaled = raw[...] / scale_ref[0]
     norm = jnp.sum(unscaled * unscaled, keepdims=True)
     norm = split_terms(jnp.broadcast_to(norm, (8, 8)))
     span = PLANE * lane
@@ -93,25 +90,25 @@
         out_ref[p] = jnp.concatenate([tile, jnp.zeros_like(tile)], axis=0).astype(BF16)
 
 
-def prepare(half, scale, copies, lane):
+def prepare(half, scale, raw, lane):
     return pl.pallas_call(
         functools.partial(prepare_kernel, lane),
         in_specs=[pl.BlockSpec(memory_space=pltpu.SMEM)] * 2 + [pl.BlockSpec(memory_space=pltpu.VMEM)],
         out_shape=jax.ShapeDtypeStruct((PLANE, HEAD, GW), BF16),
         compiler_params=params(False),
-        cost_estimate=cost(copies.size, 4 * copies.size),
+        cost_estimate=cost(raw.size, 4 * raw.size),
         name="prepare",
-    )(half.reshape(1), scale, copies)
-
-
-def unpack_kernel(lane, source_ref, got, out_ref, short_ref, norm_ref):
+    )(half.reshape(1), scale, raw)
+
+
+def unpack_kernel(lane, source_ref, got, extra, out_ref, short_ref, norm_ref):
     width = got.shape[2]
-    rows = out_ref.shape[1]
+    for p in range(PLANE):
+        out_ref[0, :, p * width : (p + 1) * width] = got[p]
     norm = jnp.zeros((8, 1), F32)
     short = jnp.zeros((8, lane), F32)
     for p in range(PLANE):
-        out_ref[0, :, p * width : (p + 1) * width] = got[p, :rows, :]
-        tile = got[p, rows:, :GW].astype(F32)[:8]
+        tile = extra[p].astype(F32)[:8]
         at = 3 * lane
         norm = norm + (tile[:, at : at + 1] + tile[:, at + 8 : at + 9] + tile[:, at + 16 : at + 17])
         terms = tile[:, :lane] + tile[:, lane : 2 * lane] + tile[:, 2 * lane : 3 * lane]
@@ -125,16 +122,26 @@
 def unpack(source, got, rows, width, lane):
     return pl.pallas_call(
         functools.partial(unpack_kernel, lane),
-        in_specs=[pl.BlockSpec(memory_space=pltpu.SMEM), pl.BlockSpec(memory_space=pltpu.VMEM)],
+        grid=(1,),
+        in_specs=[
+            pl.BlockSpec(memory_space=pltpu.SMEM),
+            pl.BlockSpec((PLANE, rows, got.shape[2]), lambda i: (0, 0, 0)),
+            pl.BlockSpec((PLANE, HEAD, GW), lambda i: (0, rows // HEAD, 0)),
+        ],
+        out_specs=[
+            pl.BlockSpec((1, rows, PLANE * got.shape[2]), lambda i: (0, 0, 0)),
+            pl.BlockSpec((width, lane), lambda i: (0, 0)),
+            pl.BlockSpec((1, 1), lambda i: (0, 0)),
+        ],
         out_shape=[
             jax.ShapeDtypeStruct((1, rows, PLANE * got.shape[2]), BF16),
             jax.ShapeDtypeStruct((width, lane), F32),
             jax.ShapeDtypeStruct((1, 1), F32),
         ],
-        compiler_params=params(False),
+        compiler_params=params(),
         cost_estimate=cost(0, 4 * got.size),
         name="unpack",
-    )(source.reshape(1), got)
+    )(source.reshape(1), got, got)
 
 
 def toeplitz_kernel(taps_ref, all_ref, far_ref):
@@ -200,10 +207,10 @@
             ref[rows, :] = value if add is None else add[rows, :] + value
 
 
-def correlate(conv_ref, feat_ref, before, feat_wide, terms):
+def correlate(conv_ref, feat, before, feat_wide, terms):
     rows = conv_ref.shape[0]
     feat_wide[:8, :] = before[before.shape[0] - 8 :, :].astype(F32)
-    feat_wide[8:, :] = feat_ref[...].astype(F32)
+    feat_wide[8:, :] = feat.astype(F32)
     for r in range(0, rows, 128):
         conv = conv_ref[r : r + 128, :]
         for j in range(len(terms)):
@@ -219,35 +226,6 @@
     raw_ref[...] = out if add is None else add[...] + out
 
 
-def put_terms(raw_ref, terms, add=None):
-    out = [jnp.sum(t, axis=0, keepdims=True) for t in terms]
-    out.append(jnp.zeros((8 - len(terms), GW), F32))
-    out = jnp.concatenate(out, axis=0)
-    raw_ref[...] = out if add is None else add[...] + out
-
-
-def by_group(kernel, name, flops, args, outs, scratch):
-    groups = outs[0].shape[1] // GW
-
-    def spec(x):
-        if len(x.shape) == 3:
-            return pl.BlockSpec((1,) + x.shape[1:], lambda g: (g, 0, 0))
-        return pl.BlockSpec((x.shape[0], GW), lambda g: (0, g))
-
-    moved = sum(x.size * x.dtype.itemsize for x in (*args, *outs))
-    return pl.pallas_call(
-        kernel,
-        grid=(groups,),
-        in_specs=[spec(x) for x in args],
-        out_specs=[spec(x) for x in outs],
-        out_shape=outs,
-        scratch_shapes=scratch,
-        compiler_params=params(),
-        cost_estimate=cost(flops * groups, moved),
-        name=name,
-    )(*args)
-
-
 def pairs_of(rows):
     return pltpu.VMEM((rows + BLK, 2 * GW), BF16)
 
@@ -262,44 +240,66 @@
 
 def early(x0, x1, tiles):
     rows, own = x0.shape
+    groups = own // GW
+    col = pl.BlockSpec((rows, GW), lambda g: (0, g))
     out = jax.ShapeDtypeStruct((rows, own), F32)
-    return by_group(
-        early_kernel, "early", 24 * rows * rows * GW, [x0, x1, tiles], [out, out], [pairs_of(2 * rows)]
-    )
-
-
-def own_terms_kernel(width, acc, f0, f1, raw_ref, feat_wide):
-    terms = [jnp.zeros((8, GW), F32)] * width
-    before = f1[f1.shape[0] - HEAD :, :]
-    put_terms(raw_ref, correlate(acc, f0, before, feat_wide, terms))
-
-
-def own_terms(width, acc, f0, f1):
-    rows, own = acc.shape
-    out = jax.ShapeDtypeStruct((8, own), F32)
-    scratch = [pltpu.VMEM((rows + 8, GW), F32)]
-    kernel = functools.partial(own_terms_kernel, width)
-    return by_group(kernel, "own_terms", 14 * rows * GW, [acc, f0, f1], [out], scratch)[0]
-
-
-def far_terms_kernel(width, mid, raw, x2, f1, f2, f3_tail, tiles, raw_ref, pairs, far, feat_wide):
+    return pl.pallas_call(
+        early_kernel,
+        grid=(groups,),
+        in_specs=[col, col, pl.BlockSpec((1, BLK, 12 * BLK), lambda g: (g, 0, 0))],
+        out_specs=[col, col],
+        out_shape=[out, out],
+        scratch_shapes=[pairs_of(2 * rows)],
+        compiler_params=params(),
+        cost_estimate=cost(24 * rows * rows * GW * groups, 12 * rows * own),
+        name="early",
+    )(x0, x1, tiles)
+
+
+def terms_kernel(
+    width, acc, mid, x2, f0, f1, f2, f3_tail, tiles, raw_ref, pairs, far, feat_wide
+):
+    rows = x2.shape[0]
     fill_pairs(pairs, [x2])
     terms = [jnp.zeros((8, GW), F32)] * width
-    before = f2[f2.shape[0] - HEAD :, :]
+    terms = correlate(acc, f0[...], f1[rows - HEAD :, :], feat_wide, terms)
     store_rows(far, tile_products(tiles, 9, 16, pairs, 12, 4), add=mid)
-    terms = correlate(far, f1, before, feat_wide, terms)
+    terms = correlate(far, f1[...], f2[rows - HEAD :, :], feat_wide, terms)
     store_rows(far, tile_products(tiles, 9, 16, pairs, 16, 4))
-    terms = correlate(far, f2, f3_tail[...], feat_wide, terms)
-    put_terms(raw_ref, terms, add=raw)
-
-
-def far_terms(width, mid, raw, x2, f1, f2, f3_tail, tiles):
-    rows, own = mid.shape
-    out = jax.ShapeDtypeStruct((8, own), F32)
-    scratch = [pairs_of(rows), pltpu.VMEM((rows, GW), F32), pltpu.VMEM((rows + 8, GW), F32)]
-    kernel = functools.partial(far_terms_kernel, width)
-    args = [mid, raw, x2, f1, f2, f3_tail, tiles]
-    return by_group(kernel, "far_terms", 16 * rows * rows * GW, args, [out], scratch)[0]
+    terms = correlate(far, f2[...], f3_tail[...], feat_wide, terms)
+    out = [jnp.sum(t, axis=0, keepdims=True) for t in terms]
+    out.append(jnp.zeros((8 - width, GW), F32))
+    raw_ref[...] = jnp.concatenate(out, axis=0)
+
+
+def all_terms(width, acc, mid, x2, f0, f1, f2, f3_tail, tiles):
+    rows, own = acc.shape
+    groups = own // GW
+    col = pl.BlockSpec((rows, GW), lambda g: (0, g))
+    return pl.pallas_call(
+        functools.partial(terms_kernel, width),
+        grid=(groups,),
+        in_specs=[
+            col,
+            col,
+            col,
+            col,
+            col,
+            col,
+            pl.BlockSpec((HEAD, GW), lambda g: (0, g)),
+            pl.BlockSpec((1,) + tiles.shape[1:], lambda g: (g, 0, 0)),
+        ],
+        out_specs=pl.BlockSpec((8, GW), lambda g: (0, g)),
+        out_shape=jax.ShapeDtypeStruct((8, own), F32),
+        scratch_shapes=[
+            pairs_of(rows),
+            pltpu.VMEM((rows, GW), F32),
+            pltpu.VMEM((rows + 8, GW), F32),
+        ],
+        compiler_params=params(),
+        cost_estimate=cost(16 * rows * rows * GW * groups, 20 * rows * own),
+        name="all_terms",
+    )(acc, mid, x2, f0, f1, f2, f3_tail, tiles)
 
 
 def third_kernel(acc_in, x2, x3, x4_head, tiles, acc_ref, head_ref, pairs):
@@ -313,9 +313,28 @@
 
 def third(acc, x2, x3, x4_head, tiles):
     rows, own = acc.shape
-    outs = [jax.ShapeDtypeStruct((rows, own), F32), jax.ShapeDtypeStruct((HEAD, own), BF16)]
-    args = [acc, x2, x3, x4_head, tiles]
-    return by_group(third_kernel, "third", 18 * rows * rows * GW, args, outs, [pairs_of(2 * rows)])
+    groups = own // GW
+    col = pl.BlockSpec((rows, GW), lambda g: (0, g))
+    return pl.pallas_call(
+        third_kernel,
+        grid=(groups,),
+        in_specs=[
+            col,
+            col,
+            col,
+            pl.BlockSpec((HEAD, GW), lambda g: (0, g)),
+            pl.BlockSpec((1,) + tiles.shape[1:], lambda g: (g, 0, 0)),
+        ],
+        out_specs=[col, pl.BlockSpec((HEAD, GW), lambda g: (0, g))],
+        out_shape=[
+            jax.ShapeDtypeStruct((rows, own), F32),
+            jax.ShapeDtypeStruct((HEAD, own), BF16),
+        ],
+        scratch_shapes=[pairs_of(2 * rows)],
+        compiler_params=params(),
+        cost_estimate=cost(18 * rows * rows * GW * groups, 12 * rows * own),
+        name="third",
+    )(acc, x2, x3, x4_head, tiles)
 
 
 def last_kernel(width, acc_in, x4, tiles, next_head, taps, extra, out_ref, pairs, wide):
@@ -374,7 +393,6 @@
     groups = own // GW
     rows = PLANE * features.shape[1]
     in_plane = [[k * PLANE + i for i in range(PLANE)] for k in range(planes)]
-    along_z = [[k * PLANE + i for k in range(planes)] for i in range(PLANE)]
 
     def swap(x):
         return lax.all_to_all(x, "ctx", 0, 0, axis_index_groups=in_plane, tiled=True)
@@ -387,38 +405,36 @@
     def after(x, *others):
         return lax.optimization_barrier((x,) + others)[0]
 
+    feat1 = hop(features, 1)
     packed = gate(upstream, gate_values)
-    feat1 = hop(features, 1)
-    x0 = swap(packed)
+    x0 = swap(packed).reshape(rows, own)
     filters = lax.dynamic_slice_in_dim(after(long_filter, packed), p * groups, groups, 0)
     taps = lax.dynamic_slice_in_dim(after(short_filter, packed), p * own, own, 1)
     tiles, far_tiles = toeplitz(filters)
-    x0 = x0.reshape(rows, own)
-    feat1 = swap(pack(after(feat1, x0)))
-    x1 = after(hop(x0, -1), feat1, tiles)
-    feat0 = swap(pack(after(features, feat1)))
-    feat0, feat1 = (x.reshape(rows, own) for x in (feat0, feat1))
-
+    feat1 = swap(pack(after(feat1, x0))).reshape(rows, own)
+    feat0 = pack(after(features, x0))
+    x1 = after(hop(x0, -1), feat0, feat1, tiles)
+    feat0 = swap(after(feat0, feat1)).reshape(rows, own)
     feat2 = hop(feat1, 1)
     feat3_tail = hop(feat1[rows - HEAD :], 2)
     x4_head = hop(x0[:HEAD], -4)
 
     acc, mid = early(x0, x1, tiles)
-    x2 = after(hop(x1, -1), acc, feat0, feat2, x4_head)
-    raw = own_terms(width, acc, feat0, feat1)
-    raw = far_terms(width, mid, raw, x2, feat1, feat2, feat3_tail, far_tiles)
-    raw = lax.psum(raw, "dp")
-    x3 = after(hop(x2, -1), raw)
+    x2 = after(hop(x1, -1), acc, feat0, feat2, feat3_tail, x4_head)
+    raw = all_terms(width, acc, mid, x2, feat0, feat1, feat2, feat3_tail, far_tiles)
+    along_z = [[k * PLANE + i for k in range(planes)] for i in range(PLANE)]
+    copies = jnp.broadcast_to(raw.astype(BF16)[None], (planes,) + raw.shape)
+    copies = lax.all_to_all(copies, "ctx", 0, 0, axis_index_groups=along_z, tiled=True)
+    x3 = after(hop(x2, -1), copies)
     x4 = hop(x3, -1)
+    raw = jnp.sum(after(copies, x3).astype(F32), axis=0)
     acc, head = third(acc, x2, x3, x4_head, tiles)
     next_head = hop(head, -1)
-
-    raw = after(raw, x3, head)
-    copies = jnp.broadcast_to(raw[None], (planes,) + raw.shape)
-    copies = lax.all_to_all(copies, "ctx", 0, 0, axis_index_groups=along_z, tiled=True)
+    copies = jnp.broadcast_to(raw[None], (lax.axis_size("dp"),) + raw.shape)
+    raw = jnp.sum(lax.all_to_all(copies, "dp", 0, 0, tiled=True), axis=0)
     lane = chans // shards
     spans = own // lane // PLANE
-    extra = prepare(z % spans, loss_scale, after(copies, x4), lane)
+    extra = prepare(z % spans, loss_scale, raw, lane)
     got = swap(finish(width, acc, x4, far_tiles, next_head, taps, extra))
     input_grad, short_grad, norm_value = unpack(z // spans, got, rows // PLANE, width, lane)
     return (input_grad, short_grad, norm_value.reshape(1))

time: 195 us -> 181 us (0.928)
  the two profiles are of different devices: /device:TPU:34 before, /device:TPU:32 now
where the time goes in v2:
time: 181 us; the launch traced here: 180 us
  blocking collectives  49.1 us (27%)
  Pallas kernels  47.9 us (26%)
  starting transfers between devices  46.6 us (26%)
  waiting for transfers between devices  26.5 us (15%)
  local copies, waits for them, and re-layouts  5.97 us (3%)
  other arithmetic  2.22 us (1%)
    ppermute x9, starting transfers between devices, hop(): return lax.ppermute(x, 'ctx', route)  30.3 us
    all_to_all x1, blocking collectives, per_device(): lax.all_to_all(copies, 'ctx', 0, 0, axis_index_groups=along_z, tiled=True)  25.3 us
    all_to_all x1, blocking collectives, swap(): lax.all_to_all(x, 'ctx', 0, 0, axis_index_groups=in_plane, tiled=True)  23.8 us
    all_to_all x3, waiting for transfers between devices, swap(): lax.all_to_all(x, 'ctx', 0, 0, axis_index_groups=in_plane, tiled=True)  20.7 us
    all_to_all x3, starting transfers between devices, swap(): lax.all_to_all(x, 'ctx', 0, 0, axis_index_groups=in_plane, tiled=True)  13 us
    pallas_call x1, Pallas kernels, all_terms(): pl.pallas_call(functools.partial(terms_kernel, width), grid=(groups,), in...  9.38 us
    pallas_call x1, Pallas kernels, third(): pl.pallas_call(third_kernel, grid=(groups,), in_specs=[col, col, col, pl....  8.04 us
    pallas_call x1, Pallas kernels, early(): pl.pallas_call(early_kernel, grid=(groups,), in_specs=[col, col, pl.Block...  7.83 us
  transfers between devices with their start and end apart: 13, of which 5 were waited for; matrix products, arithmetic and copies ran while one was open for 2% of the time, Pallas kernels for 22%

profile of v2, /device:TPU:32, one launch (start us, length us, event | category | flops | bytes accessed | tf_op | source)
XLA Modules:
  0.0 179.8 jit_solution(6439129472388457348)
XLA Ops:
  0.6 4.0 %collective-permute-start.1 = (bf16[1,128,4096]{2,1,0:T(8,128)(2,1)}, bf16[1,128,4096]{2,1,0:T(8,128)(2,1)S(1)}, u32[]{:S(2)}, u32[]{:S(2)}) collective-permute-start(bf16[1,128,4096]{2,1,0:T(8,128)(2,1)} %src_ref), channel_id=1, source_target_pairs={{0,8},{1,9},{2,10},{3,11},{4,12},{5,13},{6,14},{7,15},{8,16},{9,17... | collective-permute-start | bytes 3145736 | tf_op jit(solution)/shard_map/ppermute | solution.py:403
  4.6 2.8 %gate.1 = bf16[8,128,512]{2,1,0:T(8,128)(2,1)} custom-call(bf16[1,128,4096]{2,1,0:T(8,128)(2,1)} %up_ref.1, bf16[1,128,4096]{2,1,0:T(8,128)(2,1)} %gate_ref.1), custom_call_target="tpu_custom_call" | custom-call | flops 8192 | bytes 49152 | tf_op jit(solution)/shard_map/gate/pallas_call | solution.py:44
  7.4 23.8 %all_to_all.30 = bf16[8,128,512]{2,1,0:T(8,128)(2,1)S(1)} all-to-all(bf16[8,128,512]{2,1,0:T(8,128)(2,1)} %gate.1), channel_id=1, replica_groups={{0,1,2,3,4,5,6,7},{8,9,10,11,12,13,14,15},{16,17,18,19,20,21,22,23},{24..., dimensions={0} | all-to-all | bytes 2097152 | tf_op jit(solution)/shard_map/all_to_all | solution.py:398
  31.2 2.1 %collective-permute-start = (bf16[1024,512]{1,0:T(8,128)(2,1)S(1)}, bf16[1024,512]{1,0:T(8,128)(2,1)S(1)}, u32[]{:S(2)}, u32[]{:S(2)}) collective-permute-start(bf16[1024,512]{1,0:T(8,128)(2,1)S(1)} %bitcast.9), channel_id=1, source_target_pairs={{8,0},{9,1},{10,2},{11,3},{12,4},{13,5},{14,6},{15,7},{16,8},{17,9... | collective-permute-start | bytes 3145736 | tf_op jit(solution)/shard_map/ppermute | solution.py:403
  33.3 1.0 copy-done.6
  34.3 2.3 %pack.3 = bf16[8,128,512]{2,1,0:T(8,128)(2,1)} custom-call(bf16[1,128,4096]{2,1,0:T(8,128)(2,1)} %copy-done.6), custom_call_target="tpu_custom_call" | custom-call | bytes 32768 | tf_op jit(solution)/shard_map/pack/pallas_call | solution.py:61
  36.5 3.6 %all-to-all-start.1 = ((bf16[8,128,512]{2,1,0:T(8,128)(2,1)}), bf16[8,128,512]{2,1,0:T(8,128)(2,1)S(1)}, u32[]{:S(2)}, u32[]{:S(2)}) async-start(bf16[8,128,512]{2,1,0:T(8,128)(2,1)} %pack.3), calls=%async_computation.1 | async-start | bytes 2097152 | tf_op jit(solution)/shard_map/all_to_all | solution.py:398
  41.6 6.0 %toeplitz.1 = (bf16[4,256,4352]{2,1,0:T(8,128)(2,1)}, bf16[4,256,2048]{2,1,0:T(8,128)(2,1)}) custom-call(f32[4,1,4096]{2,1,0:T(1,128)} %reshape.40.taps_ref), custom_call_target="tpu_custom_call" | custom-call | flops 1048576 | bytes 393216 | tf_op jit(solution)/shard_map/toeplitz/pallas_call | solution.py:161
  47.6 2.3 %pack.2 = bf16[8,128,512]{2,1,0:T(8,128)(2,1)} custom-call(bf16[1,128,4096]{2,1,0:T(8,128)(2,1)} %src_ref), custom_call_target="tpu_custom_call" | custom-call | bytes 32768 | tf_op jit(solution)/shard_map/pack/pallas_call | solution.py:61
  49.9 4.2 %all-to-all-done.1 = bf16[8,128,512]{2,1,0:T(8,128)(2,1)S(1)} async-done(((bf16[8,128,512]{2,1,0:T(8,128)(2,1)}), bf16[8,128,512]{2,1,0:T(8,128)(2,1)S(1)}, u32[]{:S(2)}, u32[]{:S(2)}) %all-to-all-start.1) | async-done | bytes 1048608 | tf_op jit(solution)/shard_map/all_to_all | solution.py:398
  54.1 1.9 %collective-permute-done.x1 = bf16[1024,512]{1,0:T(8,128)(2,1)S(1)} collective-permute-done((bf16[1024,512]{1,0:T(8,128)(2,1)S(1)}, bf16[1024,512]{1,0:T(8,128)(2,1)S(1)}, u32[]{:S(2)}, u32[]{:S(2)}) %collective-permute-start) | collective-permute-done | bytes 1048608 | tf_op jit(solution)/shard_map/ppermute | solution.py:403
  57.0 2.0 %collective-permute-start.2 = (bf16[1024,512]{1,0:T(8,128)(2,1)}, bf16[1024,512]{1,0:T(8,128)(2,1)S(1)}, u32[]{:S(2)}, u32[]{:S(2)}) collective-permute-start(bf16[1024,512]{1,0:T(8,128)(2,1)} %copy-done.7), channel_id=1, source_target_pairs={{8,0},{9,1},{10,2},{11,3},{12,4},{13,5},{14,6},{15,7},{16,8},{17,9... | collective-permute-start | bytes 3145736 | tf_op jit(solution)/shard_map/ppermute | solution.py:403
  59.0 4.9 %collective-permute-start.3 = (bf16[1024,512]{1,0:T(8,128)(2,1)S(1)}, bf16[1024,512]{1,0:T(8,128)(2,1)}, u32[]{:S(2)}, u32[]{:S(2)}) collective-permute-start(bf16[1024,512]{1,0:T(8,128)(2,1)S(1)} %bitcast.6), channel_id=1, source_target_pairs={{0,8},{1,9},{2,10},{3,11},{4,12},{5,13},{6,14},{7,15},{8,16},{9,17... | collective-permute-start | bytes 3145736 | tf_op jit(solution)/shard_map/ppermute | solution.py:403
  64.0 4.3 %all-to-all-start.2 = ((bf16[8,128,512]{2,1,0:T(8,128)(2,1)}), bf16[8,128,512]{2,1,0:T(8,128)(2,1)}, u32[]{:S(2)}, u32[]{:S(2)}) async-start(bf16[8,128,512]{2,1,0:T(8,128)(2,1)} %pack.2), calls=%async_computation.2 | async-start | bytes 2097152 | tf_op jit(solution)/shard_map/all_to_all | solution.py:398
  68.2 1.3 collective-permute-start.5
  69.5 7.5 %collective-permute-start.4 = (bf16[16,512]{1,0:T(8,128)(2,1)S(1)}, bf16[16,512]{1,0:T(8,128)(2,1)S(1)}, u32[]{:S(2)}, u32[]{:S(2)}) collective-permute-start(bf16[16,512]{1,0:T(8,128)(2,1)S(1)} %slice.8), channel_id=1, source_target_pairs={{0,16},{1,17},{2,18},{3,19},{4,20},{5,21},{6,22},{7,23},{8,24},{9,... | collective-permute-start | bytes 49160 | tf_op jit(solution)/shard_map/ppermute | solution.py:403
  77.1 7.8 %early.1 = (f32[1024,512]{1,0:T(8,128)}, f32[1024,512]{1,0:T(8,128)}) custom-call(bf16[1024,512]{1,0:T(8,128)(2,1)} %bitcast.11, bf16[1024,512]{1,0:T(8,128)(2,1)} %copy-done.7, bf16[4,256,4352]{2,1,0:T(8,128)(2,1)} %get-tuple-element.24.tiles), custom_call_target="tpu_custom_call" | custom-call | flops 201326592 | bytes 98304 | tf_op jit(solution)/shard_map/early/pallas_call | solution.py:246
  84.9 2.3 %collective-permute-done.5.x4_head = bf16[16,512]{1,0:T(8,128)(2,1)S(1)} collective-permute-done((bf16[16,512]{1,0:T(8,128)(2,1)S(1)}, bf16[16,512]{1,0:T(8,128)(2,1)S(1)}, u32[]{:S(2)}, u32[]{:S(2)}) %collective-permute-start.5) | collective-permute-done | bytes 16416 | tf_op jit(solution)/shard_map/ppermute | solution.py:403
  87.2 4.4 %collective-permute-start.6 = (bf16[1024,512]{1,0:T(8,128)(2,1)S(1)}, bf16[1024,512]{1,0:T(8,128)(2,1)S(1)}, u32[]{:S(2)}, u32[]{:S(2)}) collective-permute-start(bf16[1024,512]{1,0:T(8,128)(2,1)S(1)} %collective-permute-done.2.x2), channel_id=1, source_target_pairs={{8,0},{9,1},{10,2},{11,3},{12,4},{13,5},{14,6},{15,7},{16,8},{17,9... | collective-permute-start | bytes 3145736 | tf_op jit(solution)/shard_map/ppermute | solution.py:403
  91.7 9.4 %all_terms.1 = f32[8,512]{1,0:T(8,128)} custom-call(f32[1024,512]{1,0:T(8,128)} %get-tuple-element.26.acc.acc_in, f32[1024,512]{1,0:T(8,128)} %get-tuple-element.29.mid, bf16[1024,512]{1,0:T(8,128)(2,1)} %copy-done.4, bf16[1024,512]{1,0:T(8,128)(2,1)} %bitcast.3.f0, bf16[1024,512]{1,0:T(8,128)(2,1)} %bitcast.8, bf16[1024,512]{1,0:T(8,128)(2,1)} %collective-permute-done.3.f2, ...), custom_call_target="tpu_custom_call" | custom-call | flops 134217728 | bytes 163840 | tf_op jit(solution)/shard_map/all_terms/pallas_call | solution.py:279
  101.8 25.3 %all_to_all.31 = bf16[16,8,512]{2,1,0:T(8,128)(2,1)S(1)} all-to-all(bf16[16,8,512]{2,1,0:T(8,128)(2,1)S(1)} %broadcast_in_dim.4), channel_id=1, replica_groups={{0,8,16,24,32,40,48,56,64,72,80,88,96,104,112,120},{1,9,17,25,33,41,49,..., dimensions={0} | all-to-all | bytes 262144 | tf_op jit(solution)/shard_map/all_to_all | solution.py:427
  127.1 2.2 %collective-permute-start.7 = (bf16[1024,512]{1,0:T(8,128)(2,1)S(1)}, bf16[1024,512]{1,0:T(8,128)(2,1)S(1)}, u32[]{:S(2)}, u32[]{:S(2)}) collective-permute-start(bf16[1024,512]{1,0:T(8,128)(2,1)S(1)} %collective-permute-done.6.x3), channel_id=1, source_target_pairs={{8,0},{9,1},{10,2},{11,3},{12,4},{13,5},{14,6},{15,7},{16,8},{17,9... | collective-permute-start | bytes 3145736 | tf_op jit(solution)/shard_map/ppermute | solution.py:403
  130.0 3.3 %all-to-all-start.4 = ((f32[4,8,512]{2,1,0:T(8,128)}), f32[4,8,512]{2,1,0:T(8,128)S(1)}, u32[]{:S(2)}, u32[]{:S(2)}) async-start(f32[4,8,512]{2,1,0:T(8,128)} %broadcast_in_dim.5), calls=%async_computation.4 | async-start | bytes 131072 | tf_op jit(solution)/shard_map/all_to_all | solution.py:434
  133.3 8.0 %third.1 = (f32[1024,512]{1,0:T(8,128)}, bf16[16,512]{1,0:T(8,128)(2,1)}) custom-call(f32[1024,512]{1,0:T(8,128)} %get-tuple-element.26.acc.acc_in, bf16[1024,512]{1,0:T(8,128)(2,1)} %copy-done.4, bf16[1024,512]{1,0:T(8,128)(2,1)} %copy-done.5, bf16[16,512]{1,0:T(8,128)(2,1)} %copy-done.9, bf16[4,256,4352]{2,1,0:T(8,128)(2,1)} %get-tuple-element.24.tiles), custom_call_target="tpu_custom_call" | custom-call | flops 150994944 | bytes 98304 | tf_op jit(solution)/shard_map/third/pallas_call | solution.py:318
  141.4 1.9 %collective-permute-start.8 = (bf16[16,512]{1,0:T(8,128)(2,1)}, bf16[16,512]{1,0:T(8,128)(2,1)S(1)}, u32[]{:S(2)}, u32[]{:S(2)}) collective-permute-start(bf16[16,512]{1,0:T(8,128)(2,1)} %get-tuple-element.33), channel_id=1, source_target_pairs={{8,0},{9,1},{10,2},{11,3},{12,4},{13,5},{14,6},{15,7},{16,8},{17,9... | collective-permute-start | bytes 49160 | tf_op jit(solution)/shard_map/ppermute | solution.py:403
  145.2 1.5 prepare.1.extra
  146.6 1.6 collective-permute-done.8.next_head
  149.2 5.6 %finish.1 = bf16[8,144,512]{2,1,0:T(8,128)(2,1)} custom-call(f32[1024,512]{1,0:T(8,128)} %get-tuple-element.32.acc_in, bf16[1024,512]{1,0:T(8,128)(2,1)} %copy-done.8, bf16[4,256,2048]{2,1,0:T(8,128)(2,1)} %get-tuple-element.30.tiles, bf16[16,512]{1,0:T(8,128)(2,1)} %copy-done.10, f32[7,512]{1,0:T(8,128)} %constant_dynamic-slice_fusion.taps, ...), custom_call_target="tpu_custom_call" | custom-call | flops 50331648 | bytes 65536 | tf_op jit(solution)/shard_map/finish/pallas_call | solution.py:363
  154.8 5.2 %all-to-all-start.5 = ((bf16[8,144,512]{2,1,0:T(8,128)(2,1)}), bf16[8,144,512]{2,1,0:T(8,128)(2,1)S(1)}, u32[]{:S(2)}, u32[]{:S(2)}) async-start(bf16[8,144,512]{2,1,0:T(8,128)(2,1)} %finish.1), calls=%async_computation.5 | async-start | bytes 2359296 | tf_op jit(solution)/shard_map/all_to_all | solution.py:398
  160.0 16.5 %all-to-all-done.5.got.extra = bf16[8,144,512]{2,1,0:T(8,128)(2,1)S(1)} async-done(((bf16[8,144,512]{2,1,0:T(8,128)(2,1)}), bf16[8,144,512]{2,1,0:T(8,128)(2,1)S(1)}, u32[]{:S(2)}, u32[]{:S(2)}) %all-to-all-start.5) | async-done | bytes 1179680 | tf_op jit(solution)/shard_map/all_to_all | solution.py:398
  176.4 1.0 copy-done.1
  177.5 2.3 %unpack.1 = (bf16[1,128,4096]{2,1,0:T(8,128)(2,1)}, f32[7,32]{1,0:T(8,128)}, f32[1,1]{1,0:T(1,128)}) custom-call(s32[1]{0:T(128)} %bitcast.source_ref, bf16[8,144,512]{2,1,0:T(8,128)(2,1)} %copy-done.1, bf16[8,144,512]{2,1,0:T(8,128)(2,1)} %copy-done.1), custom_call_target="tpu_custom_call" | custom-call | bytes 36864 | tf_op jit(solution)/shard_map/unpack/pallas_call | solution.py:123
  (40 shorter events, 6.2 us)
Async XLA Ops:
  0.6 142.7 %copy-start = (f32[7,4096]{1,0:T(8,128)S(1)}, f32[7,4096]{1,0:T(8,128)}, u32[]{:S(2)}) copy-start(f32[7,4096]{1,0:T(8,128)} %param.9) | copy-start | bytes 344068
  0.6 32.6 %collective-permute-start.1 = (bf16[1,128,4096]{2,1,0:T(8,128)(2,1)}, bf16[1,128,4096]{2,1,0:T(8,128)(2,1)S(1)}, u32[]{:S(2)}, u32[]{:S(2)}) collective-permute-start(bf16[1,128,4096]{2,1,0:T(8,128)(2,1)} %src_ref), channel_id=1, source_target_pairs={{0,8},{1,9},{2,10},{3,11},{4,12},{5,13},{6,14},{7,15},{8,16},{9,17... | collective-permute-start | bytes 3145736 | tf_op jit(solution)/shard_map/ppermute | solution.py:403
  31.2 37.1 %copy-start.3 = (bf16[8,128,512]{2,1,0:T(8,128)(2,1)}, bf16[8,128,512]{2,1,0:T(8,128)(2,1)S(1)}, u32[]{:S(2)}) copy-start(bf16[8,128,512]{2,1,0:T(8,128)(2,1)S(1)} %all_to_all.30) | copy-start | bytes 3145732
  31.2 24.8 %collective-permute-start = (bf16[1024,512]{1,0:T(8,128)(2,1)S(1)}, bf16[1024,512]{1,0:T(8,128)(2,1)S(1)}, u32[]{:S(2)}, u32[]{:S(2)}) collective-permute-start(bf16[1024,512]{1,0:T(8,128)(2,1)S(1)} %bitcast.9), channel_id=1, source_target_pairs={{8,0},{9,1},{10,2},{11,3},{12,4},{13,5},{14,6},{15,7},{16,8},{17,9... | collective-permute-start | bytes 3145736 | tf_op jit(solution)/shard_map/ppermute | solution.py:403
  33.2 1.0 copy-start.6
  36.5 17.6 %all-to-all-start.1 = ((bf16[8,128,512]{2,1,0:T(8,128)(2,1)}), bf16[8,128,512]{2,1,0:T(8,128)(2,1)S(1)}, u32[]{:S(2)}, u32[]{:S(2)}) async-start(bf16[8,128,512]{2,1,0:T(8,128)(2,1)} %pack.3), calls=%async_computation.1 | async-start | bytes 2097152 | tf_op jit(solution)/shard_map/all_to_all | solution.py:398
  54.1 30.8 %copy-start.2 = (bf16[8,128,512]{2,1,0:T(8,128)(2,1)}, bf16[8,128,512]{2,1,0:T(8,128)(2,1)S(1)}, u32[]{:S(2)}) copy-start(bf16[8,128,512]{2,1,0:T(8,128)(2,1)S(1)} %all-to-all-done.1) | copy-start | bytes 3145732
  56.0 1.0 copy-start.7
  57.0 30.2 %collective-permute-start.2 = (bf16[1024,512]{1,0:T(8,128)(2,1)}, bf16[1024,512]{1,0:T(8,128)(2,1)S(1)}, u32[]{:S(2)}, u32[]{:S(2)}) collective-permute-start(bf16[1024,512]{1,0:T(8,128)(2,1)} %copy-done.7), channel_id=1, source_target_pairs={{8,0},{9,1},{10,2},{11,3},{12,4},{13,5},{14,6},{15,7},{16,8},{17,9... | collective-permute-start | bytes 3145736 | tf_op jit(solution)/shard_map/ppermute | solution.py:403
  59.0 28.2 %collective-permute-start.3 = (bf16[1024,512]{1,0:T(8,128)(2,1)S(1)}, bf16[1024,512]{1,0:T(8,128)(2,1)}, u32[]{:S(2)}, u32[]{:S(2)}) collective-permute-start(bf16[1024,512]{1,0:T(8,128)(2,1)S(1)} %bitcast.6), channel_id=1, source_target_pairs={{0,8},{1,9},{2,10},{3,11},{4,12},{5,13},{6,14},{7,15},{8,16},{9,17... | collective-permute-start | bytes 3145736 | tf_op jit(solution)/shard_map/ppermute | solution.py:403
  64.0 23.3 %all-to-all-start.2 = ((bf16[8,128,512]{2,1,0:T(8,128)(2,1)}), bf16[8,128,512]{2,1,0:T(8,128)(2,1)}, u32[]{:S(2)}, u32[]{:S(2)}) async-start(bf16[8,128,512]{2,1,0:T(8,128)(2,1)} %pack.2), calls=%async_computation.2 | async-start | bytes 2097152 | tf_op jit(solution)/shard_map/all_to_all | solution.py:398
  68.2 19.0 %collective-permute-start.5 = (bf16[16,512]{1,0:T(8,128)(2,1)S(1)}, bf16[16,512]{1,0:T(8,128)(2,1)S(1)}, u32[]{:S(2)}, u32[]{:S(2)}) collective-permute-start(bf16[16,512]{1,0:T(8,128)(2,1)S(1)} %slice.9), channel_id=1, source_target_pairs={{32,0},{33,1},{34,2},{35,3},{36,4},{37,5},{38,6},{39,7},{40,8},{41... | collective-permute-start | bytes 49160 | tf_op jit(solution)/shard_map/ppermute | solution.py:403
  69.5 17.7 %collective-permute-start.4 = (bf16[16,512]{1,0:T(8,128)(2,1)S(1)}, bf16[16,512]{1,0:T(8,128)(2,1)S(1)}, u32[]{:S(2)}, u32[]{:S(2)}) collective-permute-start(bf16[16,512]{1,0:T(8,128)(2,1)S(1)} %slice.8), channel_id=1, source_target_pairs={{0,16},{1,17},{2,18},{3,19},{4,20},{5,21},{6,22},{7,23},{8,24},{9,... | collective-permute-start | bytes 49160 | tf_op jit(solution)/shard_map/ppermute | solution.py:403
  87.2 13.9 %copy-start.9 = (bf16[16,512]{1,0:T(8,128)(2,1)}, bf16[16,512]{1,0:T(8,128)(2,1)S(1)}, u32[]{:S(2)}) copy-start(bf16[16,512]{1,0:T(8,128)(2,1)S(1)} %collective-permute-done.5.x4_head) | copy-start | bytes 49156
  87.2 4.5 %copy-start.11 = (bf16[16,512]{1,0:T(8,128)(2,1)}, bf16[16,512]{1,0:T(8,128)(2,1)S(1)}, u32[]{:S(2)}) copy-start(bf16[16,512]{1,0:T(8,128)(2,1)S(1)} %collective-permute-done.4.f3_tail) | copy-start | bytes 49156
  87.2 4.5 %copy-start.4 = (bf16[1024,512]{1,0:T(8,128)(2,1)}, bf16[1024,512]{1,0:T(8,128)(2,1)S(1)}, u32[]{:S(2)}) copy-start(bf16[1024,512]{1,0:T(8,128)(2,1)S(1)} %collective-permute-done.2.x2) | copy-start | bytes 3145732
  87.2 39.9 %collective-permute-start.6 = (bf16[1024,512]{1,0:T(8,128)(2,1)S(1)}, bf16[1024,512]{1,0:T(8,128)(2,1)S(1)}, u32[]{:S(2)}, u32[]{:S(2)}) collective-permute-start(bf16[1024,512]{1,0:T(8,128)(2,1)S(1)} %collective-permute-done.2.x2), channel_id=1, source_target_pairs={{8,0},{9,1},{10,2},{11,3},{12,4},{13,5},{14,6},{15,7},{16,8},{17,9... | collective-permute-start | bytes 3145736 | tf_op jit(solution)/shard_map/ppermute | solution.py:403
  127.1 6.2 %copy-start.5 = (bf16[1024,512]{1,0:T(8,128)(2,1)}, bf16[1024,512]{1,0:T(8,128)(2,1)S(1)}, u32[]{:S(2)}) copy-start(bf16[1024,512]{1,0:T(8,128)(2,1)S(1)} %collective-permute-done.6.x3) | copy-start | bytes 3145732
  127.1 21.1 %collective-permute-start.7 = (bf16[1024,512]{1,0:T(8,128)(2,1)S(1)}, bf16[1024,512]{1,0:T(8,128)(2,1)S(1)}, u32[]{:S(2)}, u32[]{:S(2)}) collective-permute-start(bf16[1024,512]{1,0:T(8,128)(2,1)S(1)} %collective-permute-done.6.x3), channel_id=1, source_target_pairs={{8,0},{9,1},{10,2},{11,3},{12,4},{13,5},{14,6},{15,7},{16,8},{17,9... | collective-permute-start | bytes 3145736 | tf_op jit(solution)/shard_map/ppermute | solution.py:403
  130.0 14.5 %all-to-all-start.4 = ((f32[4,8,512]{2,1,0:T(8,128)}), f32[4,8,512]{2,1,0:T(8,128)S(1)}, u32[]{:S(2)}, u32[]{:S(2)}) async-start(f32[4,8,512]{2,1,0:T(8,128)} %broadcast_in_dim.5), calls=%async_computation.4 | async-start | bytes 131072 | tf_op jit(solution)/shard_map/all_to_all | solution.py:434
  141.4 6.9 %collective-permute-start.8 = (bf16[16,512]{1,0:T(8,128)(2,1)}, bf16[16,512]{1,0:T(8,128)(2,1)S(1)}, u32[]{:S(2)}, u32[]{:S(2)}) collective-permute-start(bf16[16,512]{1,0:T(8,128)(2,1)} %get-tuple-element.33), channel_id=1, source_target_pairs={{8,0},{9,1},{10,2},{11,3},{12,4},{13,5},{14,6},{15,7},{16,8},{17,9... | collective-permute-start | bytes 49160 | tf_op jit(solution)/shard_map/ppermute | solution.py:403
  148.2 0.6 copy-start.10
  148.2 1.0 copy-start.8
  154.8 21.6 %all-to-all-start.5 = ((bf16[8,144,512]{2,1,0:T(8,128)(2,1)}), bf16[8,144,512]{2,1,0:T(8,128)(2,1)S(1)}, u32[]{:S(2)}, u32[]{:S(2)}) async-start(bf16[8,144,512]{2,1,0:T(8,128)(2,1)} %finish.1), calls=%async_computation.5 | async-start | bytes 2359296 | tf_op jit(solution)/shard_map/all_to_all | solution.py:398
  176.4 1.0 copy-start.1

commit v3 on v2

--- a/solution.py
+++ b/solution.py
@@ -101,14 +101,23 @@
     )(half.reshape(1), scale, raw)
 
 
-def unpack_kernel(lane, source_ref, got, extra, out_ref, short_ref, norm_ref):
+def unpack_kernel(lane, source_ref, got, out_ref, short_ref, norm_ref, tiles, sems):
     width = got.shape[2]
+    rows = out_ref.shape[1]
+    behind = got.at[:, pl.ds(rows, HEAD), pl.ds(0, GW)]
+    terms_copy = pltpu.make_async_copy(behind, tiles, sems.at[PLANE])
+    terms_copy.start()
+    copies = []
     for p in range(PLANE):
-        out_ref[0, :, p * width : (p + 1) * width] = got[p]
+        source = got.at[p, pl.ds(0, rows), :]
+        target = out_ref.at[0, :, pl.ds(p * width, width)]
+        copies.append(pltpu.make_async_copy(source, target, sems.at[p]))
+        copies[-1].start()
+    terms_copy.wait()
     norm = jnp.zeros((8, 1), F32)
     short = jnp.zeros((8, lane), F32)
     for p in range(PLANE):
-        tile = extra[p].astype(F32)[:8]
+        tile = tiles[p].astype(F32)[:8]
         at = 3 * lane
         norm = norm + (tile[:, at : at + 1] + tile[:, at + 8 : at + 9] + tile[:, at + 16 : at + 17])
         terms = tile[:, :lane] + tile[:, lane : 2 * lane] + tile[:, 2 * lane : 3 * lane]
@@ -117,31 +126,32 @@
     short = jnp.where(jnp.abs(norm) < jnp.inf, short, jnp.zeros_like(short))
     short_ref[...] = short[: short_ref.shape[0], :]
     norm_ref[...] = norm[:1, :]
+    for copy in copies:
+        copy.wait()
 
 
 def unpack(source, got, rows, width, lane):
     return pl.pallas_call(
         functools.partial(unpack_kernel, lane),
-        grid=(1,),
-        in_specs=[
-            pl.BlockSpec(memory_space=pltpu.SMEM),
-            pl.BlockSpec((PLANE, rows, got.shape[2]), lambda i: (0, 0, 0)),
-            pl.BlockSpec((PLANE, HEAD, GW), lambda i: (0, rows // HEAD, 0)),
-        ],
+        in_specs=[pl.BlockSpec(memory_space=pltpu.SMEM), pl.BlockSpec(memory_space=pl.ANY)],
         out_specs=[
-            pl.BlockSpec((1, rows, PLANE * got.shape[2]), lambda i: (0, 0, 0)),
-            pl.BlockSpec((width, lane), lambda i: (0, 0)),
-            pl.BlockSpec((1, 1), lambda i: (0, 0)),
+            pl.BlockSpec(memory_space=pl.ANY),
+            pl.BlockSpec(memory_space=pltpu.VMEM),
+            pl.BlockSpec(memory_space=pltpu.VMEM),
         ],
         out_shape=[
             jax.ShapeDtypeStruct((1, rows, PLANE * got.shape[2]), BF16),
             jax.ShapeDtypeStruct((width, lane), F32),
             jax.ShapeDtypeStruct((1, 1), F32),
         ],
-        compiler_params=params(),
+        scratch_shapes=[
+            pltpu.VMEM((PLANE, HEAD, GW), BF16),
+            pltpu.SemaphoreType.DMA((PLANE + 1,)),
+        ],
+        compiler_params=pltpu.CompilerParams(vmem_limit_bytes=4 * 1024 * 1024),
         cost_estimate=cost(0, 4 * got.size),
         name="unpack",
-    )(source.reshape(1), got, got)
+    )(source.reshape(1), got)
 
 
 def toeplitz_kernel(taps_ref, all_ref, far_ref):
@@ -413,14 +423,15 @@
     tiles, far_tiles = toeplitz(filters)
     feat1 = swap(pack(after(feat1, x0))).reshape(rows, own)
     feat0 = pack(after(features, x0))
-    x1 = after(hop(x0, -1), feat0, feat1, tiles)
+    x1 = hop(x0, -1)
+    x1_next = after(x1, feat0, feat1, tiles)
     feat0 = swap(after(feat0, feat1)).reshape(rows, own)
     feat2 = hop(feat1, 1)
     feat3_tail = hop(feat1[rows - HEAD :], 2)
     x4_head = hop(x0[:HEAD], -4)
 
     acc, mid = early(x0, x1, tiles)
-    x2 = after(hop(x1, -1), acc, feat0, feat2, feat3_tail, x4_head)
+    x2 = after(hop(x1_next, -1), acc, feat0, feat2, feat3_tail, x4_head)
     raw = all_terms(width, acc, mid, x2, feat0, feat1, feat2, feat3_tail, far_tiles)
     along_z = [[k * PLANE + i for k in range(planes)] for i in range(PLANE)]
     copies = jnp.broadcast_to(raw.astype(BF16)[None], (planes,) + raw.shape)

time: 181 us -> 179 us (0.989)
    unnamed x24 -> x22, local copies, waits for them, and re-layouts: 4.06 us -> 3 us
where the time goes in v3:
time: 179 us; the launch traced here: 178 us
  blocking collectives  49.1 us (27%)
  Pallas kernels  47.2 us (26%)
  starting transfers between devices  46.6 us (26%)
  waiting for transfers between devices  26.4 us (15%)
  local copies, waits for them, and re-layouts  4.94 us (3%)
  other arithmetic  2.22 us (1%)
    ppermute x9, starting transfers between devices, hop(): return lax.ppermute(x, 'ctx', route)  30.3 us
    all_to_all x1, blocking collectives, per_device(): lax.all_to_all(copies, 'ctx', 0, 0, axis_index_groups=along_z, tiled=True)  25.4 us
    all_to_all x1, blocking collectives, swap(): lax.all_to_all(x, 'ctx', 0, 0, axis_index_groups=in_plane, tiled=True)  23.8 us
    all_to_all x3, waiting for transfers between devices, swap(): lax.all_to_all(x, 'ctx', 0, 0, axis_index_groups=in_plane, tiled=True)  20.6 us
    all_to_all x3, starting transfers between devices, swap(): lax.all_to_all(x, 'ctx', 0, 0, axis_index_groups=in_plane, tiled=True)  13 us
    pallas_call x1, Pallas kernels, all_terms(): pl.pallas_call(functools.partial(terms_kernel, width), grid=(groups,), in...  9.37 us
    pallas_call x1, Pallas kernels, third(): pl.pallas_call(third_kernel, grid=(groups,), in_specs=[col, col, col, pl....  8.04 us
    pallas_call x1, Pallas kernels, early(): pl.pallas_call(early_kernel, grid=(groups,), in_specs=[col, col, pl.Block...  7.81 us
  transfers between devices with their start and end apart: 13, of which 5 were waited for; matrix products, arithmetic and copies ran while one was open for 2% of the time, Pallas kernels for 22%

profile of v3, /device:TPU:32, one launch (start us, length us, event | category | flops | bytes accessed | tf_op | source)
XLA Modules:
  0.0 178.0 jit_solution(7497536107979585291)
XLA Ops:
  0.6 4.0 %collective-permute-start.1 = (bf16[1,128,4096]{2,1,0:T(8,128)(2,1)}, bf16[1,128,4096]{2,1,0:T(8,128)(2,1)S(1)}, u32[]{:S(2)}, u32[]{:S(2)}) collective-permute-start(bf16[1,128,4096]{2,1,0:T(8,128)(2,1)} %src_ref), channel_id=1, source_target_pairs={{0,8},{1,9},{2,10},{3,11},{4,12},{5,13},{6,14},{7,15},{8,16},{9,17... | collective-permute-start | bytes 3145736 | tf_op jit(solution)/shard_map/ppermute | solution.py:413
  4.6 2.8 %gate.1 = bf16[8,128,512]{2,1,0:T(8,128)(2,1)} custom-call(bf16[1,128,4096]{2,1,0:T(8,128)(2,1)} %up_ref.1, bf16[1,128,4096]{2,1,0:T(8,128)(2,1)} %gate_ref.1), custom_call_target="tpu_custom_call" | custom-call | flops 8192 | bytes 49152 | tf_op jit(solution)/shard_map/gate/pallas_call | solution.py:44
  7.4 23.8 %all_to_all.30 = bf16[8,128,512]{2,1,0:T(8,128)(2,1)S(1)} all-to-all(bf16[8,128,512]{2,1,0:T(8,128)(2,1)} %gate.1), channel_id=1, replica_groups={{0,1,2,3,4,5,6,7},{8,9,10,11,12,13,14,15},{16,17,18,19,20,21,22,23},{24..., dimensions={0} | all-to-all | bytes 2097152 | tf_op jit(solution)/shard_map/all_to_all | solution.py:408
  31.2 2.1 %collective-permute-start = (bf16[1024,512]{1,0:T(8,128)(2,1)S(1)}, bf16[1024,512]{1,0:T(8,128)(2,1)S(1)}, u32[]{:S(2)}, u32[]{:S(2)}) collective-permute-start(bf16[1024,512]{1,0:T(8,128)(2,1)S(1)} %bitcast.9), channel_id=1, source_target_pairs={{8,0},{9,1},{10,2},{11,3},{12,4},{13,5},{14,6},{15,7},{16,8},{17,9... | collective-permute-start | bytes 3145736 | tf_op jit(solution)/shard_map/ppermute | solution.py:413
  33.3 1.0 copy-done.5
  34.3 2.3 %pack.3 = bf16[8,128,512]{2,1,0:T(8,128)(2,1)} custom-call(bf16[1,128,4096]{2,1,0:T(8,128)(2,1)} %copy-done.5), custom_call_target="tpu_custom_call" | custom-call | bytes 32768 | tf_op jit(solution)/shard_map/pack/pallas_call | solution.py:61
  36.5 3.6 %all-to-all-start.1 = ((bf16[8,128,512]{2,1,0:T(8,128)(2,1)}), bf16[8,128,512]{2,1,0:T(8,128)(2,1)S(1)}, u32[]{:S(2)}, u32[]{:S(2)}) async-start(bf16[8,128,512]{2,1,0:T(8,128)(2,1)} %pack.3), calls=%async_computation.1 | async-start | bytes 2097152 | tf_op jit(solution)/shard_map/all_to_all | solution.py:408
  41.7 6.0 %toeplitz.1 = (bf16[4,256,4352]{2,1,0:T(8,128)(2,1)}, bf16[4,256,2048]{2,1,0:T(8,128)(2,1)}) custom-call(f32[4,1,4096]{2,1,0:T(1,128)} %reshape.40.taps_ref), custom_call_target="tpu_custom_call" | custom-call | flops 1048576 | bytes 393216 | tf_op jit(solution)/shard_map/toeplitz/pallas_call | solution.py:171
  47.7 2.3 %pack.2 = bf16[8,128,512]{2,1,0:T(8,128)(2,1)} custom-call(bf16[1,128,4096]{2,1,0:T(8,128)(2,1)} %src_ref), custom_call_target="tpu_custom_call" | custom-call | bytes 32768 | tf_op jit(solution)/shard_map/pack/pallas_call | solution.py:61
  50.0 4.1 %all-to-all-done.1 = bf16[8,128,512]{2,1,0:T(8,128)(2,1)S(1)} async-done(((bf16[8,128,512]{2,1,0:T(8,128)(2,1)}), bf16[8,128,512]{2,1,0:T(8,128)(2,1)S(1)}, u32[]{:S(2)}, u32[]{:S(2)}) %all-to-all-start.1) | async-done | bytes 1048608 | tf_op jit(solution)/shard_map/all_to_all | solution.py:408
  54.1 1.9 %collective-permute-done.x1 = bf16[1024,512]{1,0:T(8,128)(2,1)S(1)} collective-permute-done((bf16[1024,512]{1,0:T(8,128)(2,1)S(1)}, bf16[1024,512]{1,0:T(8,128)(2,1)S(1)}, u32[]{:S(2)}, u32[]{:S(2)}) %collective-permute-start) | collective-permute-done | bytes 1048608 | tf_op jit(solution)/shard_map/ppermute | solution.py:413
  56.0 1.0 copy-done.6
  57.0 2.0 %collective-permute-start.2 = (bf16[1024,512]{1,0:T(8,128)(2,1)}, bf16[1024,512]{1,0:T(8,128)(2,1)S(1)}, u32[]{:S(2)}, u32[]{:S(2)}) collective-permute-start(bf16[1024,512]{1,0:T(8,128)(2,1)} %copy-done.6), channel_id=1, source_target_pairs={{8,0},{9,1},{10,2},{11,3},{12,4},{13,5},{14,6},{15,7},{16,8},{17,9... | collective-permute-start | bytes 3145736 | tf_op jit(solution)/shard_map/ppermute | solution.py:413
  59.0 4.9 %collective-permute-start.3 = (bf16[1024,512]{1,0:T(8,128)(2,1)S(1)}, bf16[1024,512]{1,0:T(8,128)(2,1)}, u32[]{:S(2)}, u32[]{:S(2)}) collective-permute-start(bf16[1024,512]{1,0:T(8,128)(2,1)S(1)} %bitcast.6), channel_id=1, source_target_pairs={{0,8},{1,9},{2,10},{3,11},{4,12},{5,13},{6,14},{7,15},{8,16},{9,17... | collective-permute-start | bytes 3145736 | tf_op jit(solution)/shard_map/ppermute | solution.py:413
  63.9 4.2 %all-to-all-start.2 = ((bf16[8,128,512]{2,1,0:T(8,128)(2,1)}), bf16[8,128,512]{2,1,0:T(8,128)(2,1)}, u32[]{:S(2)}, u32[]{:S(2)}) async-start(bf16[8,128,512]{2,1,0:T(8,128)(2,1)} %pack.2), calls=%async_computation.2 | async-start | bytes 2097152 | tf_op jit(solution)/shard_map/all_to_all | solution.py:408
  68.2 1.3 collective-permute-start.5
  69.5 7.5 %collective-permute-start.4 = (bf16[16,512]{1,0:T(8,128)(2,1)S(1)}, bf16[16,512]{1,0:T(8,128)(2,1)S(1)}, u32[]{:S(2)}, u32[]{:S(2)}) collective-permute-start(bf16[16,512]{1,0:T(8,128)(2,1)S(1)} %slice.8), channel_id=1, source_target_pairs={{0,16},{1,17},{2,18},{3,19},{4,20},{5,21},{6,22},{7,23},{8,24},{9,... | collective-permute-start | bytes 49160 | tf_op jit(solution)/shard_map/ppermute | solution.py:413
  77.0 7.8 %early.1 = (f32[1024,512]{1,0:T(8,128)}, f32[1024,512]{1,0:T(8,128)}) custom-call(bf16[1024,512]{1,0:T(8,128)(2,1)} %bitcast.11, bf16[1024,512]{1,0:T(8,128)(2,1)} %copy-done.6, bf16[4,256,4352]{2,1,0:T(8,128)(2,1)} %get-tuple-element.22.tiles), custom_call_target="tpu_custom_call" | custom-call | flops 201326592 | bytes 98304 | tf_op jit(solution)/shard_map/early/pallas_call | solution.py:256
  84.9 2.3 %collective-permute-done.5.x4_head = bf16[16,512]{1,0:T(8,128)(2,1)S(1)} collective-permute-done((bf16[16,512]{1,0:T(8,128)(2,1)S(1)}, bf16[16,512]{1,0:T(8,128)(2,1)S(1)}, u32[]{:S(2)}, u32[]{:S(2)}) %collective-permute-start.5) | collective-permute-done | bytes 16416 | tf_op jit(solution)/shard_map/ppermute | solution.py:413
  87.2 4.4 %collective-permute-start.6 = (bf16[1024,512]{1,0:T(8,128)(2,1)S(1)}, bf16[1024,512]{1,0:T(8,128)(2,1)S(1)}, u32[]{:S(2)}, u32[]{:S(2)}) collective-permute-start(bf16[1024,512]{1,0:T(8,128)(2,1)S(1)} %collective-permute-done.2.x2), channel_id=1, source_target_pairs={{8,0},{9,1},{10,2},{11,3},{12,4},{13,5},{14,6},{15,7},{16,8},{17,9... | collective-permute-start | bytes 3145736 | tf_op jit(solution)/shard_map/ppermute | solution.py:413
  91.7 9.4 %all_terms.1 = f32[8,512]{1,0:T(8,128)} custom-call(f32[1024,512]{1,0:T(8,128)} %get-tuple-element.23.acc.acc_in, f32[1024,512]{1,0:T(8,128)} %get-tuple-element.29.mid, bf16[1024,512]{1,0:T(8,128)(2,1)} %copy-done.3, bf16[1024,512]{1,0:T(8,128)(2,1)} %bitcast.3.f0, bf16[1024,512]{1,0:T(8,128)(2,1)} %bitcast.8, bf16[1024,512]{1,0:T(8,128)(2,1)} %collective-permute-done.3.f2, ...), custom_call_target="tpu_custom_call" | custom-call | flops 134217728 | bytes 163840 | tf_op jit(solution)/shard_map/all_terms/pallas_call | solution.py:289
  101.8 25.4 %all_to_all.31 = bf16[16,8,512]{2,1,0:T(8,128)(2,1)S(1)} all-to-all(bf16[16,8,512]{2,1,0:T(8,128)(2,1)S(1)} %broadcast_in_dim.4), channel_id=1, replica_groups={{0,8,16,24,32,40,48,56,64,72,80,88,96,104,112,120},{1,9,17,25,33,41,49,..., dimensions={0} | all-to-all | bytes 262144 | tf_op jit(solution)/shard_map/all_to_all | solution.py:438
  127.2 2.2 %collective-permute-start.7 = (bf16[1024,512]{1,0:T(8,128)(2,1)S(1)}, bf16[1024,512]{1,0:T(8,128)(2,1)S(1)}, u32[]{:S(2)}, u32[]{:S(2)}) collective-permute-start(bf16[1024,512]{1,0:T(8,128)(2,1)S(1)} %collective-permute-done.6.x3), channel_id=1, source_target_pairs={{8,0},{9,1},{10,2},{11,3},{12,4},{13,5},{14,6},{15,7},{16,8},{17,9... | collective-permute-start | bytes 3145736 | tf_op jit(solution)/shard_map/ppermute | solution.py:413
  130.0 3.3 %all-to-all-start.4 = ((f32[4,8,512]{2,1,0:T(8,128)}), f32[4,8,512]{2,1,0:T(8,128)S(1)}, u32[]{:S(2)}, u32[]{:S(2)}) async-start(f32[4,8,512]{2,1,0:T(8,128)} %broadcast_in_dim.5), calls=%async_computation.4 | async-start | bytes 131072 | tf_op jit(solution)/shard_map/all_to_all | solution.py:445
  133.3 8.0 %third.1 = (f32[1024,512]{1,0:T(8,128)}, bf16[16,512]{1,0:T(8,128)(2,1)}) custom-call(f32[1024,512]{1,0:T(8,128)} %get-tuple-element.23.acc.acc_in, bf16[1024,512]{1,0:T(8,128)(2,1)} %copy-done.3, bf16[1024,512]{1,0:T(8,128)(2,1)} %copy-done.4, bf16[16,512]{1,0:T(8,128)(2,1)} %copy-done.8, bf16[4,256,4352]{2,1,0:T(8,128)(2,1)} %get-tuple-element.22.tiles), custom_call_target="tpu_custom_call" | custom-call | flops 150994944 | bytes 98304 | tf_op jit(solution)/shard_map/third/pallas_call | solution.py:328
  141.4 1.9 %collective-permute-start.8 = (bf16[16,512]{1,0:T(8,128)(2,1)}, bf16[16,512]{1,0:T(8,128)(2,1)S(1)}, u32[]{:S(2)}, u32[]{:S(2)}) collective-permute-start(bf16[16,512]{1,0:T(8,128)(2,1)} %get-tuple-element.33), channel_id=1, source_target_pairs={{8,0},{9,1},{10,2},{11,3},{12,4},{13,5},{14,6},{15,7},{16,8},{17,9... | collective-permute-start | bytes 49160 | tf_op jit(solution)/shard_map/ppermute | solution.py:413
  145.2 1.5 prepare.1.extra
  146.6 1.6 collective-permute-done.8.next_head
  149.2 5.6 %finish.1 = bf16[8,144,512]{2,1,0:T(8,128)(2,1)} custom-call(f32[1024,512]{1,0:T(8,128)} %get-tuple-element.32.acc_in, bf16[1024,512]{1,0:T(8,128)(2,1)} %copy-done.7, bf16[4,256,2048]{2,1,0:T(8,128)(2,1)} %get-tuple-element.30.tiles, bf16[16,512]{1,0:T(8,128)(2,1)} %copy-done.9, f32[7,512]{1,0:T(8,128)} %constant_dynamic-slice_fusion.taps, ...), custom_call_target="tpu_custom_call" | custom-call | flops 50331648 | bytes 65536 | tf_op jit(solution)/shard_map/finish/pallas_call | solution.py:373
  154.8 5.2 %all-to-all-start.5 = ((bf16[8,144,512]{2,1,0:T(8,128)(2,1)}), bf16[8,144,512]{2,1,0:T(8,128)(2,1)S(1)}, u32[]{:S(2)}, u32[]{:S(2)}) async-start(bf16[8,144,512]{2,1,0:T(8,128)(2,1)} %finish.1), calls=%async_computation.5 | async-start | bytes 2359296 | tf_op jit(solution)/shard_map/all_to_all | solution.py:408
  160.0 16.4 %all-to-all-done.5.got = bf16[8,144,512]{2,1,0:T(8,128)(2,1)S(1)} async-done(((bf16[8,144,512]{2,1,0:T(8,128)(2,1)}), bf16[8,144,512]{2,1,0:T(8,128)(2,1)S(1)}, u32[]{:S(2)}, u32[]{:S(2)}) %all-to-all-start.5) | async-done | bytes 1179680 | tf_op jit(solution)/shard_map/all_to_all | solution.py:408
  176.4 1.6 unpack.1
  (38 shorter events, 5.2 us)
Async XLA Ops:
  0.6 142.7 %copy-start = (f32[7,4096]{1,0:T(8,128)S(1)}, f32[7,4096]{1,0:T(8,128)}, u32[]{:S(2)}) copy-start(f32[7,4096]{1,0:T(8,128)} %param.9) | copy-start | bytes 344068
  0.6 32.6 %collective-permute-start.1 = (bf16[1,128,4096]{2,1,0:T(8,128)(2,1)}, bf16[1,128,4096]{2,1,0:T(8,128)(2,1)S(1)}, u32[]{:S(2)}, u32[]{:S(2)}) collective-permute-start(bf16[1,128,4096]{2,1,0:T(8,128)(2,1)} %src_ref), channel_id=1, source_target_pairs={{0,8},{1,9},{2,10},{3,11},{4,12},{5,13},{6,14},{7,15},{8,16},{9,17... | collective-permute-start | bytes 3145736 | tf_op jit(solution)/shard_map/ppermute | solution.py:413
  31.2 37.0 %copy-start.2 = (bf16[8,128,512]{2,1,0:T(8,128)(2,1)}, bf16[8,128,512]{2,1,0:T(8,128)(2,1)S(1)}, u32[]{:S(2)}) copy-start(bf16[8,128,512]{2,1,0:T(8,128)(2,1)S(1)} %all_to_all.30) | copy-start | bytes 3145732
  31.2 24.8 %collective-permute-start = (bf16[1024,512]{1,0:T(8,128)(2,1)S(1)}, bf16[1024,512]{1,0:T(8,128)(2,1)S(1)}, u32[]{:S(2)}, u32[]{:S(2)}) collective-permute-start(bf16[1024,512]{1,0:T(8,128)(2,1)S(1)} %bitcast.9), channel_id=1, source_target_pairs={{8,0},{9,1},{10,2},{11,3},{12,4},{13,5},{14,6},{15,7},{16,8},{17,9... | collective-permute-start | bytes 3145736 | tf_op jit(solution)/shard_map/ppermute | solution.py:413
  33.2 1.0 copy-start.5
  36.5 17.6 %all-to-all-start.1 = ((bf16[8,128,512]{2,1,0:T(8,128)(2,1)}), bf16[8,128,512]{2,1,0:T(8,128)(2,1)S(1)}, u32[]{:S(2)}, u32[]{:S(2)}) async-start(bf16[8,128,512]{2,1,0:T(8,128)(2,1)} %pack.3), calls=%async_computation.1 | async-start | bytes 2097152 | tf_op jit(solution)/shard_map/all_to_all | solution.py:408
  54.1 30.7 %copy-start.1 = (bf16[8,128,512]{2,1,0:T(8,128)(2,1)}, bf16[8,128,512]{2,1,0:T(8,128)(2,1)S(1)}, u32[]{:S(2)}) copy-start(bf16[8,128,512]{2,1,0:T(8,128)(2,1)S(1)} %all-to-all-done.1) | copy-start | bytes 3145732
  56.0 1.0 copy-start.6
  57.0 30.2 %collective-permute-start.2 = (bf16[1024,512]{1,0:T(8,128)(2,1)}, bf16[1024,512]{1,0:T(8,128)(2,1)S(1)}, u32[]{:S(2)}, u32[]{:S(2)}) collective-permute-start(bf16[1024,512]{1,0:T(8,128)(2,1)} %copy-done.6), channel_id=1, source_target_pairs={{8,0},{9,1},{10,2},{11,3},{12,4},{13,5},{14,6},{15,7},{16,8},{17,9... | collective-permute-start | bytes 3145736 | tf_op jit(solution)/shard_map/ppermute | solution.py:413
  59.0 28.2 %collective-permute-start.3 = (bf16[1024,512]{1,0:T(8,128)(2,1)S(1)}, bf16[1024,512]{1,0:T(8,128)(2,1)}, u32[]{:S(2)}, u32[]{:S(2)}) collective-permute-start(bf16[1024,512]{1,0:T(8,128)(2,1)S(1)} %bitcast.6), channel_id=1, source_target_pairs={{0,8},{1,9},{2,10},{3,11},{4,12},{5,13},{6,14},{7,15},{8,16},{9,17... | collective-permute-start | bytes 3145736 | tf_op jit(solution)/shard_map/ppermute | solution.py:413
  63.9 23.3 %all-to-all-start.2 = ((bf16[8,128,512]{2,1,0:T(8,128)(2,1)}), bf16[8,128,512]{2,1,0:T(8,128)(2,1)}, u32[]{:S(2)}, u32[]{:S(2)}) async-start(bf16[8,128,512]{2,1,0:T(8,128)(2,1)} %pack.2), calls=%async_computation.2 | async-start | bytes 2097152 | tf_op jit(solution)/shard_map/all_to_all | solution.py:408
  68.2 19.0 %collective-permute-start.5 = (bf16[16,512]{1,0:T(8,128)(2,1)S(1)}, bf16[16,512]{1,0:T(8,128)(2,1)S(1)}, u32[]{:S(2)}, u32[]{:S(2)}) collective-permute-start(bf16[16,512]{1,0:T(8,128)(2,1)S(1)} %slice.9), channel_id=1, source_target_pairs={{32,0},{33,1},{34,2},{35,3},{36,4},{37,5},{38,6},{39,7},{40,8},{41... | collective-permute-start | bytes 49160 | tf_op jit(solution)/shard_map/ppermute | solution.py:413
  69.5 17.7 %collective-permute-start.4 = (bf16[16,512]{1,0:T(8,128)(2,1)S(1)}, bf16[16,512]{1,0:T(8,128)(2,1)S(1)}, u32[]{:S(2)}, u32[]{:S(2)}) collective-permute-start(bf16[16,512]{1,0:T(8,128)(2,1)S(1)} %slice.8), channel_id=1, source_target_pairs={{0,16},{1,17},{2,18},{3,19},{4,20},{5,21},{6,22},{7,23},{8,24},{9,... | collective-permute-start | bytes 49160 | tf_op jit(solution)/shard_map/ppermute | solution.py:413
  87.2 13.9 %copy-start.8 = (bf16[16,512]{1,0:T(8,128)(2,1)}, bf16[16,512]{1,0:T(8,128)(2,1)S(1)}, u32[]{:S(2)}) copy-start(bf16[16,512]{1,0:T(8,128)(2,1)S(1)} %collective-permute-done.5.x4_head) | copy-start | bytes 49156
  87.2 4.5 %copy-start.10 = (bf16[16,512]{1,0:T(8,128)(2,1)}, bf16[16,512]{1,0:T(8,128)(2,1)S(1)}, u32[]{:S(2)}) copy-start(bf16[16,512]{1,0:T(8,128)(2,1)S(1)} %collective-permute-done.4.f3_tail) | copy-start | bytes 49156
  87.2 4.5 %copy-start.3 = (bf16[1024,512]{1,0:T(8,128)(2,1)}, bf16[1024,512]{1,0:T(8,128)(2,1)S(1)}, u32[]{:S(2)}) copy-start(bf16[1024,512]{1,0:T(8,128)(2,1)S(1)} %collective-permute-done.2.x2) | copy-start | bytes 3145732
  87.2 39.9 %collective-permute-start.6 = (bf16[1024,512]{1,0:T(8,128)(2,1)S(1)}, bf16[1024,512]{1,0:T(8,128)(2,1)S(1)}, u32[]{:S(2)}, u32[]{:S(2)}) collective-permute-start(bf16[1024,512]{1,0:T(8,128)(2,1)S(1)} %collective-permute-done.2.x2), channel_id=1, source_target_pairs={{8,0},{9,1},{10,2},{11,3},{12,4},{13,5},{14,6},{15,7},{16,8},{17,9... | collective-permute-start | bytes 3145736 | tf_op jit(solution)/shard_map/ppermute | solution.py:413
  127.1 6.2 %copy-start.4 = (bf16[1024,512]{1,0:T(8,128)(2,1)}, bf16[1024,512]{1,0:T(8,128)(2,1)S(1)}, u32[]{:S(2)}) copy-start(bf16[1024,512]{1,0:T(8,128)(2,1)S(1)} %collective-permute-done.6.x3) | copy-start | bytes 3145732
  127.2 21.1 %collective-permute-start.7 = (bf16[1024,512]{1,0:T(8,128)(2,1)S(1)}, bf16[1024,512]{1,0:T(8,128)(2,1)S(1)}, u32[]{:S(2)}, u32[]{:S(2)}) collective-permute-start(bf16[1024,512]{1,0:T(8,128)(2,1)S(1)} %collective-permute-done.6.x3), channel_id=1, source_target_pairs={{8,0},{9,1},{10,2},{11,3},{12,4},{13,5},{14,6},{15,7},{16,8},{17,9... | collective-permute-start | bytes 3145736 | tf_op jit(solution)/shard_map/ppermute | solution.py:413
  130.0 14.5 %all-to-all-start.4 = ((f32[4,8,512]{2,1,0:T(8,128)}), f32[4,8,512]{2,1,0:T(8,128)S(1)}, u32[]{:S(2)}, u32[]{:S(2)}) async-start(f32[4,8,512]{2,1,0:T(8,128)} %broadcast_in_dim.5), calls=%async_computation.4 | async-start | bytes 131072 | tf_op jit(solution)/shard_map/all_to_all | solution.py:445
  141.4 6.8 %collective-permute-start.8 = (bf16[16,512]{1,0:T(8,128)(2,1)}, bf16[16,512]{1,0:T(8,128)(2,1)S(1)}, u32[]{:S(2)}, u32[]{:S(2)}) collective-permute-start(bf16[16,512]{1,0:T(8,128)(2,1)} %get-tuple-element.33), channel_id=1, source_target_pairs={{8,0},{9,1},{10,2},{11,3},{12,4},{13,5},{14,6},{15,7},{16,8},{17,9... | collective-permute-start | bytes 49160 | tf_op jit(solution)/shard_map/ppermute | solution.py:413
  148.2 0.6 copy-start.9
  148.2 1.0 copy-start.7
  154.8 21.6 %all-to-all-start.5 = ((bf16[8,144,512]{2,1,0:T(8,128)(2,1)}), bf16[8,144,512]{2,1,0:T(8,128)(2,1)S(1)}, u32[]{:S(2)}, u32[]{:S(2)}) async-start(bf16[8,144,512]{2,1,0:T(8,128)(2,1)} %finish.1), calls=%async_computation.5 | async-start | bytes 2359296 | tf_op jit(solution)/shard_map/all_to_all | solution.py:408

commit v4 on v3

--- a/solution.py
+++ b/solution.py
@@ -342,7 +342,7 @@
         ],
         scratch_shapes=[pairs_of(2 * rows)],
         compiler_params=params(),
-        cost_estimate=cost(18 * rows * rows * GW * groups, 12 * rows * own),
+        cost_estimate=cost(SHORT * 72 * rows * rows * GW * groups, SHORT * 48 * rows * own),
         name="third",
     )(acc, x2, x3, x4_head, tiles)
 
@@ -435,11 +435,11 @@
     raw = all_terms(width, acc, mid, x2, feat0, feat1, feat2, feat3_tail, far_tiles)
     along_z = [[k * PLANE + i for k in range(planes)] for i in range(PLANE)]
     copies = jnp.broadcast_to(raw.astype(BF16)[None], (planes,) + raw.shape)
+    x3 = after(hop(x2, -1), copies)
     copies = lax.all_to_all(copies, "ctx", 0, 0, axis_index_groups=along_z, tiled=True)
-    x3 = after(hop(x2, -1), copies)
     x4 = hop(x3, -1)
-    raw = jnp.sum(after(copies, x3).astype(F32), axis=0)
     acc, head = third(acc, x2, x3, x4_head, tiles)
+    raw = jnp.sum(after(copies, head).astype(F32), axis=0)
     next_head = hop(head, -1)
     copies = jnp.broadcast_to(raw[None], (lax.axis_size("dp"),) + raw.shape)
     raw = jnp.sum(lax.all_to_all(copies, "dp", 0, 0, tiled=True), axis=0)

time: 179 us -> 172 us (0.961)
  the two profiles are of different devices: /device:TPU:32 before, /device:TPU:480 now
where the time goes in v4:
time: 172 us; the launch traced here: 171 us
  starting transfers between devices  64 us (37%)
  Pallas kernels  47.2 us (27%)
  waiting for transfers between devices  27.2 us (16%)
  blocking collectives  24.1 us (14%)
  local copies, waits for them, and re-layouts  4.61 us (3%)
  other arithmetic  2.22 us (1%)
    ppermute x9, starting transfers between devices, hop(): return lax.ppermute(x, 'ctx', route)  39.2 us
    all_to_all x1, blocking collectives, swap(): lax.all_to_all(x, 'ctx', 0, 0, axis_index_groups=in_plane, tiled=True)  24.1 us
    all_to_all x3, waiting for transfers between devices, swap(): lax.all_to_all(x, 'ctx', 0, 0, axis_index_groups=in_plane, tiled=True)  20.9 us
    all_to_all x3, starting transfers between devices, swap(): lax.all_to_all(x, 'ctx', 0, 0, axis_index_groups=in_plane, tiled=True)  12.4 us
    pallas_call x1, Pallas kernels, all_terms(): pl.pallas_call(functools.partial(terms_kernel, width), grid=(groups,), in...  9.36 us
    all_to_all x1, starting transfers between devices, per_device(): lax.all_to_all(copies, 'ctx', 0, 0, axis_index_groups=along_z, tiled=True)  9.08 us
    pallas_call x1, Pallas kernels, third(): pl.pallas_call(third_kernel, grid=(groups,), in_specs=[col, col, col, pl....  8.02 us
    pallas_call x1, Pallas kernels, early(): pl.pallas_call(early_kernel, grid=(groups,), in_specs=[col, col, pl.Block...  7.81 us
  transfers between devices with their start and end apart: 14, of which 6 were waited for; matrix products, arithmetic and copies ran while one was open for 3% of the time, Pallas kernels for 23%

profile of v4, /device:TPU:480, one launch (start us, length us, event | category | flops | bytes accessed | tf_op | source)
XLA Modules:
  0.0 170.8 jit_solution(7280242828827224756)
XLA Ops:
  0.6 1.4 collective-permute-start.1
  2.1 2.8 %gate.1 = bf16[8,128,512]{2,1,0:T(8,128)(2,1)} custom-call(bf16[1,128,4096]{2,1,0:T(8,128)(2,1)} %up_ref.1, bf16[1,128,4096]{2,1,0:T(8,128)(2,1)} %gate_ref.1), custom_call_target="tpu_custom_call" | custom-call | flops 8192 | bytes 49152 | tf_op jit(solution)/shard_map/gate/pallas_call | solution.py:44
  4.8 24.1 %all_to_all.30 = bf16[8,128,512]{2,1,0:T(8,128)(2,1)S(1)} all-to-all(bf16[8,128,512]{2,1,0:T(8,128)(2,1)} %gate.1), channel_id=1, replica_groups={{0,1,2,3,4,5,6,7},{8,9,10,11,12,13,14,15},{16,17,18,19,20,21,22,23},{24..., dimensions={0} | all-to-all | bytes 2097152 | tf_op jit(solution)/shard_map/all_to_all | solution.py:408
  28.9 5.3 %collective-permute-start = (bf16[1024,512]{1,0:T(8,128)(2,1)S(1)}, bf16[1024,512]{1,0:T(8,128)(2,1)}, u32[]{:S(2)}, u32[]{:S(2)}) collective-permute-start(bf16[1024,512]{1,0:T(8,128)(2,1)S(1)} %bitcast.9), channel_id=1, source_target_pairs={{8,0},{9,1},{10,2},{11,3},{12,4},{13,5},{14,6},{15,7},{16,8},{17,9... | collective-permute-start | bytes 3145736 | tf_op jit(solution)/shard_map/ppermute | solution.py:413
  34.2 1.0 copy-done.4
  35.2 2.3 %pack.3 = bf16[8,128,512]{2,1,0:T(8,128)(2,1)} custom-call(bf16[1,128,4096]{2,1,0:T(8,128)(2,1)} %copy-done.4), custom_call_target="tpu_custom_call" | custom-call | bytes 32768 | tf_op jit(solution)/shard_map/pack/pallas_call | solution.py:61
  37.5 3.6 %all-to-all-start.1 = ((bf16[8,128,512]{2,1,0:T(8,128)(2,1)}), bf16[8,128,512]{2,1,0:T(8,128)(2,1)S(1)}, u32[]{:S(2)}, u32[]{:S(2)}) async-start(bf16[8,128,512]{2,1,0:T(8,128)(2,1)} %pack.3), calls=%async_computation.1 | async-start | bytes 2097152 | tf_op jit(solution)/shard_map/all_to_all | solution.py:408
  41.1 0.9 dynamic-slice_convert_fusion
  42.6 6.0 %toeplitz.1 = (bf16[4,256,4352]{2,1,0:T(8,128)(2,1)}, bf16[4,256,2048]{2,1,0:T(8,128)(2,1)}) custom-call(f32[4,1,4096]{2,1,0:T(1,128)} %reshape.40.taps_ref), custom_call_target="tpu_custom_call" | custom-call | flops 1048576 | bytes 393216 | tf_op jit(solution)/shard_map/toeplitz/pallas_call | solution.py:171
  48.6 2.3 %pack.2 = bf16[8,128,512]{2,1,0:T(8,128)(2,1)} custom-call(bf16[1,128,4096]{2,1,0:T(8,128)(2,1)} %src_ref), custom_call_target="tpu_custom_call" | custom-call | bytes 32768 | tf_op jit(solution)/shard_map/pack/pallas_call | solution.py:61
  50.9 4.1 %all-to-all-done.1 = bf16[8,128,512]{2,1,0:T(8,128)(2,1)S(1)} async-done(((bf16[8,128,512]{2,1,0:T(8,128)(2,1)}), bf16[8,128,512]{2,1,0:T(8,128)(2,1)S(1)}, u32[]{:S(2)}, u32[]{:S(2)}) %all-to-all-start.1) | async-done | bytes 1048608 | tf_op jit(solution)/shard_map/all_to_all | solution.py:408
  55.0 3.9 %collective-permute-start.2 = (bf16[1024,512]{1,0:T(8,128)(2,1)}, bf16[1024,512]{1,0:T(8,128)(2,1)}, u32[]{:S(2)}, u32[]{:S(2)}) collective-permute-start(bf16[1024,512]{1,0:T(8,128)(2,1)} %collective-permute-done.x1), channel_id=1, source_target_pairs={{8,0},{9,1},{10,2},{11,3},{12,4},{13,5},{14,6},{15,7},{16,8},{17,9... | collective-permute-start | bytes 3145736 | tf_op jit(solution)/shard_map/ppermute | solution.py:413
  58.9 1.3 collective-permute-start.3
  60.2 3.6 %all-to-all-start.2 = ((bf16[8,128,512]{2,1,0:T(8,128)(2,1)}), bf16[8,128,512]{2,1,0:T(8,128)(2,1)S(1)}, u32[]{:S(2)}, u32[]{:S(2)}) async-start(bf16[8,128,512]{2,1,0:T(8,128)(2,1)} %pack.2), calls=%async_computation.2 | async-start | bytes 2097152 | tf_op jit(solution)/shard_map/all_to_all | solution.py:408
  63.9 8.6 %collective-permute-start.5 = (bf16[16,512]{1,0:T(8,128)(2,1)S(1)}, bf16[16,512]{1,0:T(8,128)(2,1)S(1)}, u32[]{:S(2)}, u32[]{:S(2)}) collective-permute-start(bf16[16,512]{1,0:T(8,128)(2,1)S(1)} %slice.9), channel_id=1, source_target_pairs={{32,0},{33,1},{34,2},{35,3},{36,4},{37,5},{38,6},{39,7},{40,8},{41... | collective-permute-start | bytes 49160 | tf_op jit(solution)/shard_map/ppermute | solution.py:413
  72.4 1.3 collective-permute-start.4
  73.7 7.8 %early.1 = (f32[1024,512]{1,0:T(8,128)}, f32[1024,512]{1,0:T(8,128)}) custom-call(bf16[1024,512]{1,0:T(8,128)(2,1)} %bitcast.11, bf16[1024,512]{1,0:T(8,128)(2,1)} %collective-permute-done.x1, bf16[4,256,4352]{2,1,0:T(8,128)(2,1)} %get-tuple-element.22.tiles), custom_call_target="tpu_custom_call" | custom-call | flops 201326592 | bytes 98304 | tf_op jit(solution)/shard_map/early/pallas_call | solution.py:256
  81.6 0.9 collective-permute-done.4.f3_tail
  82.8 5.2 %collective-permute-start.6 = (bf16[1024,512]{1,0:T(8,128)(2,1)}, bf16[1024,512]{1,0:T(8,128)(2,1)}, u32[]{:S(2)}, u32[]{:S(2)}) collective-permute-start(bf16[1024,512]{1,0:T(8,128)(2,1)} %collective-permute-done.2.x2), channel_id=1, source_target_pairs={{8,0},{9,1},{10,2},{11,3},{12,4},{13,5},{14,6},{15,7},{16,8},{17,9... | collective-permute-start | bytes 3145736 | tf_op jit(solution)/shard_map/ppermute | solution.py:413
  88.0 9.4 %all_terms.1 = f32[8,512]{1,0:T(8,128)} custom-call(f32[1024,512]{1,0:T(8,128)} %get-tuple-element.23.acc.acc_in, f32[1024,512]{1,0:T(8,128)} %get-tuple-element.29.mid, bf16[1024,512]{1,0:T(8,128)(2,1)} %collective-permute-done.2.x2, bf16[1024,512]{1,0:T(8,128)(2,1)} %bitcast.12, bf16[1024,512]{1,0:T(8,128)(2,1)} %bitcast.8, ...), custom_call_target="tpu_custom_call" | custom-call | flops 134217728 | bytes 163840 | tf_op jit(solution)/shard_map/all_terms/pallas_call | solution.py:289
  98.8 9.1 %all-to-all-start.3 = ((bf16[16,8,512]{2,1,0:T(8,128)(2,1)}), bf16[16,8,512]{2,1,0:T(8,128)(2,1)S(1)}, u32[]{:S(2)}, u32[]{:S(2)}) async-start(bf16[16,8,512]{2,1,0:T(8,128)(2,1)} %broadcast_in_dim.4), calls=%async_computation.3 | async-start | bytes 262144 | tf_op jit(solution)/shard_map/all_to_all | solution.py:439
  107.9 2.2 %collective-permute-done.6.x3 = bf16[1024,512]{1,0:T(8,128)(2,1)} collective-permute-done((bf16[1024,512]{1,0:T(8,128)(2,1)}, bf16[1024,512]{1,0:T(8,128)(2,1)}, u32[]{:S(2)}, u32[]{:S(2)}) %collective-permute-start.6) | collective-permute-done | bytes 1048608 | tf_op jit(solution)/shard_map/ppermute | solution.py:413
  110.1 8.0 %collective-permute-start.7 = (bf16[1024,512]{1,0:T(8,128)(2,1)}, bf16[1024,512]{1,0:T(8,128)(2,1)S(1)}, u32[]{:S(2)}, u32[]{:S(2)}) collective-permute-start(bf16[1024,512]{1,0:T(8,128)(2,1)} %collective-permute-done.6.x3), channel_id=1, source_target_pairs={{8,0},{9,1},{10,2},{11,3},{12,4},{13,5},{14,6},{15,7},{16,8},{17,9... | collective-permute-start | bytes 3145736 | tf_op jit(solution)/shard_map/ppermute | solution.py:413
  118.1 8.0 %third.1 = (f32[1024,512]{1,0:T(8,128)}, bf16[16,512]{1,0:T(8,128)(2,1)}) custom-call(f32[1024,512]{1,0:T(8,128)} %get-tuple-element.23.acc.acc_in, bf16[1024,512]{1,0:T(8,128)(2,1)} %collective-permute-done.2.x2, bf16[1024,512]{1,0:T(8,128)(2,1)} %collective-permute-done.6.x3, bf16[16,512]{1,0:T(8,128)(2,1)} %copy-done.8, ...), custom_call_target="tpu_custom_call" | custom-call | flops 38654705664 | bytes 25165824 | tf_op jit(solution)/shard_map/third/pallas_call | solution.py:328
  126.1 4.3 %collective-permute-start.8 = (bf16[16,512]{1,0:T(8,128)(2,1)}, bf16[16,512]{1,0:T(8,128)(2,1)S(1)}, u32[]{:S(2)}, u32[]{:S(2)}) collective-permute-start(bf16[16,512]{1,0:T(8,128)(2,1)} %get-tuple-element.33), channel_id=1, source_target_pairs={{8,0},{9,1},{10,2},{11,3},{12,4},{13,5},{14,6},{15,7},{16,8},{17,9... | collective-permute-start | bytes 49160 | tf_op jit(solution)/shard_map/ppermute | solution.py:413
  131.1 3.3 %all-to-all-start.4 = ((f32[4,8,512]{2,1,0:T(8,128)}), f32[4,8,512]{2,1,0:T(8,128)S(1)}, u32[]{:S(2)}, u32[]{:S(2)}) async-start(f32[4,8,512]{2,1,0:T(8,128)} %broadcast_in_dim.5), calls=%async_computation.4 | async-start | bytes 131072 | tf_op jit(solution)/shard_map/all_to_all | solution.py:445
  135.7 2.8 %all-to-all-done.4 = f32[4,8,512]{2,1,0:T(8,128)S(1)} async-done(((f32[4,8,512]{2,1,0:T(8,128)}), f32[4,8,512]{2,1,0:T(8,128)S(1)}, u32[]{:S(2)}, u32[]{:S(2)}) %all-to-all-start.4) | async-done | bytes 65568 | tf_op jit(solution)/shard_map/all_to_all | solution.py:445
  139.1 1.5 prepare.1.extra
  141.5 5.6 %finish.1 = bf16[8,144,512]{2,1,0:T(8,128)(2,1)} custom-call(f32[1024,512]{1,0:T(8,128)} %get-tuple-element.32.acc_in, bf16[1024,512]{1,0:T(8,128)(2,1)} %copy-done.5, bf16[4,256,2048]{2,1,0:T(8,128)(2,1)} %get-tuple-element.30.tiles, bf16[16,512]{1,0:T(8,128)(2,1)} %copy-done.6, f32[7,512]{1,0:T(8,128)} %constant_dynamic-slice_fusion.taps, ...), custom_call_target="tpu_custom_call" | custom-call | flops 50331648 | bytes 65536 | tf_op jit(solution)/shard_map/finish/pallas_call | solution.py:373
  147.1 5.2 %all-to-all-start.5 = ((bf16[8,144,512]{2,1,0:T(8,128)(2,1)}), bf16[8,144,512]{2,1,0:T(8,128)(2,1)S(1)}, u32[]{:S(2)}, u32[]{:S(2)}) async-start(bf16[8,144,512]{2,1,0:T(8,128)(2,1)} %finish.1), calls=%async_computation.5 | async-start | bytes 2359296 | tf_op jit(solution)/shard_map/all_to_all | solution.py:408
  152.3 16.9 %all-to-all-done.5.got = bf16[8,144,512]{2,1,0:T(8,128)(2,1)S(1)} async-done(((bf16[8,144,512]{2,1,0:T(8,128)(2,1)}), bf16[8,144,512]{2,1,0:T(8,128)(2,1)S(1)}, u32[]{:S(2)}, u32[]{:S(2)}) %all-to-all-start.5) | async-done | bytes 1179680 | tf_op jit(solution)/shard_map/all_to_all | solution.py:408
  169.2 1.6 unpack.1
  (35 shorter events, 5.3 us)
Async XLA Ops:
  0.6 133.8 %copy-start = (f32[7,4096]{1,0:T(8,128)S(1)}, f32[7,4096]{1,0:T(8,128)}, u32[]{:S(2)}) copy-start(f32[7,4096]{1,0:T(8,128)} %param.9) | copy-start | bytes 344068
  0.6 33.6 %collective-permute-start.1 = (bf16[1,128,4096]{2,1,0:T(8,128)(2,1)}, bf16[1,128,4096]{2,1,0:T(8,128)(2,1)S(1)}, u32[]{:S(2)}, u32[]{:S(2)}) collective-permute-start(bf16[1,128,4096]{2,1,0:T(8,128)(2,1)} %src_ref), channel_id=1, source_target_pairs={{0,8},{1,9},{2,10},{3,11},{4,12},{5,13},{6,14},{7,15},{8,16},{9,17... | collective-permute-start | bytes 3145736 | tf_op jit(solution)/shard_map/ppermute | solution.py:413
  28.9 34.9 %copy-start.2 = (bf16[8,128,512]{2,1,0:T(8,128)(2,1)}, bf16[8,128,512]{2,1,0:T(8,128)(2,1)S(1)}, u32[]{:S(2)}) copy-start(bf16[8,128,512]{2,1,0:T(8,128)(2,1)S(1)} %all_to_all.30) | copy-start | bytes 3145732
  28.9 26.1 %collective-permute-start = (bf16[1024,512]{1,0:T(8,128)(2,1)S(1)}, bf16[1024,512]{1,0:T(8,128)(2,1)}, u32[]{:S(2)}, u32[]{:S(2)}) collective-permute-start(bf16[1024,512]{1,0:T(8,128)(2,1)S(1)} %bitcast.9), channel_id=1, source_target_pairs={{8,0},{9,1},{10,2},{11,3},{12,4},{13,5},{14,6},{15,7},{16,8},{17,9... | collective-permute-start | bytes 3145736 | tf_op jit(solution)/shard_map/ppermute | solution.py:413
  34.2 1.0 copy-start.4
  37.5 17.5 %all-to-all-start.1 = ((bf16[8,128,512]{2,1,0:T(8,128)(2,1)}), bf16[8,128,512]{2,1,0:T(8,128)(2,1)S(1)}, u32[]{:S(2)}, u32[]{:S(2)}) async-start(bf16[8,128,512]{2,1,0:T(8,128)(2,1)} %pack.3), calls=%async_computation.1 | async-start | bytes 2097152 | tf_op jit(solution)/shard_map/all_to_all | solution.py:408
  55.0 26.6 %copy-start.1 = (bf16[8,128,512]{2,1,0:T(8,128)(2,1)}, bf16[8,128,512]{2,1,0:T(8,128)(2,1)S(1)}, u32[]{:S(2)}) copy-start(bf16[8,128,512]{2,1,0:T(8,128)(2,1)S(1)} %all-to-all-done.1) | copy-start | bytes 3145732
  55.0 27.5 %collective-permute-start.2 = (bf16[1024,512]{1,0:T(8,128)(2,1)}, bf16[1024,512]{1,0:T(8,128)(2,1)}, u32[]{:S(2)}, u32[]{:S(2)}) collective-permute-start(bf16[1024,512]{1,0:T(8,128)(2,1)} %collective-permute-done.x1), channel_id=1, source_target_pairs={{8,0},{9,1},{10,2},{11,3},{12,4},{13,5},{14,6},{15,7},{16,8},{17,9... | collective-permute-start | bytes 3145736 | tf_op jit(solution)/shard_map/ppermute | solution.py:413
  58.9 23.9 %collective-permute-start.3 = (bf16[1024,512]{1,0:T(8,128)(2,1)S(1)}, bf16[1024,512]{1,0:T(8,128)(2,1)}, u32[]{:S(2)}, u32[]{:S(2)}) collective-permute-start(bf16[1024,512]{1,0:T(8,128)(2,1)S(1)} %bitcast.6), channel_id=1, source_target_pairs={{0,8},{1,9},{2,10},{3,11},{4,12},{5,13},{6,14},{7,15},{8,16},{9,17... | collective-permute-start | bytes 3145736 | tf_op jit(solution)/shard_map/ppermute | solution.py:413
  60.2 22.3 %all-to-all-start.2 = ((bf16[8,128,512]{2,1,0:T(8,128)(2,1)}), bf16[8,128,512]{2,1,0:T(8,128)(2,1)S(1)}, u32[]{:S(2)}, u32[]{:S(2)}) async-start(bf16[8,128,512]{2,1,0:T(8,128)(2,1)} %pack.2), calls=%async_computation.2 | async-start | bytes 2097152 | tf_op jit(solution)/shard_map/all_to_all | solution.py:408
  63.9 17.7 %collective-permute-start.5 = (bf16[16,512]{1,0:T(8,128)(2,1)S(1)}, bf16[16,512]{1,0:T(8,128)(2,1)S(1)}, u32[]{:S(2)}, u32[]{:S(2)}) collective-permute-start(bf16[16,512]{1,0:T(8,128)(2,1)S(1)} %slice.9), channel_id=1, source_target_pairs={{32,0},{33,1},{34,2},{35,3},{36,4},{37,5},{38,6},{39,7},{40,8},{41... | collective-permute-start | bytes 49160 | tf_op jit(solution)/shard_map/ppermute | solution.py:413
  72.4 10.0 %collective-permute-start.4 = (bf16[16,512]{1,0:T(8,128)(2,1)S(1)}, bf16[16,512]{1,0:T(8,128)(2,1)S(1)}, u32[]{:S(2)}, u32[]{:S(2)}) collective-permute-start(bf16[16,512]{1,0:T(8,128)(2,1)S(1)} %slice.8), channel_id=1, source_target_pairs={{0,16},{1,17},{2,18},{3,19},{4,20},{5,21},{6,22},{7,23},{8,24},{9,... | collective-permute-start | bytes 49160 | tf_op jit(solution)/shard_map/ppermute | solution.py:413
  81.5 15.9 %copy-start.8 = (bf16[16,512]{1,0:T(8,128)(2,1)}, bf16[16,512]{1,0:T(8,128)(2,1)S(1)}, u32[]{:S(2)}) copy-start(bf16[16,512]{1,0:T(8,128)(2,1)S(1)} %collective-permute-done.5.x4_head) | copy-start | bytes 49156
  82.5 5.6 %copy-start.7 = (bf16[16,512]{1,0:T(8,128)(2,1)}, bf16[16,512]{1,0:T(8,128)(2,1)S(1)}, u32[]{:S(2)}) copy-start(bf16[16,512]{1,0:T(8,128)(2,1)S(1)} %collective-permute-done.4.f3_tail) | copy-start | bytes 49156
  82.5 5.6 %copy-start.3 = (bf16[8,128,512]{2,1,0:T(8,128)(2,1)}, bf16[8,128,512]{2,1,0:T(8,128)(2,1)S(1)}, u32[]{:S(2)}) copy-start(bf16[8,128,512]{2,1,0:T(8,128)(2,1)S(1)} %all-to-all-done.2) | copy-start | bytes 3145732
  82.8 27.3 %collective-permute-start.6 = (bf16[1024,512]{1,0:T(8,128)(2,1)}, bf16[1024,512]{1,0:T(8,128)(2,1)}, u32[]{:S(2)}, u32[]{:S(2)}) collective-permute-start(bf16[1024,512]{1,0:T(8,128)(2,1)} %collective-permute-done.2.x2), channel_id=1, source_target_pairs={{8,0},{9,1},{10,2},{11,3},{12,4},{13,5},{14,6},{15,7},{16,8},{17,9... | collective-permute-start | bytes 3145736 | tf_op jit(solution)/shard_map/ppermute | solution.py:413
  98.8 31.6 %all-to-all-start.3 = ((bf16[16,8,512]{2,1,0:T(8,128)(2,1)}), bf16[16,8,512]{2,1,0:T(8,128)(2,1)S(1)}, u32[]{:S(2)}, u32[]{:S(2)}) async-start(bf16[16,8,512]{2,1,0:T(8,128)(2,1)} %broadcast_in_dim.4), calls=%async_computation.3 | async-start | bytes 262144 | tf_op jit(solution)/shard_map/all_to_all | solution.py:439
  110.1 30.4 %collective-permute-start.7 = (bf16[1024,512]{1,0:T(8,128)(2,1)}, bf16[1024,512]{1,0:T(8,128)(2,1)S(1)}, u32[]{:S(2)}, u32[]{:S(2)}) collective-permute-start(bf16[1024,512]{1,0:T(8,128)(2,1)} %collective-permute-done.6.x3), channel_id=1, source_target_pairs={{8,0},{9,1},{10,2},{11,3},{12,4},{13,5},{14,6},{15,7},{16,8},{17,9... | collective-permute-start | bytes 3145736 | tf_op jit(solution)/shard_map/ppermute | solution.py:413
  126.1 14.5 %collective-permute-start.8 = (bf16[16,512]{1,0:T(8,128)(2,1)}, bf16[16,512]{1,0:T(8,128)(2,1)S(1)}, u32[]{:S(2)}, u32[]{:S(2)}) collective-permute-start(bf16[16,512]{1,0:T(8,128)(2,1)} %get-tuple-element.33), channel_id=1, source_target_pairs={{8,0},{9,1},{10,2},{11,3},{12,4},{13,5},{14,6},{15,7},{16,8},{17,9... | collective-permute-start | bytes 49160 | tf_op jit(solution)/shard_map/ppermute | solution.py:413
  131.1 7.4 %all-to-all-start.4 = ((f32[4,8,512]{2,1,0:T(8,128)}), f32[4,8,512]{2,1,0:T(8,128)S(1)}, u32[]{:S(2)}, u32[]{:S(2)}) async-start(f32[4,8,512]{2,1,0:T(8,128)} %broadcast_in_dim.5), calls=%async_computation.4 | async-start | bytes 131072 | tf_op jit(solution)/shard_map/all_to_all | solution.py:445
  140.6 0.6 copy-start.6
  140.6 1.0 copy-start.5
  147.1 22.1 %all-to-all-start.5 = ((bf16[8,144,512]{2,1,0:T(8,128)(2,1)}), bf16[8,144,512]{2,1,0:T(8,128)(2,1)S(1)}, u32[]{:S(2)}, u32[]{:S(2)}) async-start(bf16[8,144,512]{2,1,0:T(8,128)(2,1)} %finish.1), calls=%async_computation.5 | async-start | bytes 2359296 | tf_op jit(solution)/shard_map/all_to_all | solution.py:408

commit v5 on v4

--- a/solution.py
+++ b/solution.py
@@ -74,8 +74,11 @@
     return high, mid, (rest - mid.astype(F32)).astype(BF16)
 
 
-def prepare_kernel(lane, half_ref, scale_ref, raw, out_ref):
-    unscaled = raw[...] / scale_ref[0]
+def prepare_kernel(lane, half_ref, scale_ref, copies, out_ref):
+    total = copies[0]
+    for n in range(1, copies.shape[0]):
+        total = total + copies[n]
+    unscaled = jnp.concatenate([total[:8], total[8:]], axis=1) / scale_ref[0]
     norm = jnp.sum(unscaled * unscaled, keepdims=True)
     norm = split_terms(jnp.broadcast_to(norm, (8, 8)))
     span = PLANE * lane
@@ -90,15 +93,15 @@
         out_ref[p] = jnp.concatenate([tile, jnp.zeros_like(tile)], axis=0).astype(BF16)
 
 
-def prepare(half, scale, raw, lane):
+def prepare(half, scale, copies, lane):
     return pl.pallas_call(
         functools.partial(prepare_kernel, lane),
         in_specs=[pl.BlockSpec(memory_space=pltpu.SMEM)] * 2 + [pl.BlockSpec(memory_space=pltpu.VMEM)],
         out_shape=jax.ShapeDtypeStruct((PLANE, HEAD, GW), BF16),
         compiler_params=params(False),
-        cost_estimate=cost(raw.size, 4 * raw.size),
+        cost_estimate=cost(copies.size, 4 * copies.size),
         name="prepare",
-    )(half.reshape(1), scale, raw)
+    )(half.reshape(1), scale, copies)
 
 
 def unpack_kernel(lane, source_ref, got, out_ref, short_ref, norm_ref, tiles, sems):
@@ -267,7 +270,7 @@
 
 
 def terms_kernel(
-    width, acc, mid, x2, f0, f1, f2, f3_tail, tiles, raw_ref, pairs, far, feat_wide
+    width, acc, mid, x2, f0, f1, f2, f3_tail, tiles, raw_ref, pairs, far, feat_wide, two
 ):
     rows = x2.shape[0]
     fill_pairs(pairs, [x2])
@@ -279,13 +282,29 @@
     terms = correlate(far, f2[...], f3_tail[...], feat_wide, terms)
     out = [jnp.sum(t, axis=0, keepdims=True) for t in terms]
     out.append(jnp.zeros((8 - width, GW), F32))
-    raw_ref[...] = jnp.concatenate(out, axis=0)
-
-
-def all_terms(width, acc, mid, x2, f0, f1, f2, f3_tail, tiles):
+    out = jnp.concatenate(out, axis=0)
+    upper = pl.program_id(0) % 2 == 0
+
+    @pl.when(upper)
+    def _():
+        two[:8, :] = out
+
+    @pl.when(jnp.logical_not(upper))
+    def _():
+        two[8:, :] = out
+        packed = two[...].astype(BF16)
+        for n in range(raw_ref.shape[0]):
+            raw_ref[n] = packed
+
+
+def all_terms(width, planes, acc, mid, x2, f0, f1, f2, f3_tail, tiles):
     rows, own = acc.shape
     groups = own // GW
-    col = pl.BlockSpec((rows, GW), lambda g: (0, g))
+
+    def group(g):
+        return (g % 2) * (groups // 2) + g // 2
+
+    col = pl.BlockSpec((rows, GW), lambda g: (0, group(g)))
     return pl.pallas_call(
         functools.partial(terms_kernel, width),
         grid=(groups,),
@@ -296,15 +315,16 @@
             col,
             col,
             col,
-            pl.BlockSpec((HEAD, GW), lambda g: (0, g)),
-            pl.BlockSpec((1,) + tiles.shape[1:], lambda g: (g, 0, 0)),
-        ],
-        out_specs=pl.BlockSpec((8, GW), lambda g: (0, g)),
-        out_shape=jax.ShapeDtypeStruct((8, own), F32),
+            pl.BlockSpec((HEAD, GW), lambda g: (0, group(g))),
+            pl.BlockSpec((1,) + tiles.shape[1:], lambda g: (group(g), 0, 0)),
+        ],
+        out_specs=pl.BlockSpec((planes, 16, GW), lambda g: (0, 0, g // 2)),
+        out_shape=jax.ShapeDtypeStruct((planes, 16, own // 2), BF16),
         scratch_shapes=[
             pairs_of(rows),
             pltpu.VMEM((rows, GW), F32),
             pltpu.VMEM((rows + 8, GW), F32),
+            pltpu.VMEM((16, GW), F32),
         ],
         compiler_params=params(),
         cost_estimate=cost(16 * rows * rows * GW * groups, 20 * rows * own),
@@ -424,7 +444,7 @@
     feat1 = swap(pack(after(feat1, x0))).reshape(rows, own)
     feat0 = pack(after(features, x0))
     x1 = hop(x0, -1)
-    x1_next = after(x1, feat0, feat1, tiles)
+    x1_next = after(x1, feat0, feat1, tiles, taps)
     feat0 = swap(after(feat0, feat1)).reshape(rows, own)
     feat2 = hop(feat1, 1)
     feat3_tail = hop(feat1[rows - HEAD :], 2)
@@ -432,9 +452,8 @@
 
     acc, mid = early(x0, x1, tiles)
     x2 = after(hop(x1_next, -1), acc, feat0, feat2, feat3_tail, x4_head)
-    raw = all_terms(width, acc, mid, x2, feat0, feat1, feat2, feat3_tail, far_tiles)
+    copies = all_terms(width, planes, acc, mid, x2, feat0, feat1, feat2, feat3_tail, far_tiles)
     along_z = [[k * PLANE + i for k in range(planes)] for i in range(PLANE)]
-    copies = jnp.broadcast_to(raw.astype(BF16)[None], (planes,) + raw.shape)
     x3 = after(hop(x2, -1), copies)
     copies = lax.all_to_all(copies, "ctx", 0, 0, axis_index_groups=along_z, tiled=True)
     x4 = hop(x3, -1)
@@ -442,10 +461,10 @@
     raw = jnp.sum(after(copies, head).astype(F32), axis=0)
     next_head = hop(head, -1)
     copies = jnp.broadcast_to(raw[None], (lax.axis_size("dp"),) + raw.shape)
-    raw = jnp.sum(lax.all_to_all(copies, "dp", 0, 0, tiled=True), axis=0)
+    copies = lax.all_to_all(copies, "dp", 0, 0, tiled=True)
     lane = chans // shards
     spans = own // lane // PLANE
-    extra = prepare(z % spans, loss_scale, raw, lane)
+    extra = prepare(z % spans, loss_scale, copies, lane)
     got = swap(finish(width, acc, x4, far_tiles, next_head, taps, extra))
     input_grad, short_grad, norm_value = unpack(z // spans, got, rows // PLANE, width, lane)
     return (input_grad, short_grad, norm_value.reshape(1))

time: 172 us -> 170 us (0.988)
  the two profiles are of different devices: /device:TPU:480 before, /device:TPU:32 now
where the time goes in v5:
time: 170 us; the launch traced here: 169 us
  starting transfers between devices  59.9 us (35%)
  Pallas kernels  47.5 us (28%)
  waiting for transfers between devices  30.5 us (18%)
  blocking collectives  23.8 us (14%)
  local copies, waits for them, and re-layouts  4.52 us (3%)
    ppermute x9, starting transfers between devices, hop(): return lax.ppermute(x, 'ctx', route)  30.6 us
    all_to_all x1, blocking collectives, swap(): lax.all_to_all(x, 'ctx', 0, 0, axis_index_groups=in_plane, tiled=True)  23.8 us
    all_to_all x3, waiting for transfers between devices, swap(): lax.all_to_all(x, 'ctx', 0, 0, axis_index_groups=in_plane, tiled=True)  18.7 us
    all_to_all x3, starting transfers between devices, swap(): lax.all_to_all(x, 'ctx', 0, 0, axis_index_groups=in_plane, tiled=True)  13.3 us
    all_to_all x1, starting transfers between devices, per_device(): lax.all_to_all(copies, 'ctx', 0, 0, axis_index_groups=along_z, tiled=True)  12.7 us
    pallas_call x1, Pallas kernels, all_terms(): pl.pallas_call(functools.partial(terms_kernel, width), grid=(groups,), in...  9.52 us
    ppermute x9, waiting for transfers between devices, hop(): return lax.ppermute(x, 'ctx', route)  8.34 us
    pallas_call x1, Pallas kernels, third(): pl.pallas_call(third_kernel, grid=(groups,), in_specs=[col, col, col, pl....  8.04 us
  transfers between devices with their start and end apart: 14, of which 7 were waited for; matrix products, arithmetic and copies ran while one was open for 2% of the time, Pallas kernels for 24%

profile of v5, /device:TPU:32, one launch (start us, length us, event | category | flops | bytes accessed | tf_op | source)
XLA Modules:
  0.0 168.7 jit_solution(11309318584207197853)
XLA Ops:
  0.6 4.0 %collective-permute-start.1 = (bf16[1,128,4096]{2,1,0:T(8,128)(2,1)}, bf16[1,128,4096]{2,1,0:T(8,128)(2,1)S(1)}, u32[]{:S(2)}, u32[]{:S(2)}) collective-permute-start(bf16[1,128,4096]{2,1,0:T(8,128)(2,1)} %src_ref), channel_id=1, source_target_pairs={{0,8},{1,9},{2,10},{3,11},{4,12},{5,13},{6,14},{7,15},{8,16},{9,17... | collective-permute-start | bytes 3145736 | tf_op jit(solution)/shard_map/ppermute | solution.py:433
  4.6 2.8 %gate.1 = bf16[8,128,512]{2,1,0:T(8,128)(2,1)} custom-call(bf16[1,128,4096]{2,1,0:T(8,128)(2,1)} %up_ref.1, bf16[1,128,4096]{2,1,0:T(8,128)(2,1)} %gate_ref.1), custom_call_target="tpu_custom_call" | custom-call | flops 8192 | bytes 49152 | tf_op jit(solution)/shard_map/gate/pallas_call | solution.py:44
  7.4 23.8 %all_to_all.30 = bf16[8,128,512]{2,1,0:T(8,128)(2,1)S(1)} all-to-all(bf16[8,128,512]{2,1,0:T(8,128)(2,1)} %gate.1), channel_id=1, replica_groups={{0,1,2,3,4,5,6,7},{8,9,10,11,12,13,14,15},{16,17,18,19,20,21,22,23},{24..., dimensions={0} | all-to-all | bytes 2097152 | tf_op jit(solution)/shard_map/all_to_all | solution.py:428
  31.2 2.1 %collective-permute-start = (bf16[1024,512]{1,0:T(8,128)(2,1)S(1)}, bf16[1024,512]{1,0:T(8,128)(2,1)}, u32[]{:S(2)}, u32[]{:S(2)}) collective-permute-start(bf16[1024,512]{1,0:T(8,128)(2,1)S(1)} %bitcast.9), channel_id=1, source_target_pairs={{8,0},{9,1},{10,2},{11,3},{12,4},{13,5},{14,6},{15,7},{16,8},{17,9... | collective-permute-start | bytes 3145736 | tf_op jit(solution)/shard_map/ppermute | solution.py:433
  33.3 1.0 copy-done.4
  34.2 2.3 %pack.3 = bf16[8,128,512]{2,1,0:T(8,128)(2,1)} custom-call(bf16[1,128,4096]{2,1,0:T(8,128)(2,1)} %copy-done.4), custom_call_target="tpu_custom_call" | custom-call | bytes 32768 | tf_op jit(solution)/shard_map/pack/pallas_call | solution.py:61
  36.5 3.6 %all-to-all-start.1 = ((bf16[8,128,512]{2,1,0:T(8,128)(2,1)}), bf16[8,128,512]{2,1,0:T(8,128)(2,1)S(1)}, u32[]{:S(2)}, u32[]{:S(2)}) async-start(bf16[8,128,512]{2,1,0:T(8,128)(2,1)} %pack.3), calls=%async_computation.1 | async-start | bytes 2097152 | tf_op jit(solution)/shard_map/all_to_all | solution.py:428
  41.6 6.0 %toeplitz.1 = (bf16[4,256,4352]{2,1,0:T(8,128)(2,1)}, bf16[4,256,2048]{2,1,0:T(8,128)(2,1)}) custom-call(f32[4,1,4096]{2,1,0:T(1,128)} %reshape.39.taps_ref), custom_call_target="tpu_custom_call" | custom-call | flops 1048576 | bytes 393216 | tf_op jit(solution)/shard_map/toeplitz/pallas_call | solution.py:174
  48.3 2.3 %pack.2 = bf16[8,128,512]{2,1,0:T(8,128)(2,1)} custom-call(bf16[1,128,4096]{2,1,0:T(8,128)(2,1)} %src_ref), custom_call_target="tpu_custom_call" | custom-call | bytes 32768 | tf_op jit(solution)/shard_map/pack/pallas_call | solution.py:61
  50.6 3.5 %all-to-all-done.1 = bf16[8,128,512]{2,1,0:T(8,128)(2,1)S(1)} async-done(((bf16[8,128,512]{2,1,0:T(8,128)(2,1)}), bf16[8,128,512]{2,1,0:T(8,128)(2,1)S(1)}, u32[]{:S(2)}, u32[]{:S(2)}) %all-to-all-start.1) | async-done | bytes 1048608 | tf_op jit(solution)/shard_map/all_to_all | solution.py:428
  54.1 2.0 %collective-permute-done.x1 = bf16[1024,512]{1,0:T(8,128)(2,1)} collective-permute-done((bf16[1024,512]{1,0:T(8,128)(2,1)S(1)}, bf16[1024,512]{1,0:T(8,128)(2,1)}, u32[]{:S(2)}, u32[]{:S(2)}) %collective-permute-start) | collective-permute-done | bytes 1048608 | tf_op jit(solution)/shard_map/ppermute | solution.py:433
  56.1 2.0 %collective-permute-start.2 = (bf16[1024,512]{1,0:T(8,128)(2,1)}, bf16[1024,512]{1,0:T(8,128)(2,1)}, u32[]{:S(2)}, u32[]{:S(2)}) collective-permute-start(bf16[1024,512]{1,0:T(8,128)(2,1)} %collective-permute-done.x1), channel_id=1, source_target_pairs={{8,0},{9,1},{10,2},{11,3},{12,4},{13,5},{14,6},{15,7},{16,8},{17,9... | collective-permute-start | bytes 3145736 | tf_op jit(solution)/shard_map/ppermute | solution.py:433
  58.1 4.9 %collective-permute-start.3 = (bf16[1024,512]{1,0:T(8,128)(2,1)S(1)}, bf16[1024,512]{1,0:T(8,128)(2,1)}, u32[]{:S(2)}, u32[]{:S(2)}) collective-permute-start(bf16[1024,512]{1,0:T(8,128)(2,1)S(1)} %bitcast.6), channel_id=1, source_target_pairs={{0,8},{1,9},{2,10},{3,11},{4,12},{5,13},{6,14},{7,15},{8,16},{9,17... | collective-permute-start | bytes 3145736 | tf_op jit(solution)/shard_map/ppermute | solution.py:433
  63.1 3.6 %all-to-all-start.2 = ((bf16[8,128,512]{2,1,0:T(8,128)(2,1)}), bf16[8,128,512]{2,1,0:T(8,128)(2,1)S(1)}, u32[]{:S(2)}, u32[]{:S(2)}) async-start(bf16[8,128,512]{2,1,0:T(8,128)(2,1)} %pack.2), calls=%async_computation.2 | async-start | bytes 2097152 | tf_op jit(solution)/shard_map/all_to_all | solution.py:428
  66.7 1.3 collective-permute-start.5
  68.0 7.5 %collective-permute-start.4 = (bf16[16,512]{1,0:T(8,128)(2,1)S(1)}, bf16[16,512]{1,0:T(8,128)(2,1)S(1)}, u32[]{:S(2)}, u32[]{:S(2)}) collective-permute-start(bf16[16,512]{1,0:T(8,128)(2,1)S(1)} %slice.8), channel_id=1, source_target_pairs={{0,16},{1,17},{2,18},{3,19},{4,20},{5,21},{6,22},{7,23},{8,24},{9,... | collective-permute-start | bytes 49160 | tf_op jit(solution)/shard_map/ppermute | solution.py:433
  75.6 7.8 %early.1 = (f32[1024,512]{1,0:T(8,128)}, f32[1024,512]{1,0:T(8,128)}) custom-call(bf16[1024,512]{1,0:T(8,128)(2,1)} %bitcast.11, bf16[1024,512]{1,0:T(8,128)(2,1)} %collective-permute-done.x1, bf16[4,256,4352]{2,1,0:T(8,128)(2,1)} %get-tuple-element.22.tiles), custom_call_target="tpu_custom_call" | custom-call | flops 201326592 | bytes 98304 | tf_op jit(solution)/shard_map/early/pallas_call | solution.py:259
  83.4 2.9 %collective-permute-done.5.x4_head = bf16[16,512]{1,0:T(8,128)(2,1)S(1)} collective-permute-done((bf16[16,512]{1,0:T(8,128)(2,1)S(1)}, bf16[16,512]{1,0:T(8,128)(2,1)S(1)}, u32[]{:S(2)}, u32[]{:S(2)}) %collective-permute-start.5) | collective-permute-done | bytes 16416 | tf_op jit(solution)/shard_map/ppermute | solution.py:433
  86.4 4.4 %collective-permute-start.6 = (bf16[1024,512]{1,0:T(8,128)(2,1)}, bf16[1024,512]{1,0:T(8,128)(2,1)}, u32[]{:S(2)}, u32[]{:S(2)}) collective-permute-start(bf16[1024,512]{1,0:T(8,128)(2,1)} %collective-permute-done.2.x2), channel_id=1, source_target_pairs={{8,0},{9,1},{10,2},{11,3},{12,4},{13,5},{14,6},{15,7},{16,8},{17,9... | collective-permute-start | bytes 3145736 | tf_op jit(solution)/shard_map/ppermute | solution.py:433
  90.8 9.5 %all_terms.1 = bf16[16,16,256]{2,1,0:T(8,128)(2,1)} custom-call(f32[1024,512]{1,0:T(8,128)} %get-tuple-element.23.acc.acc_in, f32[1024,512]{1,0:T(8,128)} %get-tuple-element.30.mid, bf16[1024,512]{1,0:T(8,128)(2,1)} %collective-permute-done.2.x2, bf16[1024,512]{1,0:T(8,128)(2,1)} %bitcast.12, bf16[1024,512]{1,0:T(8,128)(2,1)} %bitcast.8, ...), custom_call_target="tpu_custom_call" | custom-call | flops 134217728 | bytes 163840 | tf_op jit(solution)/shard_map/all_terms/pallas_call | solution.py:308
  100.3 12.7 %all-to-all-start.3 = ((bf16[16,16,256]{2,1,0:T(8,128)(2,1)}), bf16[16,16,256]{2,1,0:T(8,128)(2,1)S(1)}, u32[]{:S(2)}, u32[]{:S(2)}) async-start(bf16[16,16,256]{2,1,0:T(8,128)(2,1)} %all_terms.1), calls=%async_computation.3 | async-start | bytes 262144 | tf_op jit(solution)/shard_map/all_to_all | solution.py:458
  113.0 2.0 %collective-permute-start.7 = (bf16[1024,512]{1,0:T(8,128)(2,1)}, bf16[1024,512]{1,0:T(8,128)(2,1)S(1)}, u32[]{:S(2)}, u32[]{:S(2)}) collective-permute-start(bf16[1024,512]{1,0:T(8,128)(2,1)} %collective-permute-done.6.x3), channel_id=1, source_target_pairs={{8,0},{9,1},{10,2},{11,3},{12,4},{13,5},{14,6},{15,7},{16,8},{17,9... | collective-permute-start | bytes 3145736 | tf_op jit(solution)/shard_map/ppermute | solution.py:433
  115.0 8.0 %third.1 = (f32[1024,512]{1,0:T(8,128)}, bf16[16,512]{1,0:T(8,128)(2,1)}) custom-call(f32[1024,512]{1,0:T(8,128)} %get-tuple-element.23.acc.acc_in, bf16[1024,512]{1,0:T(8,128)(2,1)} %collective-permute-done.2.x2, bf16[1024,512]{1,0:T(8,128)(2,1)} %collective-permute-done.6.x3, bf16[16,512]{1,0:T(8,128)(2,1)} %copy-done.9, ...), custom_call_target="tpu_custom_call" | custom-call | flops 38654705664 | bytes 25165824 | tf_op jit(solution)/shard_map/third/pallas_call | solution.py:348
  123.1 2.6 %all-to-all-done.3 = bf16[16,16,256]{2,1,0:T(8,128)(2,1)S(1)} async-done(((bf16[16,16,256]{2,1,0:T(8,128)(2,1)}), bf16[16,16,256]{2,1,0:T(8,128)(2,1)S(1)}, u32[]{:S(2)}, u32[]{:S(2)}) %all-to-all-start.3) | async-done | bytes 131104 | tf_op jit(solution)/shard_map/all_to_all | solution.py:458
  126.3 3.3 %all-to-all-start.4 = ((f32[4,16,256]{2,1,0:T(8,128)}), f32[4,16,256]{2,1,0:T(8,128)S(1)}, u32[]{:S(2)}, u32[]{:S(2)}) async-start(f32[4,16,256]{2,1,0:T(8,128)} %broadcast_in_dim.2), calls=%async_computation.4 | async-start | bytes 131072 | tf_op jit(solution)/shard_map/all_to_all | solution.py:464
  129.6 2.4 %collective-permute-start.8 = (bf16[16,512]{1,0:T(8,128)(2,1)}, bf16[16,512]{1,0:T(8,128)(2,1)S(1)}, u32[]{:S(2)}, u32[]{:S(2)}) collective-permute-start(bf16[16,512]{1,0:T(8,128)(2,1)} %get-tuple-element.34), channel_id=1, source_target_pairs={{8,0},{9,1},{10,2},{11,3},{12,4},{13,5},{14,6},{15,7},{16,8},{17,9... | collective-permute-start | bytes 49160 | tf_op jit(solution)/shard_map/ppermute | solution.py:433
  134.3 1.6 prepare.1.extra
  135.9 3.4 %collective-permute-done.8.next_head = bf16[16,512]{1,0:T(8,128)(2,1)S(1)} collective-permute-done((bf16[16,512]{1,0:T(8,128)(2,1)}, bf16[16,512]{1,0:T(8,128)(2,1)S(1)}, u32[]{:S(2)}, u32[]{:S(2)}) %collective-permute-start.8) | collective-permute-done | bytes 16416 | tf_op jit(solution)/shard_map/ppermute | solution.py:433
  140.3 5.6 %finish.1 = bf16[8,144,512]{2,1,0:T(8,128)(2,1)} custom-call(f32[1024,512]{1,0:T(8,128)} %get-tuple-element.33.acc_in, bf16[1024,512]{1,0:T(8,128)(2,1)} %copy-done.5, bf16[4,256,2048]{2,1,0:T(8,128)(2,1)} %get-tuple-element.31.tiles, bf16[16,512]{1,0:T(8,128)(2,1)} %copy-done.7, f32[7,512]{1,0:T(8,128)} %constant_dynamic-slice_fusion.taps, ...), custom_call_target="tpu_custom_call" | custom-call | flops 50331648 | bytes 65536 | tf_op jit(solution)/shard_map/finish/pallas_call | solution.py:393
  145.9 6.1 %all-to-all-start.5 = ((bf16[8,144,512]{2,1,0:T(8,128)(2,1)}), bf16[8,144,512]{2,1,0:T(8,128)(2,1)S(1)}, u32[]{:S(2)}, u32[]{:S(2)}) async-start(bf16[8,144,512]{2,1,0:T(8,128)(2,1)} %finish.1), calls=%async_computation.5 | async-start | bytes 2359296 | tf_op jit(solution)/shard_map/all_to_all | solution.py:428
  151.9 15.1 %all-to-all-done.5.got = bf16[8,144,512]{2,1,0:T(8,128)(2,1)S(1)} async-done(((bf16[8,144,512]{2,1,0:T(8,128)(2,1)}), bf16[8,144,512]{2,1,0:T(8,128)(2,1)S(1)}, u32[]{:S(2)}, u32[]{:S(2)}) %all-to-all-start.5) | async-done | bytes 1179680 | tf_op jit(solution)/shard_map/all_to_all | solution.py:428
  167.1 1.6 unpack.1
  (34 shorter events, 5.4 us)
Async XLA Ops:
  0.6 47.0 %copy-start = (f32[7,4096]{1,0:T(8,128)S(1)}, f32[7,4096]{1,0:T(8,128)}, u32[]{:S(2)}) copy-start(f32[7,4096]{1,0:T(8,128)} %param.9) | copy-start | bytes 344068
  0.6 32.6 %collective-permute-start.1 = (bf16[1,128,4096]{2,1,0:T(8,128)(2,1)}, bf16[1,128,4096]{2,1,0:T(8,128)(2,1)S(1)}, u32[]{:S(2)}, u32[]{:S(2)}) collective-permute-start(bf16[1,128,4096]{2,1,0:T(8,128)(2,1)} %src_ref), channel_id=1, source_target_pairs={{0,8},{1,9},{2,10},{3,11},{4,12},{5,13},{6,14},{7,15},{8,16},{9,17... | collective-permute-start | bytes 3145736 | tf_op jit(solution)/shard_map/ppermute | solution.py:433
  31.2 35.6 %copy-start.2 = (bf16[8,128,512]{2,1,0:T(8,128)(2,1)}, bf16[8,128,512]{2,1,0:T(8,128)(2,1)S(1)}, u32[]{:S(2)}) copy-start(bf16[8,128,512]{2,1,0:T(8,128)(2,1)S(1)} %all_to_all.30) | copy-start | bytes 3145732
  31.2 24.9 %collective-permute-start = (bf16[1024,512]{1,0:T(8,128)(2,1)S(1)}, bf16[1024,512]{1,0:T(8,128)(2,1)}, u32[]{:S(2)}, u32[]{:S(2)}) collective-permute-start(bf16[1024,512]{1,0:T(8,128)(2,1)S(1)} %bitcast.9), channel_id=1, source_target_pairs={{8,0},{9,1},{10,2},{11,3},{12,4},{13,5},{14,6},{15,7},{16,8},{17,9... | collective-permute-start | bytes 3145736 | tf_op jit(solution)/shard_map/ppermute | solution.py:433
  33.2 1.0 copy-start.4
  36.5 17.6 %all-to-all-start.1 = ((bf16[8,128,512]{2,1,0:T(8,128)(2,1)}), bf16[8,128,512]{2,1,0:T(8,128)(2,1)S(1)}, u32[]{:S(2)}, u32[]{:S(2)}) async-start(bf16[8,128,512]{2,1,0:T(8,128)(2,1)} %pack.3), calls=%async_computation.1 | async-start | bytes 2097152 | tf_op jit(solution)/shard_map/all_to_all | solution.py:428
  54.1 29.3 %copy-start.1 = (bf16[8,128,512]{2,1,0:T(8,128)(2,1)}, bf16[8,128,512]{2,1,0:T(8,128)(2,1)S(1)}, u32[]{:S(2)}) copy-start(bf16[8,128,512]{2,1,0:T(8,128)(2,1)S(1)} %all-to-all-done.1) | copy-start | bytes 3145732
  56.1 30.2 %collective-permute-start.2 = (bf16[1024,512]{1,0:T(8,128)(2,1)}, bf16[1024,512]{1,0:T(8,128)(2,1)}, u32[]{:S(2)}, u32[]{:S(2)}) collective-permute-start(bf16[1024,512]{1,0:T(8,128)(2,1)} %collective-permute-done.x1), channel_id=1, source_target_pairs={{8,0},{9,1},{10,2},{11,3},{12,4},{13,5},{14,6},{15,7},{16,8},{17,9... | collective-permute-start | bytes 3145736 | tf_op jit(solution)/shard_map/ppermute | solution.py:433
  58.1 28.2 %collective-permute-start.3 = (bf16[1024,512]{1,0:T(8,128)(2,1)S(1)}, bf16[1024,512]{1,0:T(8,128)(2,1)}, u32[]{:S(2)}, u32[]{:S(2)}) collective-permute-start(bf16[1024,512]{1,0:T(8,128)(2,1)S(1)} %bitcast.6), channel_id=1, source_target_pairs={{0,8},{1,9},{2,10},{3,11},{4,12},{5,13},{6,14},{7,15},{8,16},{9,17... | collective-permute-start | bytes 3145736 | tf_op jit(solution)/shard_map/ppermute | solution.py:433
  63.1 23.3 %all-to-all-start.2 = ((bf16[8,128,512]{2,1,0:T(8,128)(2,1)}), bf16[8,128,512]{2,1,0:T(8,128)(2,1)S(1)}, u32[]{:S(2)}, u32[]{:S(2)}) async-start(bf16[8,128,512]{2,1,0:T(8,128)(2,1)} %pack.2), calls=%async_computation.2 | async-start | bytes 2097152 | tf_op jit(solution)/shard_map/all_to_all | solution.py:428
  66.7 19.6 %collective-permute-start.5 = (bf16[16,512]{1,0:T(8,128)(2,1)S(1)}, bf16[16,512]{1,0:T(8,128)(2,1)S(1)}, u32[]{:S(2)}, u32[]{:S(2)}) collective-permute-start(bf16[16,512]{1,0:T(8,128)(2,1)S(1)} %slice.9), channel_id=1, source_target_pairs={{32,0},{33,1},{34,2},{35,3},{36,4},{37,5},{38,6},{39,7},{40,8},{41... | collective-permute-start | bytes 49160 | tf_op jit(solution)/shard_map/ppermute | solution.py:433
  68.0 18.3 %collective-permute-start.4 = (bf16[16,512]{1,0:T(8,128)(2,1)S(1)}, bf16[16,512]{1,0:T(8,128)(2,1)S(1)}, u32[]{:S(2)}, u32[]{:S(2)}) collective-permute-start(bf16[16,512]{1,0:T(8,128)(2,1)S(1)} %slice.8), channel_id=1, source_target_pairs={{0,16},{1,17},{2,18},{3,19},{4,20},{5,21},{6,22},{7,23},{8,24},{9,... | collective-permute-start | bytes 49160 | tf_op jit(solution)/shard_map/ppermute | solution.py:433
  86.3 14.0 %copy-start.9 = (bf16[16,512]{1,0:T(8,128)(2,1)}, bf16[16,512]{1,0:T(8,128)(2,1)S(1)}, u32[]{:S(2)}) copy-start(bf16[16,512]{1,0:T(8,128)(2,1)S(1)} %collective-permute-done.5.x4_head) | copy-start | bytes 49156
  86.3 4.5 %copy-start.8 = (bf16[16,512]{1,0:T(8,128)(2,1)}, bf16[16,512]{1,0:T(8,128)(2,1)S(1)}, u32[]{:S(2)}) copy-start(bf16[16,512]{1,0:T(8,128)(2,1)S(1)} %collective-permute-done.4.f3_tail) | copy-start | bytes 49156
  86.3 4.5 %copy-start.3 = (bf16[8,128,512]{2,1,0:T(8,128)(2,1)}, bf16[8,128,512]{2,1,0:T(8,128)(2,1)S(1)}, u32[]{:S(2)}) copy-start(bf16[8,128,512]{2,1,0:T(8,128)(2,1)S(1)} %all-to-all-done.2) | copy-start | bytes 3145732
  86.4 26.6 %collective-permute-start.6 = (bf16[1024,512]{1,0:T(8,128)(2,1)}, bf16[1024,512]{1,0:T(8,128)(2,1)}, u32[]{:S(2)}, u32[]{:S(2)}) collective-permute-start(bf16[1024,512]{1,0:T(8,128)(2,1)} %collective-permute-done.2.x2), channel_id=1, source_target_pairs={{8,0},{9,1},{10,2},{11,3},{12,4},{13,5},{14,6},{15,7},{16,8},{17,9... | collective-permute-start | bytes 3145736 | tf_op jit(solution)/shard_map/ppermute | solution.py:433
  100.3 25.3 %all-to-all-start.3 = ((bf16[16,16,256]{2,1,0:T(8,128)(2,1)}), bf16[16,16,256]{2,1,0:T(8,128)(2,1)S(1)}, u32[]{:S(2)}, u32[]{:S(2)}) async-start(bf16[16,16,256]{2,1,0:T(8,128)(2,1)} %all_terms.1), calls=%async_computation.3 | async-start | bytes 262144 | tf_op jit(solution)/shard_map/all_to_all | solution.py:458
  113.0 26.3 %collective-permute-start.7 = (bf16[1024,512]{1,0:T(8,128)(2,1)}, bf16[1024,512]{1,0:T(8,128)(2,1)S(1)}, u32[]{:S(2)}, u32[]{:S(2)}) collective-permute-start(bf16[1024,512]{1,0:T(8,128)(2,1)} %collective-permute-done.6.x3), channel_id=1, source_target_pairs={{8,0},{9,1},{10,2},{11,3},{12,4},{13,5},{14,6},{15,7},{16,8},{17,9... | collective-permute-start | bytes 3145736 | tf_op jit(solution)/shard_map/ppermute | solution.py:433
  126.3 7.4 %all-to-all-start.4 = ((f32[4,16,256]{2,1,0:T(8,128)}), f32[4,16,256]{2,1,0:T(8,128)S(1)}, u32[]{:S(2)}, u32[]{:S(2)}) async-start(f32[4,16,256]{2,1,0:T(8,128)} %broadcast_in_dim.2), calls=%async_computation.4 | async-start | bytes 131072 | tf_op jit(solution)/shard_map/all_to_all | solution.py:464
  129.6 9.7 %collective-permute-start.8 = (bf16[16,512]{1,0:T(8,128)(2,1)}, bf16[16,512]{1,0:T(8,128)(2,1)S(1)}, u32[]{:S(2)}, u32[]{:S(2)}) collective-permute-start(bf16[16,512]{1,0:T(8,128)(2,1)} %get-tuple-element.34), channel_id=1, source_target_pairs={{8,0},{9,1},{10,2},{11,3},{12,4},{13,5},{14,6},{15,7},{16,8},{17,9... | collective-permute-start | bytes 49160 | tf_op jit(solution)/shard_map/ppermute | solution.py:433
  133.7 0.6 copy-start.6
  139.3 0.6 copy-start.7
  139.3 1.0 copy-start.5
  145.9 21.2 %all-to-all-start.5 = ((bf16[8,144,512]{2,1,0:T(8,128)(2,1)}), bf16[8,144,512]{2,1,0:T(8,128)(2,1)S(1)}, u32[]{:S(2)}, u32[]{:S(2)}) async-start(bf16[8,144,512]{2,1,0:T(8,128)(2,1)} %finish.1), calls=%async_computation.5 | async-start | bytes 2359296 | tf_op jit(solution)/shard_map/all_to_all | solution.py:428

commit v6 on v5

--- a/solution.py
+++ b/solution.py
@@ -247,8 +247,9 @@
     last = tiles.shape[2] // BLK - 1
     fill_pairs(pairs, [x0, x1])
     store_rows(acc_ref, tile_products(tiles, 0, last, pairs, 0, 8))
-    fill_pairs(pairs, [x1])
-    store_rows(mid_ref, tile_products(tiles, 0, last, pairs, 8, 4))
+    pairs[4 * BLK : 5 * BLK, :GW] = jnp.zeros((BLK, GW), BF16)
+    behind = pairs.at[pl.ds(4 * BLK, 5 * BLK)]
+    store_rows(mid_ref, tile_products(tiles, 0, last, behind, 8, 4))
 
 
 def early(x0, x1, tiles):

time: 170 us -> 170 us (level)
  no operation moved by 1% of the time
where the time goes in v6:
time: 170 us; the launch traced here: 169 us
  starting transfers between devices  59.9 us (35%)
  Pallas kernels  47.3 us (28%)
  waiting for transfers between devices  30.8 us (18%)
  blocking collectives  23.8 us (14%)
  local copies, waits for them, and re-layouts  4.52 us (3%)
    ppermute x9, starting transfers between devices, hop(): return lax.ppermute(x, 'ctx', route)  30.6 us
    all_to_all x1, blocking collectives, swap(): lax.all_to_all(x, 'ctx', 0, 0, axis_index_groups=in_plane, tiled=True)  23.8 us
    all_to_all x3, waiting for transfers between devices, swap(): lax.all_to_all(x, 'ctx', 0, 0, axis_index_groups=in_plane, tiled=True)  18.7 us
    all_to_all x3, starting transfers between devices, swap(): lax.all_to_all(x, 'ctx', 0, 0, axis_index_groups=in_plane, tiled=True)  13.3 us
    all_to_all x1, starting transfers between devices, per_device(): lax.all_to_all(copies, 'ctx', 0, 0, axis_index_groups=along_z, tiled=True)  12.7 us
    pallas_call x1, Pallas kernels, all_terms(): pl.pallas_call(functools.partial(terms_kernel, width), grid=(groups,), in...  9.52 us
    ppermute x9, waiting for transfers between devices, hop(): return lax.ppermute(x, 'ctx', route)  8.58 us
    pallas_call x1, Pallas kernels, third(): pl.pallas_call(third_kernel, grid=(groups,), in_specs=[col, col, col, pl....  8.04 us
  transfers between devices with their start and end apart: 14, of which 7 were waited for; matrix products, arithmetic and copies ran while one was open for 2% of the time, Pallas kernels for 24%

profile of v6, /device:TPU:32, one launch (start us, length us, event | category | flops | bytes accessed | tf_op | source)
XLA Modules:
  0.0 168.7 jit_solution(16461607869233391431)
XLA Ops:
  0.6 4.0 %collective-permute-start.1 = (bf16[1,128,4096]{2,1,0:T(8,128)(2,1)}, bf16[1,128,4096]{2,1,0:T(8,128)(2,1)S(1)}, u32[]{:S(2)}, u32[]{:S(2)}) collective-permute-start(bf16[1,128,4096]{2,1,0:T(8,128)(2,1)} %src_ref), channel_id=1, source_target_pairs={{0,8},{1,9},{2,10},{3,11},{4,12},{5,13},{6,14},{7,15},{8,16},{9,17... | collective-permute-start | bytes 3145736 | tf_op jit(solution)/shard_map/ppermute | solution.py:434
  4.6 2.8 %gate.1 = bf16[8,128,512]{2,1,0:T(8,128)(2,1)} custom-call(bf16[1,128,4096]{2,1,0:T(8,128)(2,1)} %up_ref.1, bf16[1,128,4096]{2,1,0:T(8,128)(2,1)} %gate_ref.1), custom_call_target="tpu_custom_call" | custom-call | flops 8192 | bytes 49152 | tf_op jit(solution)/shard_map/gate/pallas_call | solution.py:44
  7.4 23.8 %all_to_all.30 = bf16[8,128,512]{2,1,0:T(8,128)(2,1)S(1)} all-to-all(bf16[8,128,512]{2,1,0:T(8,128)(2,1)} %gate.1), channel_id=1, replica_groups={{0,1,2,3,4,5,6,7},{8,9,10,11,12,13,14,15},{16,17,18,19,20,21,22,23},{24..., dimensions={0} | all-to-all | bytes 2097152 | tf_op jit(solution)/shard_map/all_to_all | solution.py:429
  31.2 2.1 %collective-permute-start = (bf16[1024,512]{1,0:T(8,128)(2,1)S(1)}, bf16[1024,512]{1,0:T(8,128)(2,1)}, u32[]{:S(2)}, u32[]{:S(2)}) collective-permute-start(bf16[1024,512]{1,0:T(8,128)(2,1)S(1)} %bitcast.9), channel_id=1, source_target_pairs={{8,0},{9,1},{10,2},{11,3},{12,4},{13,5},{14,6},{15,7},{16,8},{17,9... | collective-permute-start | bytes 3145736 | tf_op jit(solution)/shard_map/ppermute | solution.py:434
  33.3 1.0 copy-done.4
  34.2 2.3 %pack.3 = bf16[8,128,512]{2,1,0:T(8,128)(2,1)} custom-call(bf16[1,128,4096]{2,1,0:T(8,128)(2,1)} %copy-done.4), custom_call_target="tpu_custom_call" | custom-call | bytes 32768 | tf_op jit(solution)/shard_map/pack/pallas_call | solution.py:61
  36.5 3.6 %all-to-all-start.1 = ((bf16[8,128,512]{2,1,0:T(8,128)(2,1)}), bf16[8,128,512]{2,1,0:T(8,128)(2,1)S(1)}, u32[]{:S(2)}, u32[]{:S(2)}) async-start(bf16[8,128,512]{2,1,0:T(8,128)(2,1)} %pack.3), calls=%async_computation.1 | async-start | bytes 2097152 | tf_op jit(solution)/shard_map/all_to_all | solution.py:429
  41.6 6.0 %toeplitz.1 = (bf16[4,256,4352]{2,1,0:T(8,128)(2,1)}, bf16[4,256,2048]{2,1,0:T(8,128)(2,1)}) custom-call(f32[4,1,4096]{2,1,0:T(1,128)} %reshape.39.taps_ref), custom_call_target="tpu_custom_call" | custom-call | flops 1048576 | bytes 393216 | tf_op jit(solution)/shard_map/toeplitz/pallas_call | solution.py:174
  48.3 2.3 %pack.2 = bf16[8,128,512]{2,1,0:T(8,128)(2,1)} custom-call(bf16[1,128,4096]{2,1,0:T(8,128)(2,1)} %src_ref), custom_call_target="tpu_custom_call" | custom-call | bytes 32768 | tf_op jit(solution)/shard_map/pack/pallas_call | solution.py:61
  50.6 3.5 %all-to-all-done.1 = bf16[8,128,512]{2,1,0:T(8,128)(2,1)S(1)} async-done(((bf16[8,128,512]{2,1,0:T(8,128)(2,1)}), bf16[8,128,512]{2,1,0:T(8,128)(2,1)S(1)}, u32[]{:S(2)}, u32[]{:S(2)}) %all-to-all-start.1) | async-done | bytes 1048608 | tf_op jit(solution)/shard_map/all_to_all | solution.py:429
  54.1 2.0 %collective-permute-done.x1 = bf16[1024,512]{1,0:T(8,128)(2,1)} collective-permute-done((bf16[1024,512]{1,0:T(8,128)(2,1)S(1)}, bf16[1024,512]{1,0:T(8,128)(2,1)}, u32[]{:S(2)}, u32[]{:S(2)}) %collective-permute-start) | collective-permute-done | bytes 1048608 | tf_op jit(solution)/shard_map/ppermute | solution.py:434
  56.1 2.0 %collective-permute-start.2 = (bf16[1024,512]{1,0:T(8,128)(2,1)}, bf16[1024,512]{1,0:T(8,128)(2,1)}, u32[]{:S(2)}, u32[]{:S(2)}) collective-permute-start(bf16[1024,512]{1,0:T(8,128)(2,1)} %collective-permute-done.x1), channel_id=1, source_target_pairs={{8,0},{9,1},{10,2},{11,3},{12,4},{13,5},{14,6},{15,7},{16,8},{17,9... | collective-permute-start | bytes 3145736 | tf_op jit(solution)/shard_map/ppermute | solution.py:434
  58.1 4.9 %collective-permute-start.3 = (bf16[1024,512]{1,0:T(8,128)(2,1)S(1)}, bf16[1024,512]{1,0:T(8,128)(2,1)}, u32[]{:S(2)}, u32[]{:S(2)}) collective-permute-start(bf16[1024,512]{1,0:T(8,128)(2,1)S(1)} %bitcast.6), channel_id=1, source_target_pairs={{0,8},{1,9},{2,10},{3,11},{4,12},{5,13},{6,14},{7,15},{8,16},{9,17... | collective-permute-start | bytes 3145736 | tf_op jit(solution)/shard_map/ppermute | solution.py:434
  63.1 3.6 %all-to-all-start.2 = ((bf16[8,128,512]{2,1,0:T(8,128)(2,1)}), bf16[8,128,512]{2,1,0:T(8,128)(2,1)S(1)}, u32[]{:S(2)}, u32[]{:S(2)}) async-start(bf16[8,128,512]{2,1,0:T(8,128)(2,1)} %pack.2), calls=%async_computation.2 | async-start | bytes 2097152 | tf_op jit(solution)/shard_map/all_to_all | solution.py:429
  66.7 1.3 collective-permute-start.5
  68.0 7.5 %collective-permute-start.4 = (bf16[16,512]{1,0:T(8,128)(2,1)S(1)}, bf16[16,512]{1,0:T(8,128)(2,1)S(1)}, u32[]{:S(2)}, u32[]{:S(2)}) collective-permute-start(bf16[16,512]{1,0:T(8,128)(2,1)S(1)} %slice.8), channel_id=1, source_target_pairs={{0,16},{1,17},{2,18},{3,19},{4,20},{5,21},{6,22},{7,23},{8,24},{9,... | collective-permute-start | bytes 49160 | tf_op jit(solution)/shard_map/ppermute | solution.py:434
  75.6 7.6 %early.1 = (f32[1024,512]{1,0:T(8,128)}, f32[1024,512]{1,0:T(8,128)}) custom-call(bf16[1024,512]{1,0:T(8,128)(2,1)} %bitcast.11, bf16[1024,512]{1,0:T(8,128)(2,1)} %collective-permute-done.x1, bf16[4,256,4352]{2,1,0:T(8,128)(2,1)} %get-tuple-element.22.tiles), custom_call_target="tpu_custom_call" | custom-call | flops 201326592 | bytes 98304 | tf_op jit(solution)/shard_map/early/pallas_call | solution.py:260
  83.1 3.2 %collective-permute-done.5.x4_head = bf16[16,512]{1,0:T(8,128)(2,1)S(1)} collective-permute-done((bf16[16,512]{1,0:T(8,128)(2,1)S(1)}, bf16[16,512]{1,0:T(8,128)(2,1)S(1)}, u32[]{:S(2)}, u32[]{:S(2)}) %collective-permute-start.5) | collective-permute-done | bytes 16416 | tf_op jit(solution)/shard_map/ppermute | solution.py:434
  86.4 4.4 %collective-permute-start.6 = (bf16[1024,512]{1,0:T(8,128)(2,1)}, bf16[1024,512]{1,0:T(8,128)(2,1)}, u32[]{:S(2)}, u32[]{:S(2)}) collective-permute-start(bf16[1024,512]{1,0:T(8,128)(2,1)} %collective-permute-done.2.x2), channel_id=1, source_target_pairs={{8,0},{9,1},{10,2},{11,3},{12,4},{13,5},{14,6},{15,7},{16,8},{17,9... | collective-permute-start | bytes 3145736 | tf_op jit(solution)/shard_map/ppermute | solution.py:434
  90.8 9.5 %all_terms.1 = bf16[16,16,256]{2,1,0:T(8,128)(2,1)} custom-call(f32[1024,512]{1,0:T(8,128)} %get-tuple-element.23.acc.acc_in, f32[1024,512]{1,0:T(8,128)} %get-tuple-element.30.mid, bf16[1024,512]{1,0:T(8,128)(2,1)} %collective-permute-done.2.x2, bf16[1024,512]{1,0:T(8,128)(2,1)} %bitcast.12, bf16[1024,512]{1,0:T(8,128)(2,1)} %bitcast.8, ...), custom_call_target="tpu_custom_call" | custom-call | flops 134217728 | bytes 163840 | tf_op jit(solution)/shard_map/all_terms/pallas_call | solution.py:309
  100.3 12.7 %all-to-all-start.3 = ((bf16[16,16,256]{2,1,0:T(8,128)(2,1)}), bf16[16,16,256]{2,1,0:T(8,128)(2,1)S(1)}, u32[]{:S(2)}, u32[]{:S(2)}) async-start(bf16[16,16,256]{2,1,0:T(8,128)(2,1)} %all_terms.1), calls=%async_computation.3 | async-start | bytes 262144 | tf_op jit(solution)/shard_map/all_to_all | solution.py:459
  113.0 2.0 %collective-permute-start.7 = (bf16[1024,512]{1,0:T(8,128)(2,1)}, bf16[1024,512]{1,0:T(8,128)(2,1)S(1)}, u32[]{:S(2)}, u32[]{:S(2)}) collective-permute-start(bf16[1024,512]{1,0:T(8,128)(2,1)} %collective-permute-done.6.x3), channel_id=1, source_target_pairs={{8,0},{9,1},{10,2},{11,3},{12,4},{13,5},{14,6},{15,7},{16,8},{17,9... | collective-permute-start | bytes 3145736 | tf_op jit(solution)/shard_map/ppermute | solution.py:434
  115.0 8.0 %third.1 = (f32[1024,512]{1,0:T(8,128)}, bf16[16,512]{1,0:T(8,128)(2,1)}) custom-call(f32[1024,512]{1,0:T(8,128)} %get-tuple-element.23.acc.acc_in, bf16[1024,512]{1,0:T(8,128)(2,1)} %collective-permute-done.2.x2, bf16[1024,512]{1,0:T(8,128)(2,1)} %collective-permute-done.6.x3, bf16[16,512]{1,0:T(8,128)(2,1)} %copy-done.9, ...), custom_call_target="tpu_custom_call" | custom-call | flops 38654705664 | bytes 25165824 | tf_op jit(solution)/shard_map/third/pallas_call | solution.py:349
  123.1 2.6 %all-to-all-done.3 = bf16[16,16,256]{2,1,0:T(8,128)(2,1)S(1)} async-done(((bf16[16,16,256]{2,1,0:T(8,128)(2,1)}), bf16[16,16,256]{2,1,0:T(8,128)(2,1)S(1)}, u32[]{:S(2)}, u32[]{:S(2)}) %all-to-all-start.3) | async-done | bytes 131104 | tf_op jit(solution)/shard_map/all_to_all | solution.py:459
  126.3 3.3 %all-to-all-start.4 = ((f32[4,16,256]{2,1,0:T(8,128)}), f32[4,16,256]{2,1,0:T(8,128)S(1)}, u32[]{:S(2)}, u32[]{:S(2)}) async-start(f32[4,16,256]{2,1,0:T(8,128)} %broadcast_in_dim.2), calls=%async_computation.4 | async-start | bytes 131072 | tf_op jit(solution)/shard_map/all_to_all | solution.py:465
  129.6 2.4 %collective-permute-start.8 = (bf16[16,512]{1,0:T(8,128)(2,1)}, bf16[16,512]{1,0:T(8,128)(2,1)S(1)}, u32[]{:S(2)}, u32[]{:S(2)}) collective-permute-start(bf16[16,512]{1,0:T(8,128)(2,1)} %get-tuple-element.34), channel_id=1, source_target_pairs={{8,0},{9,1},{10,2},{11,3},{12,4},{13,5},{14,6},{15,7},{16,8},{17,9... | collective-permute-start | bytes 49160 | tf_op jit(solution)/shard_map/ppermute | solution.py:434
  134.3 1.6 prepare.1.extra
  135.9 3.4 %collective-permute-done.8.next_head = bf16[16,512]{1,0:T(8,128)(2,1)S(1)} collective-permute-done((bf16[16,512]{1,0:T(8,128)(2,1)}, bf16[16,512]{1,0:T(8,128)(2,1)S(1)}, u32[]{:S(2)}, u32[]{:S(2)}) %collective-permute-start.8) | collective-permute-done | bytes 16416 | tf_op jit(solution)/shard_map/ppermute | solution.py:434
  140.3 5.6 %finish.1 = bf16[8,144,512]{2,1,0:T(8,128)(2,1)} custom-call(f32[1024,512]{1,0:T(8,128)} %get-tuple-element.33.acc_in, bf16[1024,512]{1,0:T(8,128)(2,1)} %copy-done.5, bf16[4,256,2048]{2,1,0:T(8,128)(2,1)} %get-tuple-element.31.tiles, bf16[16,512]{1,0:T(8,128)(2,1)} %copy-done.7, f32[7,512]{1,0:T(8,128)} %constant_dynamic-slice_fusion.taps, ...), custom_call_target="tpu_custom_call" | custom-call | flops 50331648 | bytes 65536 | tf_op jit(solution)/shard_map/finish/pallas_call | solution.py:394
  145.9 6.1 %all-to-all-start.5 = ((bf16[8,144,512]{2,1,0:T(8,128)(2,1)}), bf16[8,144,512]{2,1,0:T(8,128)(2,1)S(1)}, u32[]{:S(2)}, u32[]{:S(2)}) async-start(bf16[8,144,512]{2,1,0:T(8,128)(2,1)} %finish.1), calls=%async_computation.5 | async-start | bytes 2359296 | tf_op jit(solution)/shard_map/all_to_all | solution.py:429
  151.9 15.1 %all-to-all-done.5.got = bf16[8,144,512]{2,1,0:T(8,128)(2,1)S(1)} async-done(((bf16[8,144,512]{2,1,0:T(8,128)(2,1)}), bf16[8,144,512]{2,1,0:T(8,128)(2,1)S(1)}, u32[]{:S(2)}, u32[]{:S(2)}) %all-to-all-start.5) | async-done | bytes 1179680 | tf_op jit(solution)/shard_map/all_to_all | solution.py:429
  167.1 1.6 unpack.1
  (34 shorter events, 5.4 us)
Async XLA Ops:
  0.6 47.0 %copy-start = (f32[7,4096]{1,0:T(8,128)S(1)}, f32[7,4096]{1,0:T(8,128)}, u32[]{:S(2)}) copy-start(f32[7,4096]{1,0:T(8,128)} %param.9) | copy-start | bytes 344068
  0.6 32.6 %collective-permute-start.1 = (bf16[1,128,4096]{2,1,0:T(8,128)(2,1)}, bf16[1,128,4096]{2,1,0:T(8,128)(2,1)S(1)}, u32[]{:S(2)}, u32[]{:S(2)}) collective-permute-start(bf16[1,128,4096]{2,1,0:T(8,128)(2,1)} %src_ref), channel_id=1, source_target_pairs={{0,8},{1,9},{2,10},{3,11},{4,12},{5,13},{6,14},{7,15},{8,16},{9,17... | collective-permute-start | bytes 3145736 | tf_op jit(solution)/shard_map/ppermute | solution.py:434
  31.2 35.6 %copy-start.2 = (bf16[8,128,512]{2,1,0:T(8,128)(2,1)}, bf16[8,128,512]{2,1,0:T(8,128)(2,1)S(1)}, u32[]{:S(2)}) copy-start(bf16[8,128,512]{2,1,0:T(8,128)(2,1)S(1)} %all_to_all.30) | copy-start | bytes 3145732
  31.2 24.9 %collective-permute-start = (bf16[1024,512]{1,0:T(8,128)(2,1)S(1)}, bf16[1024,512]{1,0:T(8,128)(2,1)}, u32[]{:S(2)}, u32[]{:S(2)}) collective-permute-start(bf16[1024,512]{1,0:T(8,128)(2,1)S(1)} %bitcast.9), channel_id=1, source_target_pairs={{8,0},{9,1},{10,2},{11,3},{12,4},{13,5},{14,6},{15,7},{16,8},{17,9... | collective-permute-start | bytes 3145736 | tf_op jit(solution)/shard_map/ppermute | solution.py:434
  33.2 1.0 copy-start.4
  36.5 17.6 %all-to-all-start.1 = ((bf16[8,128,512]{2,1,0:T(8,128)(2,1)}), bf16[8,128,512]{2,1,0:T(8,128)(2,1)S(1)}, u32[]{:S(2)}, u32[]{:S(2)}) async-start(bf16[8,128,512]{2,1,0:T(8,128)(2,1)} %pack.3), calls=%async_computation.1 | async-start | bytes 2097152 | tf_op jit(solution)/shard_map/all_to_all | solution.py:429
  54.1 29.0 %copy-start.1 = (bf16[8,128,512]{2,1,0:T(8,128)(2,1)}, bf16[8,128,512]{2,1,0:T(8,128)(2,1)S(1)}, u32[]{:S(2)}) copy-start(bf16[8,128,512]{2,1,0:T(8,128)(2,1)S(1)} %all-to-all-done.1) | copy-start | bytes 3145732
  56.1 30.2 %collective-permute-start.2 = (bf16[1024,512]{1,0:T(8,128)(2,1)}, bf16[1024,512]{1,0:T(8,128)(2,1)}, u32[]{:S(2)}, u32[]{:S(2)}) collective-permute-start(bf16[1024,512]{1,0:T(8,128)(2,1)} %collective-permute-done.x1), channel_id=1, source_target_pairs={{8,0},{9,1},{10,2},{11,3},{12,4},{13,5},{14,6},{15,7},{16,8},{17,9... | collective-permute-start | bytes 3145736 | tf_op jit(solution)/shard_map/ppermute | solution.py:434
  58.1 28.2 %collective-permute-start.3 = (bf16[1024,512]{1,0:T(8,128)(2,1)S(1)}, bf16[1024,512]{1,0:T(8,128)(2,1)}, u32[]{:S(2)}, u32[]{:S(2)}) collective-permute-start(bf16[1024,512]{1,0:T(8,128)(2,1)S(1)} %bitcast.6), channel_id=1, source_target_pairs={{0,8},{1,9},{2,10},{3,11},{4,12},{5,13},{6,14},{7,15},{8,16},{9,17... | collective-permute-start | bytes 3145736 | tf_op jit(solution)/shard_map/ppermute | solution.py:434
  63.1 23.3 %all-to-all-start.2 = ((bf16[8,128,512]{2,1,0:T(8,128)(2,1)}), bf16[8,128,512]{2,1,0:T(8,128)(2,1)S(1)}, u32[]{:S(2)}, u32[]{:S(2)}) async-start(bf16[8,128,512]{2,1,0:T(8,128)(2,1)} %pack.2), calls=%async_computation.2 | async-start | bytes 2097152 | tf_op jit(solution)/shard_map/all_to_all | solution.py:429
  66.7 19.6 %collective-permute-start.5 = (bf16[16,512]{1,0:T(8,128)(2,1)S(1)}, bf16[16,512]{1,0:T(8,128)(2,1)S(1)}, u32[]{:S(2)}, u32[]{:S(2)}) collective-permute-start(bf16[16,512]{1,0:T(8,128)(2,1)S(1)} %slice.9), channel_id=1, source_target_pairs={{32,0},{33,1},{34,2},{35,3},{36,4},{37,5},{38,6},{39,7},{40,8},{41... | collective-permute-start | bytes 49160 | tf_op jit(solution)/shard_map/ppermute | solution.py:434
  68.0 18.3 %collective-permute-start.4 = (bf16[16,512]{1,0:T(8,128)(2,1)S(1)}, bf16[16,512]{1,0:T(8,128)(2,1)S(1)}, u32[]{:S(2)}, u32[]{:S(2)}) collective-permute-start(bf16[16,512]{1,0:T(8,128)(2,1)S(1)} %slice.8), channel_id=1, source_target_pairs={{0,16},{1,17},{2,18},{3,19},{4,20},{5,21},{6,22},{7,23},{8,24},{9,... | collective-permute-start | bytes 49160 | tf_op jit(solution)/shard_map/ppermute | solution.py:434
  86.3 14.0 %copy-start.9 = (bf16[16,512]{1,0:T(8,128)(2,1)}, bf16[16,512]{1,0:T(8,128)(2,1)S(1)}, u32[]{:S(2)}) copy-start(bf16[16,512]{1,0:T(8,128)(2,1)S(1)} %collective-permute-done.5.x4_head) | copy-start | bytes 49156
  86.3 4.5 %copy-start.8 = (bf16[16,512]{1,0:T(8,128)(2,1)}, bf16[16,512]{1,0:T(8,128)(2,1)S(1)}, u32[]{:S(2)}) copy-start(bf16[16,512]{1,0:T(8,128)(2,1)S(1)} %collective-permute-done.4.f3_tail) | copy-start | bytes 49156
  86.3 4.5 %copy-start.3 = (bf16[8,128,512]{2,1,0:T(8,128)(2,1)}, bf16[8,128,512]{2,1,0:T(8,128)(2,1)S(1)}, u32[]{:S(2)}) copy-start(bf16[8,128,512]{2,1,0:T(8,128)(2,1)S(1)} %all-to-all-done.2) | copy-start | bytes 3145732
  86.4 26.6 %collective-permute-start.6 = (bf16[1024,512]{1,0:T(8,128)(2,1)}, bf16[1024,512]{1,0:T(8,128)(2,1)}, u32[]{:S(2)}, u32[]{:S(2)}) collective-permute-start(bf16[1024,512]{1,0:T(8,128)(2,1)} %collective-permute-done.2.x2), channel_id=1, source_target_pairs={{8,0},{9,1},{10,2},{11,3},{12,4},{13,5},{14,6},{15,7},{16,8},{17,9... | collective-permute-start | bytes 3145736 | tf_op jit(solution)/shard_map/ppermute | solution.py:434
  100.3 25.3 %all-to-all-start.3 = ((bf16[16,16,256]{2,1,0:T(8,128)(2,1)}), bf16[16,16,256]{2,1,0:T(8,128)(2,1)S(1)}, u32[]{:S(2)}, u32[]{:S(2)}) async-start(bf16[16,16,256]{2,1,0:T(8,128)(2,1)} %all_terms.1), calls=%async_computation.3 | async-start | bytes 262144 | tf_op jit(solution)/shard_map/all_to_all | solution.py:459
  113.0 26.3 %collective-permute-start.7 = (bf16[1024,512]{1,0:T(8,128)(2,1)}, bf16[1024,512]{1,0:T(8,128)(2,1)S(1)}, u32[]{:S(2)}, u32[]{:S(2)}) collective-permute-start(bf16[1024,512]{1,0:T(8,128)(2,1)} %collective-permute-done.6.x3), channel_id=1, source_target_pairs={{8,0},{9,1},{10,2},{11,3},{12,4},{13,5},{14,6},{15,7},{16,8},{17,9... | collective-permute-start | bytes 3145736 | tf_op jit(solution)/shard_map/ppermute | solution.py:434
  126.3 7.4 %all-to-all-start.4 = ((f32[4,16,256]{2,1,0:T(8,128)}), f32[4,16,256]{2,1,0:T(8,128)S(1)}, u32[]{:S(2)}, u32[]{:S(2)}) async-start(f32[4,16,256]{2,1,0:T(8,128)} %broadcast_in_dim.2), calls=%async_computation.4 | async-start | bytes 131072 | tf_op jit(solution)/shard_map/all_to_all | solution.py:465
  129.6 9.7 %collective-permute-start.8 = (bf16[16,512]{1,0:T(8,128)(2,1)}, bf16[16,512]{1,0:T(8,128)(2,1)S(1)}, u32[]{:S(2)}, u32[]{:S(2)}) collective-permute-start(bf16[16,512]{1,0:T(8,128)(2,1)} %get-tuple-element.34), channel_id=1, source_target_pairs={{8,0},{9,1},{10,2},{11,3},{12,4},{13,5},{14,6},{15,7},{16,8},{17,9... | collective-permute-start | bytes 49160 | tf_op jit(solution)/shard_map/ppermute | solution.py:434
  133.7 0.6 copy-start.6
  139.3 0.6 copy-start.7
  139.3 1.0 copy-start.5
  145.9 21.2 %all-to-all-start.5 = ((bf16[8,144,512]{2,1,0:T(8,128)(2,1)}), bf16[8,144,512]{2,1,0:T(8,128)(2,1)S(1)}, u32[]{:S(2)}, u32[]{:S(2)}) async-start(bf16[8,144,512]{2,1,0:T(8,128)(2,1)} %finish.1), calls=%async_computation.5 | async-start | bytes 2359296 | tf_op jit(solution)/shard_map/all_to_all | solution.py:429
